TPU v7x, 256 devices: a whole 4x4x8 slice. The times are simulated.
256 devices in a mesh: gx: 32 (over y, x, core), gy: 8 (over z).
Axes of the slice: x: 4, y: 4, z: 8, core: 2. Of those that a mesh axis runs over, the one named last changes fastest.
Arguments:
- right_side: float32 [64, 32, 8192], P(None, 'gy', 'gx'), may hold values from -10 to 10
- start_pressure: float32 [64, 32, 8192], P(None, 'gy', 'gx'), may hold values from -1.5 to 1.5
- conductance: float32 [3, 64, 32, 8192], P(None, None, 'gy', 'gx'), may hold values from 0.3 to 3
- inverses: float32 [32, 64, 64, 256], P('gx'), may hold values from -0.05 to 1.6, as said below
Outputs:
- pressure: float32 [64, 32, 8192], P(None, 'gy', 'gx')
- residual: float32 [64, 32, 8192], P(None, 'gy', 'gx')
- direction: float32 [64, 32, 8192], P(None, 'gy', 'gx')
Inputs may be any that keep to these rules, and one draw needn't show every extreme that they name: Each block inverses[r, :, :, b] is symmetric with a dominant positive diagonal.
All inputs are finite; a program needn't handle non-finite values.
Results may differ from a plain program's by a relative error of at most 0.00026.
Values sent between devices are 32-bit elements; how exact they have to be, the bound alone decides.
No kernel may reach another device: no remote copies, remote signals or barrier semaphores. Data moves between devices by JAX's collectives and lax.ppermute only.
A program may use at most 128 MiB of HBM per device.

v0:
```python
import math

import jax
import jax.numpy as jnp
from jax import lax
from jax.sharding import PartitionSpec as P

exact_products = lax.Precision.HIGHEST


def partner(value, axis, distance):
    mask = 2**distance
    pairs = [(source, source ^ mask) for source in range(lax.axis_size(axis))]
    return lax.ppermute(value, axis, pairs)


def padded(block, sides, width):
    for axis, dim in sides:
        count = lax.axis_size(axis)
        forward = [(i, i + 1) for i in range(count - 1)]
        forward.append((count - 1, 0))
        backward = [(target, source) for source, target in forward]
        low = lax.ppermute(
            lax.slice_in_dim(block, block.shape[dim] - width, None, axis=dim), axis, forward
        )
        high = lax.ppermute(lax.slice_in_dim(block, 0, width, axis=dim), axis, backward)
        block = jnp.concatenate([low, block, high], axis=dim)
    return block


def dft_table(group_size, sign):
    indices = jnp.arange(group_size, dtype=jnp.int32)
    product = indices[:, None] * indices[None, :] % group_size
    phase_angle = sign * 2.0 * math.pi * product.astype(jnp.float32) / group_size
    return (jnp.cos(phase_angle), jnp.sin(phase_angle))


def complex_dot(real_part, imag_part, cosine, sine_part):
    real_out = jnp.matmul(real_part, cosine, precision=exact_products) - jnp.matmul(
        imag_part, sine_part, precision=exact_products
    )
    imag_out = jnp.matmul(real_part, sine_part, precision=exact_products) + jnp.matmul(
        imag_part, cosine, precision=exact_products
    )
    return (real_out, imag_out)


def twiddle(real_part, imag_part, residue, sign, length):
    columns = jnp.arange(real_part.shape[-1], dtype=jnp.int32)
    product = residue * columns % length
    phase_angle = sign * 2.0 * math.pi * product.astype(jnp.float32) / length
    cosine = jnp.cos(phase_angle)
    sine_part = jnp.sin(phase_angle)
    return (real_part * cosine - imag_part * sine_part, real_part * sine_part + imag_part * cosine)


def reverse_bits_scalar(position, levels):
    reversed_index = jnp.zeros((), jnp.int32)
    for bit_digit in range(levels):
        reversed_index = reversed_index + (position >> bit_digit & 1) * (
            1 << levels - 1 - bit_digit
        )
    return reversed_index


def rotate(complex_pair, cosine, sine_part):
    return jnp.stack(
        [
            cosine * complex_pair[0] - sine_part * complex_pair[1],
            sine_part * complex_pair[0] + cosine * complex_pair[1],
        ]
    )


def partner_of(stacked, bit_level):
    return partner(stacked, "gx", bit_level)


def forward_swaps(values_in, position, levels):
    stacked = jnp.stack([values_in, jnp.zeros_like(values_in)])
    for bit_level in reversed(range(levels)):
        half_span = 1 << bit_level
        partner_data = partner_of(stacked, bit_level)
        upper_half = position >> bit_level & 1 == 1
        offset = (position & half_span - 1).astype(jnp.float32)
        phase_angle = -math.pi * offset / half_span
        turned = rotate(partner_data - stacked, jnp.cos(phase_angle), jnp.sin(phase_angle))
        stacked = jnp.where(upper_half, turned, stacked + partner_data)
    return stacked


def inverse_swaps(stacked, position, levels):
    for bit_level in range(levels):
        half_span = 1 << bit_level
        partner_data = partner_of(stacked, bit_level)
        upper_half = position >> bit_level & 1 == 1
        offset = (position & half_span - 1).astype(jnp.float32)
        phase_angle = math.pi * offset / half_span
        cosine = jnp.cos(phase_angle)
        sine_part = jnp.sin(phase_angle)
        stacked = jnp.where(
            upper_half,
            partner_data - rotate(stacked, cosine, sine_part),
            stacked + rotate(partner_data, cosine, sine_part),
        )
    return stacked


def precondition(values_in, inverse_block):
    group_size = lax.axis_size("gx")
    levels = group_size.bit_length() - 1
    position = lax.axis_index("gx")
    local_cells = values_in.shape[2]
    length = local_cells * group_size
    forward_cos, forward_sin = dft_table(local_cells, -1.0)
    back_cos, back_sin = dft_table(local_cells, 1.0)
    residue = reverse_bits_scalar(position, levels)
    stacked = forward_swaps(values_in, position, levels)
    twisted_real, twisted_imag = twiddle(stacked[0], stacked[1], residue, -1.0, length)
    spectrum = jnp.stack(complex_dot(twisted_real, twisted_imag, forward_cos, forward_sin))
    solved = jnp.einsum("wzb,czyb->cwyb", inverse_block, spectrum, precision=exact_products)
    real_part, imag_part = complex_dot(solved[0], solved[1], back_cos, back_sin)
    real_part, imag_part = twiddle(real_part, imag_part, residue, 1.0, length)
    stacked = inverse_swaps(jnp.stack([real_part, imag_part]), position, levels)
    return stacked[0] / length


def extend(stacked_fields):
    return padded(stacked_fields, (("gx", 3), ("gy", 2)), 1)


def shards(right_side, start_pressure, conductance, inverses):
    along_x, along_y, along_z = (conductance[0], conductance[1], conductance[2])
    extended_start = extend(jnp.stack([start_pressure, along_x, along_y]))
    ahead_x = extended_start[1, :, 1:-1, 2:]
    ahead_y = extended_start[2, :, 2:, 1:-1]
    ahead_z = jnp.roll(along_z, -1, axis=0)
    row_count = start_pressure.shape[1]
    rows_global = lax.axis_index("gy") * row_count + jnp.arange(row_count, dtype=jnp.int32)
    total_rows = row_count * lax.axis_size("gy")
    lower_rows = (rows_global != 0).astype(jnp.float32)[None, :, None]
    upper_rows = (rows_global != total_rows - 1).astype(jnp.float32)[None, :, None]

    def operate(extended):
        centre = extended[0, :, 1:-1, 1:-1]
        behind_x = extended[0, :, 1:-1, :-2]
        before_x = extended[0, :, 1:-1, 2:]
        behind_y = extended[0, :, :-2, 1:-1] * lower_rows
        before_y = extended[0, :, 2:, 1:-1] * upper_rows
        zero_plane = jnp.zeros_like(centre[:1])
        behind_z = jnp.concatenate([zero_plane, centre[:-1]], axis=0)
        before_z = jnp.concatenate([centre[1:], zero_plane], axis=0)
        result_x = along_x * (centre - behind_x) + ahead_x * (centre - before_x)
        result_y = along_y * (centre - behind_y) + ahead_y * (centre - before_y)
        result_z = along_z * (centre - behind_z) + ahead_z * (centre - before_z)
        return result_x + result_y + result_z

    inverse_block = inverses[0]
    residual_start = right_side - operate(extended_start)
    precond_start = precondition(residual_start, inverse_block)
    image_field = operate(extend(precond_start[None]))
    first_dot = lax.psum(jnp.sum(residual_start * precond_start), ("gx", "gy"))
    curvature = lax.psum(jnp.sum(precond_start * image_field), ("gx", "gy"))
    step_length = first_dot / curvature
    pressure = start_pressure + step_length * precond_start
    residual = residual_start - step_length * image_field
    precond_next = precondition(residual, inverse_block)
    second_dot = lax.psum(jnp.sum(residual * precond_next), ("gx", "gy"))
    direction = precond_next + second_dot / first_dot * precond_start
    return (pressure, residual, direction)


def solution(mesh):
    placed = (
        P(None, "gy", "gx"),
        P(None, "gy", "gx"),
        P(None, None, "gy", "gx"),
        P("gx", None, None, None),
    )
    return jax.shard_map(
        shards,
        mesh=mesh,
        in_specs=placed,
        out_specs=(P(None, "gy", "gx"), P(None, "gy", "gx"), P(None, "gy", "gx")),
        check_vma=False,
    )
```

profile of v0, /device:TPU:2, one launch (start us, length us, event | category | flops | bytes accessed | tf_op | source)
XLA Modules:
  0.0 503.5 jit_solution(2577638508985285508)
XLA Ops:
  12.0 5.3 %collective-permute-start.3 = (f32[3,64,1,258]{3,1,2,0:T(8,128)S(1)}, f32[3,64,1,258]{3,1,2,0:T(8,128)S(1)}, u32[]{:S(2)}, u32[]{:S(2)}) collective-permute-start(f32[3,64,1,258]{3,1,2,0:T(8,128)S(1)} %get-tuple-element.22), channel_id=1, source_target_pairs={{1,0},{2,1},{3,2},{4,3},{5,4},{6,5},{7,6},{0,7},{9,8},{10,9},{11,1... | collective-permute-start | bytes 594440 | tf_op jit(solution)/shard_map/ppermute | solution.py:26
  17.4 6.4 %collective-permute-done.3 = f32[3,64,1,258]{3,1,2,0:T(8,128)S(1)} collective-permute-done((f32[3,64,1,258]{3,1,2,0:T(8,128)S(1)}, f32[3,64,1,258]{3,1,2,0:T(8,128)S(1)}, u32[]{:S(2)}, u32[]{:S(2)}) %collective-permute-start.3) | collective-permute-done | bytes 198176 | tf_op jit(solution)/shard_map/ppermute | solution.py:26
  32.3 10.9 %collective-permute-done.4 = f32[2,64,4,256]{3,1,2,0:T(8,128)S(1)} collective-permute-done((f32[2,64,4,256]{3,1,2,0:T(8,128)S(1)}, f32[2,64,4,256]{3,1,2,0:T(8,128)S(1)}, u32[]{:S(2)}, u32[]{:S(2)}) %collective-permute-start.4) | collective-permute-done | bytes 524320 | tf_op jit(solution)/shard_map/ppermute | solution.py:14
  46.0 10.3 %collective-permute-done.5 = f32[2,64,4,256]{3,1,2,0:T(8,128)S(1)} collective-permute-done((f32[2,64,4,256]{3,1,2,0:T(8,128)}, f32[2,64,4,256]{3,1,2,0:T(8,128)S(1)}, u32[]{:S(2)}, u32[]{:S(2)}) %collective-permute-start.5) | collective-permute-done | bytes 524320 | tf_op jit(solution)/shard_map/ppermute | solution.py:14
  58.4 6.1 %collective-permute-start.6 = (f32[2,64,4,256]{3,1,2,0:T(8,128)S(1)}, f32[2,64,4,256]{3,1,2,0:T(8,128)S(1)}, u32[]{:S(2)}, u32[]{:S(2)}) collective-permute-start(f32[2,64,4,256]{3,1,2,0:T(8,128)S(1)} %maximum_select_fusion.1), channel_id=1, source_target_pairs={{0,32},{8,40},{16,48},{24,56},{32,0},{40,8},{48,16},{56,24},{64,96... | collective-permute-start | bytes 1572872 | tf_op jit(solution)/shard_map/ppermute | solution.py:14
  64.6 10.7 %collective-permute-done.6 = f32[2,64,4,256]{3,1,2,0:T(8,128)S(1)} collective-permute-done((f32[2,64,4,256]{3,1,2,0:T(8,128)S(1)}, f32[2,64,4,256]{3,1,2,0:T(8,128)S(1)}, u32[]{:S(2)}, u32[]{:S(2)}) %collective-permute-start.6) | collective-permute-done | bytes 524320 | tf_op jit(solution)/shard_map/ppermute | solution.py:14
  75.8 11.8 %collective-permute-done.7 = f32[2,64,4,256]{3,1,2,0:T(8,128)S(1)} collective-permute-done((f32[2,64,4,256]{3,1,2,0:T(8,128)S(1)}, f32[2,64,4,256]{3,1,2,0:T(8,128)S(1)}, u32[]{:S(2)}, u32[]{:S(2)}) %collective-permute-start.7) | collective-permute-done | bytes 524320 | tf_op jit(solution)/shard_map/ppermute | solution.py:14
  88.1 9.2 %copy.39 = f32[64,64,256,1]{1,0,3,2:T(8,128)} copy(f32[64,64,256,1]{2,1,0,3:T(8,128)} %bitcast.312) | data formatting | bytes 8388608 | tf_op jit(solution)/shard_map/squeeze | solution.py:158
  103.7 15.9 %convolution_bitcast_fusion.1 = f32[2,64,4,256]{1,2,0,3:T(4,128)S(1)} fusion(f32[2,64,4,256]{1,2,0,3:T(4,128)S(1)} %copy.23, f32[64,64,256,1]{1,0,3,2:T(8,128)} %copy.39), kind=kOutput, calls=%fused_computation.1 | convolution fusion | flops 100663296 | bytes 5242880 | tf_op jit(solution)/shard_map/wzb,czyb->cwyb/dot_general | solution.py:121
  131.7 12.4 %collective-permute-done.10 = f32[2,64,4,256]{3,1,2,0:T(8,128)S(1)} collective-permute-done((f32[2,64,4,256]{3,1,2,0:T(8,128)}, f32[2,64,4,256]{3,1,2,0:T(8,128)S(1)}, u32[]{:S(2)}, u32[]{:S(2)}) %collective-permute-start.10) | collective-permute-done | bytes 524320 | tf_op jit(solution)/shard_map/ppermute | solution.py:14
  149.8 11.7 %collective-permute-done.11 = f32[2,64,4,256]{3,1,2,0:T(8,128)S(1)} collective-permute-done((f32[2,64,4,256]{3,1,2,0:T(8,128)S(1)}, f32[2,64,4,256]{3,1,2,0:T(8,128)S(1)}, u32[]{:S(2)}, u32[]{:S(2)}) %collective-permute-start.11) | collective-permute-done | bytes 524320 | tf_op jit(solution)/shard_map/ppermute | solution.py:14
  165.4 10.7 %collective-permute-done.12 = f32[2,64,4,256]{3,1,2,0:T(8,128)S(1)} collective-permute-done((f32[2,64,4,256]{3,1,2,0:T(8,128)S(1)}, f32[2,64,4,256]{3,1,2,0:T(8,128)S(1)}, u32[]{:S(2)}, u32[]{:S(2)}) %collective-permute-start.12) | collective-permute-done | bytes 524320 | tf_op jit(solution)/shard_map/ppermute | solution.py:14
  182.1 9.9 %collective-permute-done.13 = f32[2,64,4,256]{3,1,2,0:T(8,128)S(1)} collective-permute-done((f32[2,64,4,256]{3,1,2,0:T(8,128)S(1)}, f32[2,64,4,256]{3,1,2,0:T(8,128)S(1)}, u32[]{:S(2)}, u32[]{:S(2)}) %collective-permute-start.13) | collective-permute-done | bytes 524320 | tf_op jit(solution)/shard_map/ppermute | solution.py:14
  205.4 77.0 %all-reduce.6 = (f32[]{:T(128)}, f32[]{:T(128)}) all-reduce(f32[]{:T(128)} %get-tuple-element.7, f32[]{:T(128)} %get-tuple-element.6), channel_id=1, replica_groups=mesh['gx'=32,'gy'=8] {'gx','gy'}, use_global_device_ids=true, to_apply=%region_1.2 | all-reduce | flops 2 | bytes 16 | tf_op jit(solution)/shard_map/psum | solution.py:162
  285.6 13.5 %collective-permute-done.18 = f32[2,64,4,256]{3,1,2,0:T(8,128)S(1)} collective-permute-done((f32[2,64,4,256]{3,1,2,0:T(8,128)S(1)}, f32[2,64,4,256]{3,1,2,0:T(8,128)S(1)}, u32[]{:S(2)}, u32[]{:S(2)}) %collective-permute-start.18) | collective-permute-done | bytes 524320 | tf_op jit(solution)/shard_map/ppermute | solution.py:14
  299.4 12.8 %collective-permute-done.19 = f32[2,64,4,256]{3,1,2,0:T(8,128)S(1)} collective-permute-done((f32[2,64,4,256]{3,1,2,0:T(8,128)S(1)}, f32[2,64,4,256]{3,1,2,0:T(8,128)S(1)}, u32[]{:S(2)}, u32[]{:S(2)}) %collective-permute-start.19) | collective-permute-done | bytes 524320 | tf_op jit(solution)/shard_map/ppermute | solution.py:14
  314.7 11.3 %collective-permute-done.20 = f32[2,64,4,256]{3,1,2,0:T(8,128)S(1)} collective-permute-done((f32[2,64,4,256]{3,1,2,0:T(8,128)S(1)}, f32[2,64,4,256]{3,1,2,0:T(8,128)S(1)}, u32[]{:S(2)}, u32[]{:S(2)}) %collective-permute-start.20) | collective-permute-done | bytes 524320 | tf_op jit(solution)/shard_map/ppermute | solution.py:14
  326.8 10.5 %collective-permute-done.21 = f32[2,64,4,256]{3,1,2,0:T(8,128)S(1)} collective-permute-done((f32[2,64,4,256]{3,1,2,0:T(8,128)S(1)}, f32[2,64,4,256]{3,1,2,0:T(8,128)S(1)}, u32[]{:S(2)}, u32[]{:S(2)}) %collective-permute-start.21) | collective-permute-done | bytes 524320 | tf_op jit(solution)/shard_map/ppermute | solution.py:14
  345.8 15.6 %convolution_bitcast_fusion = f32[2,64,4,256]{1,2,0,3:T(4,128)S(1)} fusion(f32[2,64,4,256]{1,2,0,3:T(4,128)S(1)} %copy.30, f32[64,64,256,1]{1,0,3,2:T(8,128)} %copy.39), kind=kOutput, calls=%fused_computation | convolution fusion | flops 100663296 | bytes 5242880 | tf_op jit(solution)/shard_map/wzb,czyb->cwyb/dot_general | solution.py:121
  370.8 13.4 %collective-permute-done.24 = f32[2,64,4,256]{3,1,2,0:T(8,128)S(1)} collective-permute-done((f32[2,64,4,256]{3,1,2,0:T(8,128)S(1)}, f32[2,64,4,256]{3,1,2,0:T(8,128)S(1)}, u32[]{:S(2)}, u32[]{:S(2)}) %collective-permute-start.24) | collective-permute-done | bytes 524320 | tf_op jit(solution)/shard_map/ppermute | solution.py:14
  386.7 12.5 %collective-permute-done.25 = f32[2,64,4,256]{3,1,2,0:T(8,128)S(1)} collective-permute-done((f32[2,64,4,256]{3,1,2,0:T(8,128)S(1)}, f32[2,64,4,256]{3,1,2,0:T(8,128)S(1)}, u32[]{:S(2)}, u32[]{:S(2)}) %collective-permute-start.25) | collective-permute-done | bytes 524320 | tf_op jit(solution)/shard_map/ppermute | solution.py:14
  400.4 11.3 %collective-permute-done.26 = f32[2,64,4,256]{3,1,2,0:T(8,128)S(1)} collective-permute-done((f32[2,64,4,256]{3,1,2,0:T(8,128)S(1)}, f32[2,64,4,256]{3,1,2,0:T(8,128)S(1)}, u32[]{:S(2)}, u32[]{:S(2)}) %collective-permute-start.26) | collective-permute-done | bytes 524320 | tf_op jit(solution)/shard_map/ppermute | solution.py:14
  414.7 10.1 %collective-permute-done.27 = f32[2,64,4,256]{3,1,2,0:T(8,128)S(1)} collective-permute-done((f32[2,64,4,256]{3,1,2,0:T(8,128)S(1)}, f32[2,64,4,256]{3,1,2,0:T(8,128)S(1)}, u32[]{:S(2)}, u32[]{:S(2)}) %collective-permute-start.27) | collective-permute-done | bytes 524320 | tf_op jit(solution)/shard_map/ppermute | solution.py:14
  425.6 74.3 %psum.23 = f32[]{:T(128)} all-reduce(f32[]{:T(128)} %get-tuple-element.10), channel_id=1, replica_groups=mesh['gx'=32,'gy'=8] {'gx','gy'}, use_global_device_ids=true, to_apply=%region_5.6 | all-reduce | flops 1 | bytes 8 | tf_op jit(solution)/shard_map/psum | solution.py:168
  (197 shorter events, 104.1 us)
Async XLA Ops:
  3.8 5.6 %collective-permute-start.1 = (f32[3,64,4,1]{3,1,2,0:T(8,128)}, f32[3,64,4,1]{3,1,2,0:T(8,128)S(1)}, u32[]{:S(2)}, u32[]{:S(2)}) collective-permute-start(f32[3,64,4,1]{3,1,2,0:T(8,128)} %get-tuple-element.31), channel_id=1, source_target_pairs={{8,0},{16,8},{24,16},{32,24},{40,32},{48,40},{56,48},{64,56},{72,6... | collective-permute-start | bytes 9224 | tf_op jit(solution)/shard_map/ppermute | solution.py:26
  3.8 7.8 %collective-permute-start = (f32[3,64,4,1]{3,1,2,0:T(8,128)S(1)}, f32[3,64,4,1]{3,1,2,0:T(8,128)S(1)}, u32[]{:S(2)}, u32[]{:S(2)}) collective-permute-start(f32[3,64,4,1]{3,1,2,0:T(8,128)S(1)} %get-tuple-element.30), channel_id=1, source_target_pairs={{0,8},{8,16},{16,24},{24,32},{32,40},{40,48},{48,56},{56,64},{64,7... | collective-permute-start | bytes 9224 | tf_op jit(solution)/shard_map/ppermute | solution.py:23
  12.0 11.8 %collective-permute-start.3 = (f32[3,64,1,258]{3,1,2,0:T(8,128)S(1)}, f32[3,64,1,258]{3,1,2,0:T(8,128)S(1)}, u32[]{:S(2)}, u32[]{:S(2)}) collective-permute-start(f32[3,64,1,258]{3,1,2,0:T(8,128)S(1)} %get-tuple-element.22), channel_id=1, source_target_pairs={{1,0},{2,1},{3,2},{4,3},{5,4},{6,5},{7,6},{0,7},{9,8},{10,9},{11,1... | collective-permute-start | bytes 594440 | tf_op jit(solution)/shard_map/ppermute | solution.py:26
  17.2 10.0 %collective-permute-start.2 = (f32[3,64,1,258]{3,1,2,0:T(8,128)S(1)}, f32[3,64,1,258]{3,1,2,0:T(8,128)S(1)}, u32[]{:S(2)}, u32[]{:S(2)}) collective-permute-start(f32[3,64,1,258]{3,1,2,0:T(8,128)S(1)} %get-tuple-element.21), channel_id=1, source_target_pairs={{0,1},{1,2},{2,3},{3,4},{4,5},{5,6},{6,7},{7,0},{8,9},{9,10},{10,1... | collective-permute-start | bytes 594440 | tf_op jit(solution)/shard_map/ppermute | solution.py:23
  28.8 14.4 %collective-permute-start.4 = (f32[2,64,4,256]{3,1,2,0:T(8,128)S(1)}, f32[2,64,4,256]{3,1,2,0:T(8,128)S(1)}, u32[]{:S(2)}, u32[]{:S(2)}) collective-permute-start(f32[2,64,4,256]{3,1,2,0:T(8,128)S(1)} %stack.216), channel_id=1, source_target_pairs={{0,128},{8,136},{16,144},{24,152},{32,160},{40,168},{48,176},{56,1... | collective-permute-start | bytes 1572872 | tf_op jit(solution)/shard_map/ppermute | solution.py:14
  44.2 12.1 %collective-permute-start.5 = (f32[2,64,4,256]{3,1,2,0:T(8,128)}, f32[2,64,4,256]{3,1,2,0:T(8,128)S(1)}, u32[]{:S(2)}, u32[]{:S(2)}) collective-permute-start(f32[2,64,4,256]{3,1,2,0:T(8,128)} %maximum_select_fusion), channel_id=1, source_target_pairs={{0,64},{8,72},{16,80},{24,88},{32,96},{40,104},{48,112},{56,120},{... | collective-permute-start | bytes 1572872 | tf_op jit(solution)/shard_map/ppermute | solution.py:14
  58.4 16.9 %collective-permute-start.6 = (f32[2,64,4,256]{3,1,2,0:T(8,128)S(1)}, f32[2,64,4,256]{3,1,2,0:T(8,128)S(1)}, u32[]{:S(2)}, u32[]{:S(2)}) collective-permute-start(f32[2,64,4,256]{3,1,2,0:T(8,128)S(1)} %maximum_select_fusion.1), channel_id=1, source_target_pairs={{0,32},{8,40},{16,48},{24,56},{32,0},{40,8},{48,16},{56,24},{64,96... | collective-permute-start | bytes 1572872 | tf_op jit(solution)/shard_map/ppermute | solution.py:14
  75.5 12.0 %collective-permute-start.7 = (f32[2,64,4,256]{3,1,2,0:T(8,128)S(1)}, f32[2,64,4,256]{3,1,2,0:T(8,128)S(1)}, u32[]{:S(2)}, u32[]{:S(2)}) collective-permute-start(f32[2,64,4,256]{3,1,2,0:T(8,128)S(1)} %maximum_select_fusion.2), channel_id=1, source_target_pairs={{0,16},{8,24},{16,0},{24,8},{32,48},{40,56},{48,32},{56,40},{64,80... | collective-permute-start | bytes 1572872 | tf_op jit(solution)/shard_map/ppermute | solution.py:14
  87.8 9.7 %collective-permute-start.8 = (f32[2,64,4,256]{3,1,2,0:T(8,128)S(1)}, f32[2,64,4,256]{3,1,2,0:T(8,128)S(1)}, u32[]{:S(2)}, u32[]{:S(2)}) collective-permute-start(f32[2,64,4,256]{3,1,2,0:T(8,128)S(1)} %maximum_select_fusion.3), channel_id=1, source_target_pairs={{0,8},{8,0},{16,24},{24,16},{32,40},{40,32},{48,56},{56,48},{64,72... | collective-permute-start | bytes 1572872 | tf_op jit(solution)/shard_map/ppermute | solution.py:14
  129.8 14.4 %collective-permute-start.10 = (f32[2,64,4,256]{3,1,2,0:T(8,128)}, f32[2,64,4,256]{3,1,2,0:T(8,128)S(1)}, u32[]{:S(2)}, u32[]{:S(2)}) collective-permute-start(f32[2,64,4,256]{3,1,2,0:T(8,128)} %fusion.4), channel_id=1, source_target_pairs={{0,16},{8,24},{16,0},{24,8},{32,48},{40,56},{48,32},{56,40},{64,80... | collective-permute-start | bytes 1572872 | tf_op jit(solution)/shard_map/ppermute | solution.py:14
  146.5 15.0 %collective-permute-start.11 = (f32[2,64,4,256]{3,1,2,0:T(8,128)S(1)}, f32[2,64,4,256]{3,1,2,0:T(8,128)S(1)}, u32[]{:S(2)}, u32[]{:S(2)}) collective-permute-start(f32[2,64,4,256]{3,1,2,0:T(8,128)S(1)} %fusion.5), channel_id=1, source_target_pairs={{0,32},{8,40},{16,48},{24,56},{32,0},{40,8},{48,16},{56,24},{64,96... | collective-permute-start | bytes 1572872 | tf_op jit(solution)/shard_map/ppermute | solution.py:14
  163.5 12.6 %collective-permute-start.12 = (f32[2,64,4,256]{3,1,2,0:T(8,128)S(1)}, f32[2,64,4,256]{3,1,2,0:T(8,128)S(1)}, u32[]{:S(2)}, u32[]{:S(2)}) collective-permute-start(f32[2,64,4,256]{3,1,2,0:T(8,128)S(1)} %fusion.6), channel_id=1, source_target_pairs={{0,64},{8,72},{16,80},{24,88},{32,96},{40,104},{48,112},{56,120},{... | collective-permute-start | bytes 1572872 | tf_op jit(solution)/shard_map/ppermute | solution.py:14
  178.0 13.9 %collective-permute-start.13 = (f32[2,64,4,256]{3,1,2,0:T(8,128)S(1)}, f32[2,64,4,256]{3,1,2,0:T(8,128)S(1)}, u32[]{:S(2)}, u32[]{:S(2)}) collective-permute-start(f32[2,64,4,256]{3,1,2,0:T(8,128)S(1)} %fusion.7), channel_id=1, source_target_pairs={{0,128},{8,136},{16,144},{24,152},{32,160},{40,168},{48,176},{56,1... | collective-permute-start | bytes 1572872 | tf_op jit(solution)/shard_map/ppermute | solution.py:14
  192.3 4.5 collective-permute-start.14
  196.9 4.9 collective-permute-start.17
  197.1 6.0 %collective-permute-start.16 = (f32[1,64,1,258]{3,1,2,0:T(8,128)S(1)}, f32[1,64,1,258]{3,1,2,0:T(8,128)S(1)}, u32[]{:S(2)}, u32[]{:S(2)}) collective-permute-start(f32[1,64,1,258]{3,1,2,0:T(8,128)S(1)} %get-tuple-element.60), channel_id=1, source_target_pairs={{0,1},{1,2},{2,3},{3,4},{4,5},{5,6},{6,7},{7,0},{8,9},{9,10},{10,1... | collective-permute-start | bytes 198152 | tf_op jit(solution)/shard_map/ppermute | solution.py:23
  283.8 15.2 %collective-permute-start.18 = (f32[2,64,4,256]{3,1,2,0:T(8,128)S(1)}, f32[2,64,4,256]{3,1,2,0:T(8,128)S(1)}, u32[]{:S(2)}, u32[]{:S(2)}) collective-permute-start(f32[2,64,4,256]{3,1,2,0:T(8,128)S(1)} %stack.241), channel_id=1, source_target_pairs={{0,128},{8,136},{16,144},{24,152},{32,160},{40,168},{48,176},{56,1... | collective-permute-start | bytes 1572872 | tf_op jit(solution)/shard_map/ppermute | solution.py:14
  299.3 12.9 %collective-permute-start.19 = (f32[2,64,4,256]{3,1,2,0:T(8,128)S(1)}, f32[2,64,4,256]{3,1,2,0:T(8,128)S(1)}, u32[]{:S(2)}, u32[]{:S(2)}) collective-permute-start(f32[2,64,4,256]{3,1,2,0:T(8,128)S(1)} %maximum_select_fusion.5), channel_id=1, source_target_pairs={{0,64},{8,72},{16,80},{24,88},{32,96},{40,104},{48,112},{56,120},{... | collective-permute-start | bytes 1572872 | tf_op jit(solution)/shard_map/ppermute | solution.py:14
  312.5 13.5 %collective-permute-start.20 = (f32[2,64,4,256]{3,1,2,0:T(8,128)S(1)}, f32[2,64,4,256]{3,1,2,0:T(8,128)S(1)}, u32[]{:S(2)}, u32[]{:S(2)}) collective-permute-start(f32[2,64,4,256]{3,1,2,0:T(8,128)S(1)} %maximum_select_fusion.6), channel_id=1, source_target_pairs={{0,32},{8,40},{16,48},{24,56},{32,0},{40,8},{48,16},{56,24},{64,96... | collective-permute-start | bytes 1572872 | tf_op jit(solution)/shard_map/ppermute | solution.py:14
  326.2 11.0 %collective-permute-start.21 = (f32[2,64,4,256]{3,1,2,0:T(8,128)S(1)}, f32[2,64,4,256]{3,1,2,0:T(8,128)S(1)}, u32[]{:S(2)}, u32[]{:S(2)}) collective-permute-start(f32[2,64,4,256]{3,1,2,0:T(8,128)S(1)} %maximum_select_fusion.7), channel_id=1, source_target_pairs={{0,16},{8,24},{16,0},{24,8},{32,48},{40,56},{48,32},{56,40},{64,80... | collective-permute-start | bytes 1572872 | tf_op jit(solution)/shard_map/ppermute | solution.py:14
  370.1 14.1 %collective-permute-start.24 = (f32[2,64,4,256]{3,1,2,0:T(8,128)S(1)}, f32[2,64,4,256]{3,1,2,0:T(8,128)S(1)}, u32[]{:S(2)}, u32[]{:S(2)}) collective-permute-start(f32[2,64,4,256]{3,1,2,0:T(8,128)S(1)} %fusion.8), channel_id=1, source_target_pairs={{0,16},{8,24},{16,0},{24,8},{32,48},{40,56},{48,32},{56,40},{64,80... | collective-permute-start | bytes 1572872 | tf_op jit(solution)/shard_map/ppermute | solution.py:14
  384.5 14.7 %collective-permute-start.25 = (f32[2,64,4,256]{3,1,2,0:T(8,128)S(1)}, f32[2,64,4,256]{3,1,2,0:T(8,128)S(1)}, u32[]{:S(2)}, u32[]{:S(2)}) collective-permute-start(f32[2,64,4,256]{3,1,2,0:T(8,128)S(1)} %fusion.9), channel_id=1, source_target_pairs={{0,32},{8,40},{16,48},{24,56},{32,0},{40,8},{48,16},{56,24},{64,96... | collective-permute-start | bytes 1572872 | tf_op jit(solution)/shard_map/ppermute | solution.py:14
  399.4 12.3 %collective-permute-start.26 = (f32[2,64,4,256]{3,1,2,0:T(8,128)S(1)}, f32[2,64,4,256]{3,1,2,0:T(8,128)S(1)}, u32[]{:S(2)}, u32[]{:S(2)}) collective-permute-start(f32[2,64,4,256]{3,1,2,0:T(8,128)S(1)} %fusion.10), channel_id=1, source_target_pairs={{0,64},{8,72},{16,80},{24,88},{32,96},{40,104},{48,112},{56,120},{... | collective-permute-start | bytes 1572872 | tf_op jit(solution)/shard_map/ppermute | solution.py:14
  411.9 12.9 %collective-permute-start.27 = (f32[2,64,4,256]{3,1,2,0:T(8,128)S(1)}, f32[2,64,4,256]{3,1,2,0:T(8,128)S(1)}, u32[]{:S(2)}, u32[]{:S(2)}) collective-permute-start(f32[2,64,4,256]{3,1,2,0:T(8,128)S(1)} %fusion.11), channel_id=1, source_target_pairs={{0,128},{8,136},{16,144},{24,152},{32,160},{40,168},{48,176},{56,1... | collective-permute-start | bytes 1572872 | tf_op jit(solution)/shard_map/ppermute | solution.py:14
  (26 other events, 342.8 us)
where the time goes:
time: 512 us; the launch traced here: 503 us
  waiting for transfers between devices  211 us (41%)
  blocking collectives  151 us (29%)
  matrix products  53.4 us (10%)
  starting transfers between devices  40.5 us (8%)
  local copies, waits for them, and re-layouts  23.1 us (5%)
  other arithmetic  18.3 us (4%)
  between operations  6.08 us (1%)
    ppermute x20, waiting for transfers between devices, partner(): return lax.ppermute(value, axis, pairs)  189 us
    psum x1, blocking collectives, shards(): first_dot = lax.psum(jnp.sum(residual_start * precond_start), ('gx', 'gy'))  77 us
    psum x1, blocking collectives, shards(): second_dot = lax.psum(jnp.sum(residual * precond_next), ('gx', 'gy'))  74.3 us
    ppermute x20, starting transfers between devices, partner(): return lax.ppermute(value, axis, pairs)  32 us
    dot_general x2, matrix products, precondition(): jnp.einsum('wzb,czyb->cwyb', inverse_block, spectrum, precision=exact_pro...  31.5 us
    ppermute x4, waiting for transfers between devices, padded(): lax.ppermute(lax.slice_in_dim(block, 0, width, axis=dim), axis, backward)  13.3 us
  transfers between devices with their start and end apart: 28, of which 27 were waited for; matrix products, arithmetic and copies ran while one was open for 3% of the time, Pallas kernels for 0%

commit v1 on v0

v1 whole, which is shorter than its diff:
```python
import functools
import math

import jax
import jax.numpy as jnp
import numpy as np
from jax import lax
from jax.experimental import pallas as pl
from jax.experimental.pallas import tpu as pltpu
from jax.sharding import PartitionSpec as P

NZ = 64
ROWS = 4
CELLS = 256
GROUP = 32
COLS = 8
LENGTH = CELLS * GROUP
PLANE = ROWS * NZ
HALF = 128

f32 = jnp.float32
bf16 = jnp.bfloat16


def reverse_bits(number):
    return int(f"{number:05b}"[::-1], 2)


def column_tables():
    residue = np.array([reverse_bits(i) for i in range(GROUP)])
    angle = 2.0 * np.pi * np.outer(residue, np.arange(GROUP)) / GROUP
    same = np.eye(COLS)

    def table(real_row, imag_row):
        pair = np.stack([real_row, imag_row], axis=1)
        full = pair[:, :, None, :, None] * same[None, None, :, None, :]
        return full.reshape(GROUP * 2 * COLS, CELLS).astype(np.float32)

    cosine, sine = np.cos(angle), np.sin(angle)
    return table(cosine, -sine), table(-sine, -cosine)


def wave_table():
    angle = 2.0 * np.pi * np.outer(np.arange(CELLS), np.arange(CELLS)) / CELLS
    cosine, sine = np.cos(angle), np.sin(angle)
    real_rows = np.concatenate([cosine, -sine], axis=1).reshape(GROUP, 1, COLS, 2 * CELLS)
    imag_rows = np.concatenate([sine, cosine], axis=1).reshape(GROUP, 1, COLS, 2 * CELLS)
    full = np.concatenate([real_rows, imag_rows], axis=1).reshape(2 * CELLS, 2 * CELLS)
    full = full.astype(np.float32)
    high = full.astype(jnp.bfloat16)
    low = (full - high.astype(np.float32)).astype(jnp.bfloat16)
    return high, low


def split(values):
    high = values.astype(bf16)
    return high, (values - high.astype(f32)).astype(bf16)


def products(left, right, contract):
    dims = (contract, ((), ()))
    (left_high, left_low), (right_high, right_low) = left, right

    def one(a, b):
        return lax.dot_general(a, b, dims, preferred_element_type=f32)

    return one(left_high, right_high) + (one(left_high, right_low) + one(left_low, right_high))


def lanes_of(shape):
    return lax.broadcasted_iota(jnp.int32, shape, 1)


def roll_half(tile):
    return pltpu.roll(tile, 64, 1)


def low_row_packed(field):
    tile = field[:, :HALF]
    lane = lanes_of((HALF, HALF))
    return jnp.where(lane < 64, tile[:HALF], roll_half(tile[HALF:]))


def high_row_packed(field):
    tile = field[:, HALF:]
    lane = lanes_of((HALF, HALF))
    return jnp.where(lane < 64, roll_half(tile[:HALF]), tile[HALF:])


def behind_rows(field, halo):
    first, second = field[:, :HALF], field[:, HALF:]
    turned, turned_second = roll_half(first), roll_half(second)
    lane = lanes_of(first.shape)
    return jnp.concatenate(
        [jnp.where(lane < 64, halo, turned), jnp.where(lane < 64, turned, turned_second)], axis=1
    )


def before_rows(field, halo):
    first, second = field[:, :HALF], field[:, HALF:]
    turned, turned_second = roll_half(first), roll_half(second)
    lane = lanes_of(first.shape)
    return jnp.concatenate(
        [jnp.where(lane < 64, turned, turned_second), jnp.where(lane < 64, turned_second, halo)], axis=1
    )


def operate(centre, x_pair, y_pair, along, ahead_x, ahead_y):
    along_x, along_y, along_z = along
    plane = lanes_of(centre.shape) % NZ
    first, last = plane == 0, plane == NZ - 1
    ahead_z = jnp.where(last, pltpu.roll(along_z, NZ - 1, 1), pltpu.roll(along_z, PLANE - 1, 1))
    behind_z = jnp.where(first, 0.0, pltpu.roll(centre, 1, 1))
    before_z = jnp.where(last, 0.0, pltpu.roll(centre, PLANE - 1, 1))
    result_x = along_x * (centre - x_pair[0]) + ahead_x * (centre - x_pair[1])
    result_y = along_y * (centre - y_pair[0]) + ahead_y * (centre - y_pair[1])
    result_z = along_z * (centre - behind_z) + ahead_z * (centre - before_z)
    return result_x + result_y + result_z


def turned(ref, lead=()):
    rows = [ref[lead + (slice(None), y, slice(None))] for y in range(ROWS)]
    return jnp.concatenate(rows, axis=0).T


def entry_kernel(place, right_ref, start_ref, cond_ref, left_ref, next_ref, under_ref, over_ref, chunk_ref, residual_ref):
    start = turned(start_ref)
    along = [turned(cond_ref, (axis,)) for axis in range(3)]
    row = lax.broadcasted_iota(jnp.int32, (CELLS, PLANE), 0)
    behind_x = jnp.where(row == 0, left_ref[0:1], pltpu.roll(start, 1, 0))
    before_x = jnp.where(row == CELLS - 1, next_ref[0:1], pltpu.roll(start, CELLS - 1, 0))
    ahead_x = jnp.where(row == CELLS - 1, next_ref[1:2], pltpu.roll(along[0], CELLS - 1, 0))
    under = under_ref[...]
    over = over_ref[...]
    under_t = jnp.concatenate([under, under], axis=0).T
    over_t = jnp.concatenate([over[:NZ], over[:NZ]], axis=0).T
    ahead_t = jnp.concatenate([over[NZ:], over[NZ:]], axis=0).T
    under_t = jnp.where(place[1] == 0, 0.0, under_t)
    over_t = jnp.where(place[1] == place[3] - 1, 0.0, over_t)
    behind_y = behind_rows(start, under_t)
    before_y = before_rows(start, over_t)
    ahead_y = before_rows(along[1], ahead_t)
    image = operate(start, (behind_x, before_x), (behind_y, before_y), along, ahead_x, ahead_y)
    residual = turned(right_ref) - image
    residual_ref[...] = residual
    chunk_ref[:, 0:COLS, :] = residual.reshape(GROUP, COLS, PLANE)
    for axis in range(3):
        low = COLS * (axis + 1)
        chunk_ref[:, low : low + COLS, :] = along[axis].reshape(GROUP, COLS, PLANE)


def table_kernel(cosine_ref, sine_ref, turn_ref, high_ref, low_ref):
    turn = turn_ref[...]
    table = cosine_ref[...] * turn[:, 0:1] + sine_ref[...] * turn[:, 1:2]
    high_ref[...], low_ref[...] = split(table)


def spread_kernel(chunk_ref, high_ref, low_ref, out_ref):
    field = chunk_ref[:, 0:COLS, :].reshape(CELLS, PLANE)
    table = (high_ref[...], low_ref[...])
    out_ref[...] = products(table, split(field), ((1,), (0,))).reshape(GROUP, 2 * COLS, PLANE)


def solve_kernel(which, parts_ref, inverse_ref, high_ref, low_ref, dots_ref, out_ref, sums_ref, wave, solved):
    table = (high_ref[...], low_ref[...])
    parts = parts_ref[...].reshape(2 * CELLS, PLANE).T
    wave[...] = products(split(parts), table, ((1,), (0,)))
    total = jnp.zeros((8, HALF), f32)
    for half in range(2):
        for pair in range(2):
            places = [(2 * pair + y, part * CELLS + half * HALF) for y in range(2) for part in range(2)]

            def step(group, sums):
                tiles = [
                    wave[pl.ds(pl.multiple_of(y * NZ + group * 8, 8), 8), lane : lane + HALF] for y, lane in places
                ]
                for z in range(8):
                    block = inverse_ref[group * 8 + z, :, half * HALF : (half + 1) * HALF]
                    sums = tuple(so_far + block * tile[z : z + 1] for so_far, tile in zip(sums, tiles))
                return sums

            sums = lax.fori_loop(0, NZ // 8, step, tuple(jnp.zeros((NZ, HALF), f32) for _ in places))
            for result, (y, lane) in zip(sums, places):
                solved[y * NZ : (y + 1) * NZ, lane : lane + HALF] = result
                product = result * wave[y * NZ : (y + 1) * NZ, lane : lane + HALF]
                total = total + jnp.sum(product.reshape(NZ // 8, 8, HALF), axis=0)
    row = lax.broadcasted_iota(jnp.int32, (8, HALF), 0)
    sums_ref[...] = dots_ref[...] + jnp.where(row == which, jnp.sum(total, axis=0, keepdims=True) / LENGTH, 0.0)
    out_ref[...] = products(table, split(solved[...]), ((1,), (1,))).reshape(GROUP, 2 * COLS, PLANE)


def gather_field(parts_ref, high_ref, low_ref):
    parts = parts_ref[...].reshape(2 * CELLS, PLANE)
    table = (high_ref[...], low_ref[...])
    return products(table, split(parts), ((0,), (0,))) * (1.0 / LENGTH)


def gather_kernel(parts_ref, high_ref, low_ref, field_ref, edge_low_ref, edge_high_ref, row_low_ref, row_high_ref):
    field = gather_field(parts_ref, high_ref, low_ref)
    field_ref[...] = field
    edges = field.reshape(GROUP, COLS, PLANE)
    edge_low_ref[...] = edges[:, 0, :]
    edge_high_ref[...] = edges[:, COLS - 1, :]
    row_low_ref[...] = low_row_packed(field)
    row_high_ref[...] = high_row_packed(field)


def edge_rows(edge):
    return jnp.broadcast_to(edge[:, None, :], (GROUP, COLS, PLANE)).reshape(CELLS, PLANE)


def image_kernel(
    place,
    field_ref,
    chunk_ref,
    left_ref,
    next_ref,
    under_ref,
    over_ref,
    cond_next_ref,
    cond_over_ref,
    dots_ref,
    high_ref,
    low_ref,
    image_ref,
    parts_ref,
    sums_ref,
):
    field = field_ref[...]
    along = [
        chunk_ref[:, COLS * (axis + 1) : COLS * (axis + 2), :].reshape(CELLS, PLANE) for axis in range(3)
    ]
    column = lax.broadcasted_iota(jnp.int32, (CELLS, PLANE), 0) % COLS
    left, after, cond_after = left_ref[...], next_ref[...], cond_next_ref[...]
    left = jnp.where(place[0] == 0, pltpu.roll(left, 1, 0), left)
    at_end = place[0] == place[2] - 1
    after = jnp.where(at_end, pltpu.roll(after, GROUP - 1, 0), after)
    cond_after = jnp.where(at_end, pltpu.roll(cond_after, GROUP - 1, 0), cond_after)
    behind_x = jnp.where(column == 0, edge_rows(left), pltpu.roll(field, 1, 0))
    before_x = jnp.where(column == COLS - 1, edge_rows(after), pltpu.roll(field, CELLS - 1, 0))
    ahead_x = jnp.where(column == COLS - 1, edge_rows(cond_after), pltpu.roll(along[0], CELLS - 1, 0))
    under, over, cond_over = under_ref[...], over_ref[...], cond_over_ref[...]
    under = jnp.concatenate([under, roll_half(under)], axis=0)
    over = jnp.concatenate([roll_half(over), over], axis=0)
    cond_over = jnp.concatenate([roll_half(cond_over), cond_over], axis=0)
    under = jnp.where(place[1] == 0, 0.0, under)
    over = jnp.where(place[1] == place[3] - 1, 0.0, over)
    behind_y = behind_rows(field, under)
    before_y = before_rows(field, over)
    ahead_y = before_rows(along[1], cond_over)
    image = operate(field, (behind_x, before_x), (behind_y, before_y), along, ahead_x, ahead_y)
    image_ref[...] = image
    table = (high_ref[...], low_ref[...])
    parts_ref[...] = products(table, split(image), ((1,), (0,))).reshape(GROUP, 2 * COLS, PLANE)
    product = field * image
    total = jnp.sum((product[:, :HALF] + product[:, HALF:]), axis=0, keepdims=True)
    row = lax.broadcasted_iota(jnp.int32, (8, HALF), 0)
    sums_ref[...] = dots_ref[...] + jnp.where(row == 1, total, 0.0)


def edges_kernel(chunk_ref, edge_ref, row_ref):
    edge_ref[...] = chunk_ref[:, COLS, :]
    row_ref[...] = low_row_packed(chunk_ref[:, 2 * COLS : 3 * COLS, :].reshape(CELLS, PLANE))


def pack_kernel(parts_ref, high_ref, low_ref, field_ref, image_ref, out_ref):
    out_ref[:, 0:COLS, :] = field_ref[...].reshape(GROUP, COLS, PLANE)
    out_ref[:, COLS : 2 * COLS, :] = image_ref[...].reshape(GROUP, COLS, PLANE)
    latest = gather_field(parts_ref, high_ref, low_ref)
    out_ref[:, 2 * COLS :, :] = latest.reshape(GROUP, COLS, PLANE)


def finish_kernel(packed_ref, start_ref, residual_ref, dots_ref, pressure_out, residual_out, direction_out):
    sums = jnp.sum(dots_ref[...], axis=1, keepdims=True)
    first, curvature, third = sums[0:1], sums[1:2], sums[2:3]
    step = first / curvature
    second = first - 2.0 * step * curvature + step * step * third
    ratio = second / first
    field = packed_ref[:, 0:COLS, :].reshape(CELLS, PLANE)
    image = packed_ref[:, COLS : 2 * COLS, :].reshape(CELLS, PLANE)
    latest = packed_ref[:, 2 * COLS :, :].reshape(CELLS, PLANE)
    change = (step * field).T
    residual = (residual_ref[...] - step * image).T
    direction = ((field - step * latest) + ratio * field).T
    for y in range(ROWS):
        rows = slice(y * NZ, (y + 1) * NZ)
        pressure_out[:, y, :] = start_ref[:, y, :] + change[rows]
        residual_out[:, y, :] = residual[rows]
        direction_out[:, y, :] = direction[rows]


def shape(*dims, dtype=f32):
    return jax.ShapeDtypeStruct(dims, dtype)


def call(kernel, outs, *args, smem=0, scratch=(), cost=0):
    specs = [pl.BlockSpec(memory_space=pltpu.SMEM)] * smem
    specs += [pl.BlockSpec(memory_space=pltpu.VMEM)] * (len(args) - smem)
    many = isinstance(outs, (tuple, list))
    out_spec = pl.BlockSpec(memory_space=pltpu.VMEM)
    return pl.pallas_call(
        kernel,
        out_shape=outs,
        in_specs=specs,
        out_specs=[out_spec] * len(outs) if many else out_spec,
        scratch_shapes=list(scratch),
        compiler_params=pltpu.CompilerParams(vmem_limit_bytes=40 * 1024 * 1024),
        cost_estimate=pl.CostEstimate(flops=cost, bytes_accessed=2**20, transcendentals=0),
    )(*args)


def shift(value, axis, step):
    count = lax.axis_size(axis)
    return lax.ppermute(value, axis, [(i, (i + step) % count) for i in range(count)])


def exchange(parts):
    return lax.all_to_all(parts, "gx", 0, 0, tiled=True)


def all_sum(value):
    for axis in ("gy", "gx"):
        count = lax.axis_size(axis)
        distance = 1
        while distance < count:
            value = value + lax.ppermute(value, axis, [(i, i ^ distance) for i in range(count)])
            distance *= 2
    return value


def shards(right_side, start_pressure, conductance, inverses):
    place = jnp.stack(
        [lax.axis_index("gx"), lax.axis_index("gy"), lax.axis_size("gx"), lax.axis_size("gy")]
    ).astype(jnp.int32)
    field_shape = shape(CELLS, PLANE)
    parts_shape = shape(GROUP, 2 * COLS, PLANE)
    edge_shape, row_shape, dots_shape = shape(GROUP, PLANE), shape(HALF, HALF), shape(8, HALF)

    def column(values):
        return values.T.reshape(1, PLANE)

    along_x, along_y = conductance[0], conductance[1]
    to_left = jnp.concatenate([column(start_pressure[:, :, 0]), column(along_x[:, :, 0])], axis=0)
    to_right = column(start_pressure[:, :, CELLS - 1])
    to_under = jnp.concatenate([start_pressure[:, 0, :], along_y[:, 0, :]], axis=0)
    to_over = start_pressure[:, ROWS - 1, :]
    under = shift(to_over, "gy", 1)
    over = shift(to_under, "gy", -1)
    left = shift(to_right, "gx", 1)
    after = shift(to_left, "gx", -1)

    cosine_table, sine_table = column_tables()
    residues = jnp.asarray([reverse_bits(i) for i in range(GROUP)], jnp.int32)
    columns = lax.axis_index("gx") * COLS + jnp.arange(COLS, dtype=jnp.int32)
    angle = (residues[:, None] * columns[None, :]).astype(f32) * (2.0 * math.pi / LENGTH)
    turn = jnp.stack([jnp.cos(angle), jnp.sin(angle)], axis=-1)
    turn = jnp.broadcast_to(turn[:, None], (GROUP, 2, COLS, 2)).reshape(2 * CELLS, 2)
    table = call(
        table_kernel,
        [shape(2 * CELLS, CELLS, dtype=bf16)] * 2,
        jnp.asarray(cosine_table),
        jnp.asarray(sine_table),
        turn,
    )
    waves = [jnp.asarray(part) for part in wave_table()]
    inverse = inverses.reshape(inverses.shape[1:])

    def solve(which, parts, dots):
        return call(
            functools.partial(solve_kernel, which),
            [parts_shape, dots_shape],
            parts,
            inverse,
            *waves,
            dots,
            scratch=[pltpu.VMEM((PLANE, 2 * CELLS), f32)] * 2,
            cost=2 * 10**9,
        )

    chunk, residual = call(
        entry_kernel,
        [shape(GROUP, 4 * COLS, PLANE), field_shape],
        place,
        right_side,
        start_pressure,
        conductance,
        left,
        after,
        under,
        over,
        smem=1,
    )
    chunk = exchange(chunk)
    parts = exchange(call(spread_kernel, parts_shape, chunk, *table))
    cond_edge, cond_row = call(edges_kernel, [edge_shape, row_shape], chunk)
    cond_after = shift(cond_edge, "gx", -1)
    cond_over = shift(cond_row, "gy", -1)
    parts, dots = solve(0, parts, jnp.zeros((8, HALF), f32))
    parts = exchange(parts)
    field, edge_low, edge_high, row_low, row_high = call(
        gather_kernel, [field_shape, edge_shape, edge_shape, row_shape, row_shape], parts, *table
    )
    under = shift(row_high, "gy", 1)
    over = shift(row_low, "gy", -1)
    left = shift(edge_high, "gx", 1)
    after = shift(edge_low, "gx", -1)
    image, parts, dots = call(
        image_kernel,
        [field_shape, parts_shape, dots_shape],
        place,
        field,
        chunk,
        left,
        after,
        under,
        over,
        cond_after,
        cond_over,
        dots,
        *table,
        smem=1,
    )
    parts, dots = solve(2, exchange(parts), dots)
    dots = all_sum(dots)
    parts = exchange(parts)
    packed = exchange(call(pack_kernel, shape(GROUP, 3 * COLS, PLANE), parts, *table, field, image))
    cells = shape(NZ, ROWS, CELLS)
    return tuple(call(finish_kernel, [cells] * 3, packed, start_pressure, residual, dots))


def solution(mesh):
    placed = (
        P(None, "gy", "gx"),
        P(None, "gy", "gx"),
        P(None, None, "gy", "gx"),
        P("gx", None, None, None),
    )
    return jax.shard_map(
        shards,
        mesh=mesh,
        in_specs=placed,
        out_specs=(P(None, "gy", "gx"), P(None, "gy", "gx"), P(None, "gy", "gx")),
        check_vma=False,
    )
```

time: 512 us -> 177 us (0.35); the launches traced: 503 us -> 176 us
  waiting for transfers between devices: 211 us -> 48.9 us
  blocking collectives: 151 us -> 52 us
  matrix products: 53.4 us -> 0 us
  other arithmetic: 18.3 us -> 0.25 us
  Pallas kernels: 0 us -> 16.6 us
  local copies, waits for them, and re-layouts: 23.1 us -> 10.5 us
  starting transfers between devices: 40.5 us -> 47.4 us
  between operations: 6.08 us -> 0.91 us
    ppermute x28 -> x18, waiting for transfers between devices: 211 us -> 25 us  [the longest x8 22.1 us: all_sum(): lax.ppermute(value, axis, [(i, i ^ distance) for i in range(count)])]
    psum x2 -> x0, blocking collectives: 151 us -> none  [the longest x1 77 us: shards(): first_dot = lax.psum(jnp.sum(residual_start * precond_start), ('gx', 'gy'))]
    dot_general x18 -> x0, matrix products: 53.4 us -> none  [the longest x2 31.5 us: precondition(): jnp.einsum('wzb,czyb->cwyb', inverse_block, spectrum, precision=exact_pro...]
    all_to_all x0 -> x3, blocking collectives: none -> 52 us  [exchange(): return lax.all_to_all(parts, 'gx', 0, 0, tiled=True)]
    all_to_all x0 -> x3, waiting for transfers between devices: none -> 23.8 us  [exchange(): return lax.all_to_all(parts, 'gx', 0, 0, tiled=True)]
    all_to_all x0 -> x3, starting transfers between devices: none -> 20.4 us  [exchange(): return lax.all_to_all(parts, 'gx', 0, 0, tiled=True)]
    pallas_call x0 -> x10, Pallas kernels: none -> 16.6 us  [call(): pl.pallas_call(kernel, out_shape=outs, in_specs=specs, out_specs=[out_spe...]
    ppermute x28 -> x18, starting transfers between devices: 40.5 us -> 27 us  [the longest x10 14.8 us: shift(): lax.ppermute(value, axis, [(i, (i + step) % count) for i in range(count)])]
  transfers between devices with their start and end apart: 28 -> 21, of which waited for: 27 -> 13; matrix products, arithmetic and copies ran while one was open for 3% -> 2% of each run, Pallas kernels for 0% -> 0%
where the time goes in v1:
time: 177 us; the launch traced here: 176 us
  blocking collectives  52 us (29%)
  waiting for transfers between devices  48.9 us (28%)
  starting transfers between devices  47.4 us (27%)
  Pallas kernels  16.6 us (9%)
  local copies, waits for them, and re-layouts  10.5 us (6%)
    all_to_all x3, blocking collectives, exchange(): return lax.all_to_all(parts, 'gx', 0, 0, tiled=True)  52 us
    all_to_all x3, waiting for transfers between devices, exchange(): return lax.all_to_all(parts, 'gx', 0, 0, tiled=True)  23.8 us
    ppermute x8, waiting for transfers between devices, all_sum(): lax.ppermute(value, axis, [(i, i ^ distance) for i in range(count)])  22.1 us
    all_to_all x3, starting transfers between devices, exchange(): return lax.all_to_all(parts, 'gx', 0, 0, tiled=True)  20.4 us
    pallas_call x10, Pallas kernels, call(): pl.pallas_call(kernel, out_shape=outs, in_specs=specs, out_specs=[out_spe...  16.6 us
    ppermute x10, starting transfers between devices, shift(): lax.ppermute(value, axis, [(i, (i + step) % count) for i in range(count)])  14.8 us
    ppermute x8, starting transfers between devices, all_sum(): lax.ppermute(value, axis, [(i, i ^ distance) for i in range(count)])  12.2 us
    unnamed x27, local copies, waits for them, and re-layouts  6.28 us
  transfers between devices with their start and end apart: 21, of which 13 were waited for; matrix products, arithmetic and copies ran while one was open for 2% of the time, Pallas kernels for 0%

profile of v1, /device:TPU:2, one launch (start us, length us, event | category | flops | bytes accessed | tf_op | source)
XLA Modules:
  0.0 176.5 jit_solution(4052347886453402468)
XLA Ops:
  6.4 4.0 %collective-permute-start.3 = (f32[128,256]{1,0:T(8,128)S(1)}, f32[128,256]{1,0:T(8,128)S(1)}, u32[]{:S(2)}, u32[]{:S(2)}) collective-permute-start(f32[128,256]{1,0:T(8,128)S(1)} %pad_maximum_fusion), channel_id=1, source_target_pairs={{0,7},{1,0},{2,1},{3,2},{4,3},{5,4},{6,5},{7,6},{8,15},{9,8},{10,9... | collective-permute-start | bytes 393224 | tf_op jit(solution)/shard_map/ppermute | solution.py:314
  15.7 2.7 %shard_map.112 = (f32[32,32,256]{2,1,0:T(8,128)}, f32[256,256]{1,0:T(8,128)S(1)}) custom-call(s32[4]{0:T(128)S(1)} %pad_add_fusion.place, f32[64,4,256]{2,1,0:T(4,128)S(1)} %copy-done.5, f32[64,4,256]{2,1,0:T(4,128)S(1)} %copy-done, f32[3,64,4,256]{3,2,1,0:T(4,128)S(1)} %copy-done.2, f32[1,256]{1,0:T(1,128)S(1)} %collective-permute-done.left_ref, ...), custom_call_target="tpu_custom_call" | custom-call | bytes 1048576 | tf_op jit(solution)/shard_map/pallas_call | solution.py:301
  18.4 10.3 %all-to-all-start = ((f32[32,32,256]{2,1,0:T(8,128)}), f32[32,32,256]{2,1,0:T(8,128)S(1)}, u32[]{:S(2)}, u32[]{:S(2)}) async-start(f32[32,32,256]{2,1,0:T(8,128)} %get-tuple-element.21), calls=%async_computation | async-start | bytes 2097152 | tf_op jit(solution)/shard_map/all_to_all | solution.py:318
  29.3 15.5 %all-to-all-done.chunk_ref = f32[32,32,256]{2,1,0:T(8,128)S(1)} async-done(((f32[32,32,256]{2,1,0:T(8,128)}), f32[32,32,256]{2,1,0:T(8,128)S(1)}, u32[]{:S(2)}, u32[]{:S(2)}) %all-to-all-start) | async-done | bytes 1048608 | tf_op jit(solution)/shard_map/all_to_all | solution.py:318
  45.2 15.1 %all_to_all.30.parts_ref = f32[32,16,256]{2,1,0:T(8,128)S(1)} all-to-all(f32[32,16,256]{2,1,0:T(8,128)S(1)} %shard_map.114), channel_id=1, replica_groups=mesh['gx'=32,'gy'=8] {'gx'}, dimensions={0} | all-to-all | bytes 1048576 | tf_op jit(solution)/shard_map/all_to_all | solution.py:318
  60.3 2.2 %copy-done.6 = f32[1,64,64,256]{3,2,1,0:T(8,128)S(1)} copy-done((f32[1,64,64,256]{3,2,1,0:T(8,128)S(1)}, f32[1,64,64,256]{3,2,1,0:T(8,128)}, u32[]{:S(2)}) %copy-start.6) | copy-done | bytes 4194328
  63.5 4.6 %shard_map.115 = (f32[32,16,256]{2,1,0:T(8,128)}, f32[8,128]{1,0:T(8,128)S(1)}) custom-call(f32[32,16,256]{2,1,0:T(8,128)S(1)} %all_to_all.30.parts_ref, f32[64,64,256]{2,1,0:T(8,128)S(1)} %bitcast.27, bf16[512,512]{1,0:T(8,128)(2,1)S(1)} %copy-done.9, bf16[512,512]{1,0:T(8,128)(2,1)S(1)} %copy-done.8, f32[8,128]{1,0:T(8,128)S(1)} %broadcast_in_dim.5.dots_ref), custom_call_target="tpu_custom_call" | custom-call | flops 2000000000 | bytes 1048576 | tf_op jit(solution)/shard_map/pallas_call | solution.py:301
  68.1 5.0 %all-to-all-start.2 = ((f32[32,16,256]{2,1,0:T(8,128)}), f32[32,16,256]{2,1,0:T(8,128)S(1)}, u32[]{:S(2)}, u32[]{:S(2)}) async-start(f32[32,16,256]{2,1,0:T(8,128)} %get-tuple-element.24), calls=%async_computation.2 | async-start | bytes 1048576 | tf_op jit(solution)/shard_map/all_to_all | solution.py:318
  75.5 8.3 %all-to-all-done.2.parts_ref = f32[32,16,256]{2,1,0:T(8,128)S(1)} async-done(((f32[32,16,256]{2,1,0:T(8,128)}), f32[32,16,256]{2,1,0:T(8,128)S(1)}, u32[]{:S(2)}, u32[]{:S(2)}) %all-to-all-start.2) | async-done | bytes 524320 | tf_op jit(solution)/shard_map/all_to_all | solution.py:318
  84.3 3.2 %collective-permute-start.7 = (f32[128,128]{1,0:T(8,128)S(1)}, f32[128,128]{1,0:T(8,128)S(1)}, u32[]{:S(2)}, u32[]{:S(2)}) collective-permute-start(f32[128,128]{1,0:T(8,128)S(1)} %get-tuple-element.29), channel_id=1, source_target_pairs={{0,7},{1,0},{2,1},{3,2},{4,3},{5,4},{6,5},{7,6},{8,15},{9,8},{10,9... | collective-permute-start | bytes 196616 | tf_op jit(solution)/shard_map/ppermute | solution.py:314
  92.4 21.6 %all_to_all.31.parts_ref = f32[32,16,256]{2,1,0:T(8,128)S(1)} all-to-all(f32[32,16,256]{2,1,0:T(8,128)S(1)} %get-tuple-element.33), channel_id=1, replica_groups=mesh['gx'=32,'gy'=8] {'gx'}, dimensions={0} | all-to-all | bytes 1048576 | tf_op jit(solution)/shard_map/all_to_all | solution.py:318
  115.0 4.0 %shard_map.119 = (f32[32,16,256]{2,1,0:T(8,128)S(1)}, f32[8,128]{1,0:T(8,128)S(1)}) custom-call(f32[32,16,256]{2,1,0:T(8,128)S(1)} %all_to_all.31.parts_ref, f32[64,64,256]{2,1,0:T(8,128)S(1)} %bitcast.28, bf16[512,512]{1,0:T(8,128)(2,1)S(1)} %copy-done.10, bf16[512,512]{1,0:T(8,128)(2,1)S(1)} %copy-done.8, f32[8,128]{1,0:T(8,128)S(1)} %get-tuple-element.34.dots_ref), custom_call_target="tpu_custom_call" | custom-call | flops 2000000000 | bytes 1048576 | tf_op jit(solution)/shard_map/pallas_call | solution.py:301
  119.1 15.4 %all_to_all.32.parts_ref = f32[32,16,256]{2,1,0:T(8,128)S(1)} all-to-all(f32[32,16,256]{2,1,0:T(8,128)S(1)} %get-tuple-element.35), channel_id=1, replica_groups=mesh['gx'=32,'gy'=8] {'gx'}, dimensions={0} | all-to-all | bytes 1048576 | tf_op jit(solution)/shard_map/all_to_all | solution.py:318
  135.7 5.1 %all-to-all-start.5 = ((f32[32,24,256]{2,1,0:T(8,128)}), f32[32,24,256]{2,1,0:T(8,128)S(1)}, u32[]{:S(2)}, u32[]{:S(2)}) async-start(f32[32,24,256]{2,1,0:T(8,128)} %shard_map.120), calls=%async_computation.5 | async-start | bytes 1572864 | tf_op jit(solution)/shard_map/all_to_all | solution.py:318
  140.9 3.6 %collective-permute-done.10 = f32[8,128]{1,0:T(8,128)S(1)} collective-permute-done((f32[8,128]{1,0:T(8,128)S(1)}, f32[8,128]{1,0:T(8,128)S(1)}, u32[]{:S(2)}, u32[]{:S(2)}) %collective-permute-start.10) | collective-permute-done | bytes 4128 | tf_op jit(solution)/shard_map/ppermute | solution.py:326
  145.0 4.0 %collective-permute-done.11 = f32[8,128]{1,0:T(8,128)S(1)} collective-permute-done((f32[8,128]{1,0:T(8,128)S(1)}, f32[8,128]{1,0:T(8,128)S(1)}, u32[]{:S(2)}, u32[]{:S(2)}) %collective-permute-start.11) | collective-permute-done | bytes 4128 | tf_op jit(solution)/shard_map/ppermute | solution.py:326
  149.0 4.6 %collective-permute-start.12 = (f32[8,128]{1,0:T(8,128)S(1)}, f32[8,128]{1,0:T(8,128)S(1)}, u32[]{:S(2)}, u32[]{:S(2)}) collective-permute-start(f32[8,128]{1,0:T(8,128)S(1)} %add.37), channel_id=1, source_target_pairs={{0,4},{1,5},{2,6},{3,7},{4,0},{5,1},{6,2},{7,3},{8,12},{9,13},{10,... | collective-permute-start | bytes 12296 | tf_op jit(solution)/shard_map/ppermute | solution.py:326
  153.6 3.0 %collective-permute-done.12 = f32[8,128]{1,0:T(8,128)S(1)} collective-permute-done((f32[8,128]{1,0:T(8,128)S(1)}, f32[8,128]{1,0:T(8,128)S(1)}, u32[]{:S(2)}, u32[]{:S(2)}) %collective-permute-start.12) | collective-permute-done | bytes 4128 | tf_op jit(solution)/shard_map/ppermute | solution.py:326
  158.1 3.3 %collective-permute-done.14 = f32[8,128]{1,0:T(8,128)S(1)} collective-permute-done((f32[8,128]{1,0:T(8,128)S(1)}, f32[8,128]{1,0:T(8,128)S(1)}, u32[]{:S(2)}, u32[]{:S(2)}) %collective-permute-start.14) | collective-permute-done | bytes 4128 | tf_op jit(solution)/shard_map/ppermute | solution.py:326
  161.3 2.1 %collective-permute-start.15 = (f32[8,128]{1,0:T(8,128)S(1)}, f32[8,128]{1,0:T(8,128)S(1)}, u32[]{:S(2)}, u32[]{:S(2)}) collective-permute-start(f32[8,128]{1,0:T(8,128)S(1)} %add.40), channel_id=1, source_target_pairs={{0,32},{8,40},{16,48},{24,56},{32,0},{40,8},{48,16},{56,24},{64,96... | collective-permute-start | bytes 12296 | tf_op jit(solution)/shard_map/ppermute | solution.py:326
  163.4 3.0 %collective-permute-done.15 = f32[8,128]{1,0:T(8,128)S(1)} collective-permute-done((f32[8,128]{1,0:T(8,128)S(1)}, f32[8,128]{1,0:T(8,128)S(1)}, u32[]{:S(2)}, u32[]{:S(2)}) %collective-permute-start.15) | collective-permute-done | bytes 4128 | tf_op jit(solution)/shard_map/ppermute | solution.py:326
  168.0 2.1 %collective-permute-done.16 = f32[8,128]{1,0:T(8,128)S(1)} collective-permute-done((f32[8,128]{1,0:T(8,128)S(1)}, f32[8,128]{1,0:T(8,128)S(1)}, u32[]{:S(2)}, u32[]{:S(2)}) %collective-permute-start.16) | collective-permute-done | bytes 4128 | tf_op jit(solution)/shard_map/ppermute | solution.py:326
  170.1 3.1 %collective-permute-start.17 = (f32[8,128]{1,0:T(8,128)S(1)}, f32[8,128]{1,0:T(8,128)S(1)}, u32[]{:S(2)}, u32[]{:S(2)}) collective-permute-start(f32[8,128]{1,0:T(8,128)S(1)} %add.42), channel_id=1, source_target_pairs={{0,128},{8,136},{16,144},{24,152},{32,160},{40,168},{48,176},{56,1... | collective-permute-start | bytes 12296 | tf_op jit(solution)/shard_map/ppermute | solution.py:326
  173.1 2.0 %collective-permute-done.17 = f32[8,128]{1,0:T(8,128)S(1)} collective-permute-done((f32[8,128]{1,0:T(8,128)S(1)}, f32[8,128]{1,0:T(8,128)S(1)}, u32[]{:S(2)}, u32[]{:S(2)}) %collective-permute-start.17) | collective-permute-done | bytes 4128 | tf_op jit(solution)/shard_map/ppermute | solution.py:326
  (86 shorter events, 27.8 us)
Async XLA Ops:
  2.0 11.8 %collective-permute-start.2 = (f32[64,256]{1,0:T(8,128)S(1)}, f32[64,256]{1,0:T(8,128)S(1)}, u32[]{:S(2)}, u32[]{:S(2)}) collective-permute-start(f32[64,256]{1,0:T(8,128)S(1)} %bitcast.31), channel_id=1, source_target_pairs={{0,1},{1,2},{2,3},{3,4},{4,5},{5,6},{6,7},{7,0},{8,9},{9,10},{10,1... | collective-permute-start | bytes 196616 | tf_op jit(solution)/shard_map/ppermute | solution.py:314
  5.2 7.2 %collective-permute-start = (f32[1,256]{1,0:T(1,128)S(1)}, f32[1,256]{1,0:T(1,128)S(1)}, u32[]{:S(2)}, u32[]{:S(2)}) collective-permute-start(f32[1,256]{1,0:T(1,128)S(1)} %reshape.121), channel_id=1, source_target_pairs={{0,8},{8,16},{16,24},{24,32},{32,40},{40,48},{48,56},{56,64},{64,7... | collective-permute-start | bytes 3080 | tf_op jit(solution)/shard_map/ppermute | solution.py:314
  6.4 7.4 %collective-permute-start.3 = (f32[128,256]{1,0:T(8,128)S(1)}, f32[128,256]{1,0:T(8,128)S(1)}, u32[]{:S(2)}, u32[]{:S(2)}) collective-permute-start(f32[128,256]{1,0:T(8,128)S(1)} %pad_maximum_fusion), channel_id=1, source_target_pairs={{0,7},{1,0},{2,1},{3,2},{4,3},{5,4},{6,5},{7,6},{8,15},{9,8},{10,9... | collective-permute-start | bytes 393224 | tf_op jit(solution)/shard_map/ppermute | solution.py:314
  10.9 2.8 %collective-permute-start.1 = (f32[2,256]{1,0:T(2,128)S(1)}, f32[2,256]{1,0:T(2,128)S(1)}, u32[]{:S(2)}, u32[]{:S(2)}) collective-permute-start(f32[2,256]{1,0:T(2,128)S(1)} %pad_maximum_fusion.2), channel_id=1, source_target_pairs={{0,248},{8,0},{16,8},{24,16},{32,24},{40,32},{48,40},{56,48},{64,5... | collective-permute-start | bytes 6152 | tf_op jit(solution)/shard_map/ppermute | solution.py:314
  15.7 44.6 %copy-start.8 = (bf16[512,512]{1,0:T(8,128)(2,1)S(1)}, bf16[512,512]{1,0:T(8,128)(2,1)}, u32[]{:S(2)}) copy-start(bf16[512,512]{1,0:T(8,128)(2,1)} %constant.33.clone.low_ref) | copy-start | bytes 1572868
  18.4 26.4 %all-to-all-start = ((f32[32,32,256]{2,1,0:T(8,128)}), f32[32,32,256]{2,1,0:T(8,128)S(1)}, u32[]{:S(2)}, u32[]{:S(2)}) async-start(f32[32,32,256]{2,1,0:T(8,128)} %get-tuple-element.21), calls=%async_computation | async-start | bytes 2097152 | tf_op jit(solution)/shard_map/all_to_all | solution.py:318
  68.1 15.7 %all-to-all-start.2 = ((f32[32,16,256]{2,1,0:T(8,128)}), f32[32,16,256]{2,1,0:T(8,128)S(1)}, u32[]{:S(2)}, u32[]{:S(2)}) async-start(f32[32,16,256]{2,1,0:T(8,128)} %get-tuple-element.24), calls=%async_computation.2 | async-start | bytes 1048576 | tf_op jit(solution)/shard_map/all_to_all | solution.py:318
  73.3 14.3 %collective-permute-start.8 = (f32[32,256]{1,0:T(8,128)S(1)}, f32[32,256]{1,0:T(8,128)S(1)}, u32[]{:S(2)}, u32[]{:S(2)}) collective-permute-start(f32[32,256]{1,0:T(8,128)S(1)} %get-tuple-element.30), channel_id=1, source_target_pairs={{0,248},{8,0},{16,8},{24,16},{32,24},{40,32},{48,40},{56,48},{64,5... | collective-permute-start | bytes 98312 | tf_op jit(solution)/shard_map/ppermute | solution.py:314
  73.4 15.9 %collective-permute-start.9 = (f32[128,128]{1,0:T(8,128)S(1)}, f32[128,128]{1,0:T(8,128)S(1)}, u32[]{:S(2)}, u32[]{:S(2)}) collective-permute-start(f32[128,128]{1,0:T(8,128)S(1)} %get-tuple-element.31), channel_id=1, source_target_pairs={{0,7},{1,0},{2,1},{3,2},{4,3},{5,4},{6,5},{7,6},{8,15},{9,8},{10,9... | collective-permute-start | bytes 196616 | tf_op jit(solution)/shard_map/ppermute | solution.py:314
  83.8 30.2 %copy-start.7 = (f32[1,64,64,256]{3,2,1,0:T(8,128)S(1)}, f32[1,64,64,256]{3,2,1,0:T(8,128)}, u32[]{:S(2)}) copy-start(f32[1,64,64,256]{3,2,1,0:T(8,128)} %param.12) | copy-start | bytes 12582916
  84.3 6.7 %collective-permute-start.6 = (f32[128,128]{1,0:T(8,128)S(1)}, f32[128,128]{1,0:T(8,128)S(1)}, u32[]{:S(2)}, u32[]{:S(2)}) collective-permute-start(f32[128,128]{1,0:T(8,128)S(1)} %get-tuple-element.28), channel_id=1, source_target_pairs={{0,1},{1,2},{2,3},{3,4},{4,5},{5,6},{6,7},{7,0},{8,9},{9,10},{10,1... | collective-permute-start | bytes 196616 | tf_op jit(solution)/shard_map/ppermute | solution.py:314
  84.3 6.6 %collective-permute-start.7 = (f32[128,128]{1,0:T(8,128)S(1)}, f32[128,128]{1,0:T(8,128)S(1)}, u32[]{:S(2)}, u32[]{:S(2)}) collective-permute-start(f32[128,128]{1,0:T(8,128)S(1)} %get-tuple-element.29), channel_id=1, source_target_pairs={{0,7},{1,0},{2,1},{3,2},{4,3},{5,4},{6,5},{7,6},{8,15},{9,8},{10,9... | collective-permute-start | bytes 196616 | tf_op jit(solution)/shard_map/ppermute | solution.py:314
  87.6 3.3 %collective-permute-start.4 = (f32[32,256]{1,0:T(8,128)S(1)}, f32[32,256]{1,0:T(8,128)S(1)}, u32[]{:S(2)}, u32[]{:S(2)}) collective-permute-start(f32[32,256]{1,0:T(8,128)S(1)} %get-tuple-element.26), channel_id=1, source_target_pairs={{0,8},{8,16},{16,24},{24,32},{32,40},{40,48},{48,56},{56,64},{64,7... | collective-permute-start | bytes 98312 | tf_op jit(solution)/shard_map/ppermute | solution.py:314
  87.6 3.3 %collective-permute-start.5 = (f32[32,256]{1,0:T(8,128)S(1)}, f32[32,256]{1,0:T(8,128)S(1)}, u32[]{:S(2)}, u32[]{:S(2)}) collective-permute-start(f32[32,256]{1,0:T(8,128)S(1)} %get-tuple-element.27), channel_id=1, source_target_pairs={{0,248},{8,0},{16,8},{24,16},{32,24},{40,32},{48,40},{56,48},{64,5... | collective-permute-start | bytes 98312 | tf_op jit(solution)/shard_map/ppermute | solution.py:314
  119.1 56.1 %copy-start.1 = (f32[64,4,256]{2,1,0:T(4,128)S(1)}, f32[64,4,256]{2,1,0:T(4,128)}, u32[]{:S(2)}) copy-start(f32[64,4,256]{2,1,0:T(4,128)} %start_ref.3) | copy-start | bytes 786436
  135.7 39.4 %all-to-all-start.5 = ((f32[32,24,256]{2,1,0:T(8,128)}), f32[32,24,256]{2,1,0:T(8,128)S(1)}, u32[]{:S(2)}, u32[]{:S(2)}) async-start(f32[32,24,256]{2,1,0:T(8,128)} %shard_map.120), calls=%async_computation.5 | async-start | bytes 1572864 | tf_op jit(solution)/shard_map/all_to_all | solution.py:318
  140.8 3.7 %collective-permute-start.10 = (f32[8,128]{1,0:T(8,128)S(1)}, f32[8,128]{1,0:T(8,128)S(1)}, u32[]{:S(2)}, u32[]{:S(2)}) collective-permute-start(f32[8,128]{1,0:T(8,128)S(1)} %get-tuple-element.38), channel_id=1, source_target_pairs={{0,1},{1,0},{2,3},{3,2},{4,5},{5,4},{6,7},{7,6},{8,9},{9,8},{10,11... | collective-permute-start | bytes 12296 | tf_op jit(solution)/shard_map/ppermute | solution.py:326
  144.5 4.5 %collective-permute-start.11 = (f32[8,128]{1,0:T(8,128)S(1)}, f32[8,128]{1,0:T(8,128)S(1)}, u32[]{:S(2)}, u32[]{:S(2)}) collective-permute-start(f32[8,128]{1,0:T(8,128)S(1)} %add.36), channel_id=1, source_target_pairs={{0,2},{1,3},{2,0},{3,1},{4,6},{5,7},{6,4},{7,5},{8,10},{9,11},{10,... | collective-permute-start | bytes 12296 | tf_op jit(solution)/shard_map/ppermute | solution.py:326
  149.0 7.5 %collective-permute-start.12 = (f32[8,128]{1,0:T(8,128)S(1)}, f32[8,128]{1,0:T(8,128)S(1)}, u32[]{:S(2)}, u32[]{:S(2)}) collective-permute-start(f32[8,128]{1,0:T(8,128)S(1)} %add.37), channel_id=1, source_target_pairs={{0,4},{1,5},{2,6},{3,7},{4,0},{5,1},{6,2},{7,3},{8,12},{9,13},{10,... | collective-permute-start | bytes 12296 | tf_op jit(solution)/shard_map/ppermute | solution.py:326
  156.5 1.2 collective-permute-start.13
  157.7 3.6 %collective-permute-start.14 = (f32[8,128]{1,0:T(8,128)S(1)}, f32[8,128]{1,0:T(8,128)S(1)}, u32[]{:S(2)}, u32[]{:S(2)}) collective-permute-start(f32[8,128]{1,0:T(8,128)S(1)} %add.39), channel_id=1, source_target_pairs={{0,16},{8,24},{16,0},{24,8},{32,48},{40,56},{48,32},{56,40},{64,80... | collective-permute-start | bytes 12296 | tf_op jit(solution)/shard_map/ppermute | solution.py:326
  161.3 5.1 %collective-permute-start.15 = (f32[8,128]{1,0:T(8,128)S(1)}, f32[8,128]{1,0:T(8,128)S(1)}, u32[]{:S(2)}, u32[]{:S(2)}) collective-permute-start(f32[8,128]{1,0:T(8,128)S(1)} %add.40), channel_id=1, source_target_pairs={{0,32},{8,40},{16,48},{24,56},{32,0},{40,8},{48,16},{56,24},{64,96... | collective-permute-start | bytes 12296 | tf_op jit(solution)/shard_map/ppermute | solution.py:326
  166.4 3.6 %collective-permute-start.16 = (f32[8,128]{1,0:T(8,128)S(1)}, f32[8,128]{1,0:T(8,128)S(1)}, u32[]{:S(2)}, u32[]{:S(2)}) collective-permute-start(f32[8,128]{1,0:T(8,128)S(1)} %add.41), channel_id=1, source_target_pairs={{0,64},{8,72},{16,80},{24,88},{32,96},{40,104},{48,112},{56,120},{... | collective-permute-start | bytes 12296 | tf_op jit(solution)/shard_map/ppermute | solution.py:326
  170.1 5.1 %collective-permute-start.17 = (f32[8,128]{1,0:T(8,128)S(1)}, f32[8,128]{1,0:T(8,128)S(1)}, u32[]{:S(2)}, u32[]{:S(2)}) collective-permute-start(f32[8,128]{1,0:T(8,128)S(1)} %add.42), channel_id=1, source_target_pairs={{0,128},{8,136},{16,144},{24,152},{32,160},{40,168},{48,176},{56,1... | collective-permute-start | bytes 12296 | tf_op jit(solution)/shard_map/ppermute | solution.py:326
  (9 other events, 104.2 us)

commit v2 on v1

v2 whole, which is shorter than its diff:
```python
import functools
import math

import jax
import jax.numpy as jnp
import numpy as np
from jax import lax
from jax.experimental import pallas as pl
from jax.experimental.pallas import tpu as pltpu
from jax.sharding import PartitionSpec as P

NZ = 64
ROWS = 4
CELLS = 256
GROUP = 32
COLS = 8
LENGTH = CELLS * GROUP
PLANE = ROWS * NZ
HALF = 128

f32 = jnp.float32
bf16 = jnp.bfloat16


def reverse_bits(number):
    return int(f"{number:05b}"[::-1], 2)


def column_tables():
    residue = np.array([reverse_bits(i) for i in range(GROUP)])
    angle = 2.0 * np.pi * np.outer(residue, np.arange(GROUP)) / GROUP
    same = np.eye(COLS)

    def table(real_row, imag_row):
        pair = np.stack([real_row, imag_row], axis=1)
        full = pair[:, :, None, :, None] * same[None, None, :, None, :]
        return full.reshape(GROUP * 2 * COLS, CELLS).astype(np.float32)

    cosine, sine = np.cos(angle), np.sin(angle)
    return table(cosine, -sine), table(-sine, -cosine)


def edge_tables():
    residue = np.array([reverse_bits(i) for i in range(GROUP)])
    angle = 2.0 * np.pi * np.outer(residue, np.arange(GROUP)) / GROUP
    same = np.eye(4).reshape(2, 2, 2, 2)

    def table(real_row, imag_row):
        pair = np.stack([real_row, imag_row], axis=1)
        full = pair[:, None, None, :, None, None, :] * same[None, :, :, None, :, :, None]
        return full.reshape(GROUP * 8, 4 * GROUP).astype(np.float32)

    cosine, sine = np.cos(angle), np.sin(angle)
    return table(cosine, -sine), table(-sine, -cosine)


def wave_table():
    angle = 2.0 * np.pi * np.outer(np.arange(CELLS), np.arange(CELLS)) / CELLS
    cosine, sine = np.cos(angle), np.sin(angle)
    real_rows = np.concatenate([cosine, -sine], axis=1).reshape(GROUP, 1, COLS, 2 * CELLS)
    imag_rows = np.concatenate([sine, cosine], axis=1).reshape(GROUP, 1, COLS, 2 * CELLS)
    full = np.concatenate([real_rows, imag_rows], axis=1).reshape(2 * CELLS, 2 * CELLS)
    full = full.astype(np.float32)
    high = full.astype(jnp.bfloat16)
    low = (full - high.astype(np.float32)).astype(jnp.bfloat16)
    return high, low


def split(values):
    high = values.astype(bf16)
    return high, (values - high.astype(f32)).astype(bf16)


def products(left, right, contract):
    dims = (contract, ((), ()))
    (left_high, left_low), (right_high, right_low) = left, right

    def one(a, b):
        return lax.dot_general(a, b, dims, preferred_element_type=f32)

    return one(left_high, right_high) + (one(left_high, right_low) + one(left_low, right_high))


def lanes_of(shape):
    return lax.broadcasted_iota(jnp.int32, shape, 1)


def roll_half(tile):
    return pltpu.roll(tile, 64, 1)


def low_row_packed(field):
    tile = field[:, :HALF]
    lane = lanes_of((HALF, HALF))
    return jnp.where(lane < 64, tile[:HALF], roll_half(tile[HALF:]))


def high_row_packed(field):
    tile = field[:, HALF:]
    lane = lanes_of((HALF, HALF))
    return jnp.where(lane < 64, roll_half(tile[:HALF]), tile[HALF:])


def behind_rows(field, halo):
    first, second = field[:, :HALF], field[:, HALF:]
    turned, turned_second = roll_half(first), roll_half(second)
    lane = lanes_of(first.shape)
    return jnp.concatenate(
        [jnp.where(lane < 64, halo, turned), jnp.where(lane < 64, turned, turned_second)], axis=1
    )


def before_rows(field, halo):
    first, second = field[:, :HALF], field[:, HALF:]
    turned, turned_second = roll_half(first), roll_half(second)
    lane = lanes_of(first.shape)
    return jnp.concatenate(
        [jnp.where(lane < 64, turned, turned_second), jnp.where(lane < 64, turned_second, halo)], axis=1
    )


def operate(centre, x_pair, y_pair, along, ahead_x, ahead_y):
    along_x, along_y, along_z = along
    plane = lanes_of(centre.shape) % NZ
    first, last = plane == 0, plane == NZ - 1
    ahead_z = jnp.where(last, pltpu.roll(along_z, NZ - 1, 1), pltpu.roll(along_z, PLANE - 1, 1))
    behind_z = jnp.where(first, 0.0, pltpu.roll(centre, 1, 1))
    before_z = jnp.where(last, 0.0, pltpu.roll(centre, PLANE - 1, 1))
    result_x = along_x * (centre - x_pair[0]) + ahead_x * (centre - x_pair[1])
    result_y = along_y * (centre - y_pair[0]) + ahead_y * (centre - y_pair[1])
    result_z = along_z * (centre - behind_z) + ahead_z * (centre - before_z)
    return result_x + result_y + result_z


def turned(ref, lead=()):
    rows = [ref[lead + (slice(None), y, slice(None))] for y in range(ROWS)]
    return jnp.concatenate(rows, axis=0).T


def y_neighbours(place, field, along_y, under, over, cond_over):
    under = jnp.concatenate([under, roll_half(under)], axis=0)
    over = jnp.concatenate([roll_half(over), over], axis=0)
    cond_over = jnp.concatenate([roll_half(cond_over), cond_over], axis=0)
    under = jnp.where(place[1] == 0, 0.0, under)
    over = jnp.where(place[1] == place[3] - 1, 0.0, over)
    pair = (behind_rows(field, under), before_rows(field, over))
    return pair, before_rows(along_y, cond_over)


def entry_kernel(
    start_hbm,
    cond_hbm,
    right_hbm,
    field_ref,
    along_ref,
    right_out,
    left_ref,
    right_ref,
    under_ref,
    over_ref,
    start_ref,
    cond_ref,
    rhs_ref,
    semaphores,
):
    copies = [pltpu.make_async_copy(start_hbm, start_ref, semaphores.at[0])]
    copies += [pltpu.make_async_copy(cond_hbm.at[i], cond_ref.at[i], semaphores.at[1 + i]) for i in range(3)]
    copies += [pltpu.make_async_copy(right_hbm, rhs_ref, semaphores.at[4])]
    for copy in copies:
        copy.start()
    copies[0].wait()
    field = turned(start_ref)
    field_ref[...] = field
    left_ref[0:1] = field[0:1]
    right_ref[0:1] = field[CELLS - 1 :]
    under_ref[:HALF] = low_row_packed(field)
    over_ref[...] = high_row_packed(field)
    for axis in range(3):
        copies[1 + axis].wait()
        along = turned(cond_ref, (axis,))
        if axis == 0:
            left_ref[1:2] = along[0:1]
        if axis == 1:
            under_ref[HALF:] = low_row_packed(along)
        along_ref[:, COLS * axis : COLS * (axis + 1), :] = along.reshape(GROUP, COLS, PLANE)
    copies[4].wait()
    right_out[...] = turned(rhs_ref)


def residual_kernel(place, rhs_ref, field_ref, chunk_ref, left_ref, next_ref, under_ref, over_ref, out_ref, residual_ref):
    field = field_ref[...]
    along = coefficients(chunk_ref)
    row = lax.broadcasted_iota(jnp.int32, (CELLS, PLANE), 0)
    behind_x = jnp.where(row == 0, left_ref[0:1], pltpu.roll(field, 1, 0))
    before_x = jnp.where(row == CELLS - 1, next_ref[0:1], pltpu.roll(field, CELLS - 1, 0))
    ahead_x = jnp.where(row == CELLS - 1, next_ref[1:2], pltpu.roll(along[0], CELLS - 1, 0))
    y_pair, ahead_y = y_neighbours(
        place, field, along[1], under_ref[...], over_ref[:HALF], over_ref[HALF:]
    )
    image = operate(field, (behind_x, before_x), y_pair, along, ahead_x, ahead_y)
    residual = rhs_ref[...] - image
    residual_ref[...] = residual
    out_ref[:, 0 : 3 * COLS, :] = chunk_ref[...]
    out_ref[:, 3 * COLS :, :] = residual.reshape(GROUP, COLS, PLANE)


def coefficients(chunk_ref):
    return [chunk_ref[:, COLS * axis : COLS * (axis + 1), :].reshape(CELLS, PLANE) for axis in range(3)]


def table_kernel(cosine_ref, sine_ref, turn_ref, high_ref, low_ref):
    turn = turn_ref[...]
    table = cosine_ref[...] * turn[:, 0:1] + sine_ref[...] * turn[:, 1:2]
    high_ref[...], low_ref[...] = split(table)


def spread_kernel(field_ref, high_ref, low_ref, out_ref):
    field = field_ref[:, 3 * COLS :, :].reshape(CELLS, PLANE)
    table = (high_ref[...], low_ref[...])
    out_ref[...] = products(table, split(field), ((1,), (0,))).reshape(GROUP, 2 * COLS, PLANE)


def solve_kernel(which, parts_ref, inverse_ref, high_ref, low_ref, dots_ref, out_ref, sums_ref, wave, solved, back, held, semaphores):
    copies = []
    for half in range(2):
        lanes = pl.ds(half * HALF, HALF)
        source = inverse_ref.at[:, :, lanes]
        copies.append(pltpu.make_async_copy(source, held.at[half], semaphores.at[half]))
        copies[half].start()
    table = (high_ref[...], low_ref[...])
    parts = parts_ref[...].reshape(2 * CELLS, PLANE).T
    wave[...] = products(split(parts), table, ((1,), (0,)))
    total = jnp.zeros((8, HALF), f32)
    for half in range(2):
        copies[half].wait()
        for pair in range(2):
            places = [(2 * pair + y, part * CELLS + half * HALF) for y in range(2) for part in range(2)]

            def step(group, sums):
                tiles = [
                    wave[pl.ds(pl.multiple_of(y * NZ + group * 8, 8), 8), lane : lane + HALF] for y, lane in places
                ]
                for z in range(8):
                    block = held[half, group * 8 + z]
                    sums = tuple(so_far + block * tile[z : z + 1] for so_far, tile in zip(sums, tiles))
                return sums

            sums = lax.fori_loop(0, NZ // 8, step, tuple(jnp.zeros((NZ, HALF), f32) for _ in places))
            for result, (y, lane) in zip(sums, places):
                solved[y * NZ : (y + 1) * NZ, lane : lane + HALF] = result
                product = result * wave[y * NZ : (y + 1) * NZ, lane : lane + HALF]
                total = total + jnp.sum(product.reshape(NZ // 8, 8, HALF), axis=0)
    row = lax.broadcasted_iota(jnp.int32, (8, HALF), 0)
    sums_ref[...] = dots_ref[...] + jnp.where(row == which, jnp.sum(total, axis=0, keepdims=True) / LENGTH, 0.0)
    parts = products(table, split(solved[...]), ((1,), (1,))).reshape(GROUP, 2 * COLS, PLANE)
    for half in range(2):
        out_ref[:, 16 * half : 16 * (half + 1), :] = parts[:, :, half * HALF : (half + 1) * HALF]
    if which == 0:
        back[...] = parts
        for side, (column, step) in enumerate(((COLS - 1, 1), (0, GROUP - 1))):
            for part in range(2):
                rows = pltpu.roll(back[:, part * COLS + column, :], step, 0)
                for half in range(2):
                    out_ref[:, 32 + 4 * half + 2 * side + part, :] = rows[:, half * HALF : (half + 1) * HALF]
    else:
        out_ref[:, 32:40, :] = jnp.broadcast_to(sums_ref[...][None], (GROUP, 8, HALF))


def gather_field(parts_ref, high_ref, low_ref):
    parts = jnp.concatenate(
        [parts_ref[:, 16 * half : 16 * (half + 1), :].reshape(2 * CELLS, HALF) for half in range(2)], axis=1
    )
    table = (high_ref[...], low_ref[...])
    return products(table, split(parts), ((0,), (0,))) * (1.0 / LENGTH)


def gather_kernel(
    parts_ref, high_ref, low_ref, edge_high_ref, edge_low_ref, field_ref, left_ref, next_ref, row_low_ref, row_high_ref
):
    field = gather_field(parts_ref, high_ref, low_ref)
    field_ref[...] = field
    row_low_ref[...] = low_row_packed(field)
    row_high_ref[...] = high_row_packed(field)
    beside = parts_ref[:, 32:40, :].reshape(CELLS, HALF)
    edges = products((edge_high_ref[...], edge_low_ref[...]), split(beside), ((0,), (0,))) * (1.0 / LENGTH)
    left_ref[...] = jnp.concatenate([edges[0:32], edges[64:96]], axis=1)
    next_ref[...] = jnp.concatenate([edges[32:64], edges[96:128]], axis=1)


def edge_rows(edge):
    return jnp.broadcast_to(edge[:, None, :], (GROUP, COLS, PLANE)).reshape(CELLS, PLANE)


def image_kernel(
    place,
    field_ref,
    chunk_ref,
    left_ref,
    next_ref,
    under_ref,
    over_ref,
    cond_next_ref,
    cond_over_ref,
    dots_ref,
    high_ref,
    low_ref,
    image_ref,
    parts_ref,
    sums_ref,
):
    field = field_ref[...]
    along = coefficients(chunk_ref)
    column = lax.broadcasted_iota(jnp.int32, (CELLS, PLANE), 0) % COLS
    cond_after = cond_next_ref[...]
    at_end = place[0] == place[2] - 1
    cond_after = jnp.where(at_end, pltpu.roll(cond_after, GROUP - 1, 0), cond_after)
    behind_x = jnp.where(column == 0, edge_rows(left_ref[...]), pltpu.roll(field, 1, 0))
    before_x = jnp.where(column == COLS - 1, edge_rows(next_ref[...]), pltpu.roll(field, CELLS - 1, 0))
    ahead_x = jnp.where(column == COLS - 1, edge_rows(cond_after), pltpu.roll(along[0], CELLS - 1, 0))
    y_pair, ahead_y = y_neighbours(place, field, along[1], under_ref[...], over_ref[...], cond_over_ref[...])
    image = operate(field, (behind_x, before_x), y_pair, along, ahead_x, ahead_y)
    image_ref[...] = image
    table = (high_ref[...], low_ref[...])
    parts_ref[...] = products(table, split(image), ((1,), (0,))).reshape(GROUP, 2 * COLS, PLANE)
    product = field * image
    total = jnp.sum((product[:, :HALF] + product[:, HALF:]), axis=0, keepdims=True)
    row = lax.broadcasted_iota(jnp.int32, (8, HALF), 0)
    sums_ref[...] = dots_ref[...] + jnp.where(row == 1, total, 0.0)


def edges_kernel(chunk_ref, edge_ref, row_ref):
    edge_ref[...] = chunk_ref[:, 0, :]
    row_ref[...] = low_row_packed(chunk_ref[:, COLS : 2 * COLS, :].reshape(CELLS, PLANE))


def pack_kernel(parts_ref, high_ref, low_ref, field_ref, image_ref, out_ref, sums_ref):
    out_ref[:, 0:COLS, :] = field_ref[...].reshape(GROUP, COLS, PLANE)
    out_ref[:, COLS : 2 * COLS, :] = image_ref[...].reshape(GROUP, COLS, PLANE)
    latest = gather_field(parts_ref, high_ref, low_ref)
    out_ref[:, 2 * COLS :, :] = latest.reshape(GROUP, COLS, PLANE)
    sums_ref[...] = jnp.sum(parts_ref[:, 32:40, :], axis=0)


def finish_kernel(packed_ref, start_ref, residual_ref, dots_ref, pressure_out, residual_out, direction_out):
    sums = jnp.sum(dots_ref[...], axis=1, keepdims=True)
    first, curvature, third = sums[0:1], sums[1:2], sums[2:3]
    step = first / curvature
    second = first - 2.0 * step * curvature + step * step * third
    ratio = second / first
    field = packed_ref[:, 0:COLS, :].reshape(CELLS, PLANE)
    image = packed_ref[:, COLS : 2 * COLS, :].reshape(CELLS, PLANE)
    latest = packed_ref[:, 2 * COLS :, :].reshape(CELLS, PLANE)
    change = (step * field).T
    residual = (residual_ref[...] - step * image).T
    direction = ((field - step * latest) + ratio * field).T
    for y in range(ROWS):
        rows = slice(y * NZ, (y + 1) * NZ)
        pressure_out[:, y, :] = start_ref[:, y, :] + change[rows]
        residual_out[:, y, :] = residual[rows]
        direction_out[:, y, :] = direction[rows]


def shape(*dims, dtype=f32):
    return jax.ShapeDtypeStruct(dims, dtype)


def call(kernel, outs, *args, smem=0, hbm=(), scratch=(), cost=0):
    specs = [pl.BlockSpec(memory_space=pltpu.SMEM if i < smem else pltpu.VMEM) for i in range(len(args))]
    args = list(args)
    for i in hbm:
        specs[i] = pl.BlockSpec(memory_space=pltpu.HBM)
        args[i] = pltpu.with_memory_space_constraint(args[i], pltpu.HBM)
    many = isinstance(outs, (tuple, list))
    out_spec = pl.BlockSpec(memory_space=pltpu.VMEM)
    return pl.pallas_call(
        kernel,
        out_shape=outs,
        in_specs=specs,
        out_specs=[out_spec] * len(outs) if many else out_spec,
        scratch_shapes=list(scratch),
        compiler_params=pltpu.CompilerParams(vmem_limit_bytes=16 * 1024 * 1024),
        cost_estimate=pl.CostEstimate(flops=cost, bytes_accessed=2**20, transcendentals=0),
    )(*args)


def shift(value, axis, step):
    count = lax.axis_size(axis)
    return lax.ppermute(value, axis, [(i, (i + step) % count) for i in range(count)])


def exchange(parts):
    return lax.all_to_all(parts, "gx", 0, 0, tiled=True)


def sum_over(value, axis):
    count = lax.axis_size(axis)
    distance = 1
    while distance < count:
        value = value + lax.ppermute(value, axis, [(i, i ^ distance) for i in range(count)])
        distance *= 2
    return value


def turns(columns, repeats):
    residues = jnp.asarray([reverse_bits(i) for i in range(GROUP)], jnp.int32)
    angle = (residues[:, None] * columns[None, :] % LENGTH).astype(f32) * (2.0 * math.pi / LENGTH)
    turn = jnp.stack([jnp.cos(angle), jnp.sin(angle)], axis=-1)
    return jnp.broadcast_to(turn[:, None], (GROUP, repeats) + turn.shape[1:]).reshape(-1, 2)


def shards(right_side, start_pressure, conductance, inverses):
    place = jnp.stack(
        [lax.axis_index("gx"), lax.axis_index("gy"), lax.axis_size("gx"), lax.axis_size("gy")]
    ).astype(jnp.int32)
    field_shape = shape(CELLS, PLANE)
    parts_shape = shape(GROUP, 2 * COLS, PLANE)
    wide_shape = shape(GROUP, 5 * COLS, HALF)
    edge_shape, row_shape, dots_shape = shape(GROUP, PLANE), shape(HALF, HALF), shape(8, HALF)

    cells_shape = shape(NZ, ROWS, CELLS)
    start, along, turned_right, to_left, to_right, to_under, to_over = call(
        entry_kernel,
        [
            field_shape,
            shape(GROUP, 3 * COLS, PLANE),
            field_shape,
            shape(8, PLANE),
            shape(8, PLANE),
            shape(2 * HALF, HALF),
            row_shape,
        ],
        start_pressure,
        conductance,
        right_side,
        hbm=(0, 1, 2),
        scratch=[
            pltpu.VMEM((NZ, ROWS, CELLS), f32),
            pltpu.VMEM((3, NZ, ROWS, CELLS), f32),
            pltpu.VMEM((NZ, ROWS, CELLS), f32),
            pltpu.SemaphoreType.DMA((5,)),
        ],
    )
    under = shift(to_over, "gy", 1)
    over = shift(to_under, "gy", -1)
    left = shift(to_right, "gx", 1)
    after = shift(to_left, "gx", -1)
    chunk, residual = call(
        residual_kernel,
        [shape(GROUP, 4 * COLS, PLANE), field_shape],
        place,
        turned_right,
        start,
        along,
        left,
        after,
        under,
        over,
        smem=1,
    )
    chunk = exchange(chunk)

    first = lax.axis_index("gx") * COLS
    columns = first + jnp.arange(COLS, dtype=jnp.int32)
    table = call(
        table_kernel,
        [shape(2 * CELLS, CELLS, dtype=bf16)] * 2,
        *[jnp.asarray(part) for part in column_tables()],
        turns(columns, 2),
    )
    beside = jnp.stack([first - 1, first - 1, first + COLS, first + COLS]).astype(jnp.int32) % LENGTH
    edge_table = call(
        table_kernel,
        [shape(CELLS, HALF, dtype=bf16)] * 2,
        *[jnp.asarray(part) for part in edge_tables()],
        turns(beside, 2),
    )
    waves = [jnp.asarray(part) for part in wave_table()]
    inverse = inverses.reshape(inverses.shape[1:])

    def solve(which, parts, dots):
        return call(
            functools.partial(solve_kernel, which),
            [wide_shape, dots_shape],
            parts,
            inverse,
            *waves,
            dots,
            hbm=(1,),
            scratch=[
                pltpu.VMEM((PLANE, 2 * CELLS), f32),
                pltpu.VMEM((PLANE, 2 * CELLS), f32),
                pltpu.VMEM((GROUP, 2 * COLS, PLANE), f32),
                pltpu.VMEM((2, NZ, NZ, HALF), f32),
                pltpu.SemaphoreType.DMA((2,)),
            ],
            cost=2 * 10**9,
        )

    parts = exchange(call(spread_kernel, parts_shape, chunk, *table))
    cond_edge, cond_row = call(edges_kernel, [edge_shape, row_shape], chunk)
    cond_after = shift(cond_edge, "gx", -1)
    cond_over = shift(cond_row, "gy", -1)
    parts, cond_after, cond_over = lax.optimization_barrier((parts, cond_after, cond_over))
    parts, dots = solve(0, parts, jnp.zeros((8, HALF), f32))
    field, left, after, row_low, row_high = call(
        gather_kernel,
        [field_shape, edge_shape, edge_shape, row_shape, row_shape],
        exchange(parts),
        *table,
        *edge_table,
    )
    under = shift(row_high, "gy", 1)
    over = shift(row_low, "gy", -1)
    image, parts, dots = call(
        image_kernel,
        [field_shape, parts_shape, dots_shape],
        place,
        field,
        chunk,
        left,
        after,
        under,
        over,
        cond_after,
        cond_over,
        dots,
        *table,
        smem=1,
    )
    parts, _ = solve(2, exchange(parts), dots)
    packed, dots = call(
        pack_kernel, [shape(GROUP, 3 * COLS, PLANE), dots_shape], exchange(parts), *table, field, image
    )
    dots = sum_over(dots, "gy")
    return tuple(call(finish_kernel, [cells_shape] * 3, exchange(packed), start_pressure, residual, dots))


def solution(mesh):
    placed = (
        P(None, "gy", "gx"),
        P(None, "gy", "gx"),
        P(None, None, "gy", "gx"),
        P("gx", None, None, None),
    )
    return jax.shard_map(
        shards,
        mesh=mesh,
        in_specs=placed,
        out_specs=(P(None, "gy", "gx"), P(None, "gy", "gx"), P(None, "gy", "gx")),
        check_vma=False,
    )
```

time: 177 us -> 151 us (0.85)
  blocking collectives: 52 us -> 31.8 us
  local copies, waits for them, and re-layouts: 10.5 us -> 1.38 us
  Pallas kernels: 16.6 us -> 22.2 us
  starting transfers between devices: 47.4 us -> 42.7 us
  waiting for transfers between devices: 48.9 us -> 51.5 us
    all_to_all x3 -> x2, blocking collectives: 52 us -> 31.8 us  [exchange(): return lax.all_to_all(parts, 'gx', 0, 0, tiled=True)]
    ppermute x8 -> x3, waiting for transfers between devices: 22.1 us -> 11.5 us  [sum_over(): lax.ppermute(value, axis, [(i, i ^ distance) for i in range(count)])]
    ppermute x8 -> x3, starting transfers between devices: 12.2 us -> 4.19 us  [sum_over(): lax.ppermute(value, axis, [(i, i ^ distance) for i in range(count)])]
    all_to_all x3 -> x4, waiting for transfers between devices: 23.8 us -> 30.9 us  [exchange(): return lax.all_to_all(parts, 'gx', 0, 0, tiled=True)]
    ppermute x10 -> x8, waiting for transfers between devices: 2.91 us -> 9.15 us  [shift(): lax.ppermute(value, axis, [(i, (i + step) % count) for i in range(count)])]
    pallas_call x10 -> x12, Pallas kernels: 16.6 us -> 22.2 us  [call(): pl.pallas_call(kernel, out_shape=outs, in_specs=specs, out_specs=[out_spe...]
    unnamed x27 -> x18, local copies, waits for them, and re-layouts: 6.28 us -> 1.08 us
    all_to_all x3 -> x4, starting transfers between devices: 20.4 us -> 24.2 us  [exchange(): return lax.all_to_all(parts, 'gx', 0, 0, tiled=True)]
  transfers between devices with their start and end apart: 21 -> 15, of which waited for: 13 -> 10; matrix products, arithmetic and copies ran while one was open for 2% -> 0% of each run, Pallas kernels for 0% -> 0%
where the time goes in v2:
time: 151 us
  waiting for transfers between devices  51.5 us (34%)
  starting transfers between devices  42.7 us (28%)
  blocking collectives  31.8 us (21%)
  Pallas kernels  22.2 us (15%)
    all_to_all x2, blocking collectives, exchange(): return lax.all_to_all(parts, 'gx', 0, 0, tiled=True)  31.8 us
    all_to_all x4, waiting for transfers between devices, exchange(): return lax.all_to_all(parts, 'gx', 0, 0, tiled=True)  30.9 us
    all_to_all x4, starting transfers between devices, exchange(): return lax.all_to_all(parts, 'gx', 0, 0, tiled=True)  24.2 us
    pallas_call x12, Pallas kernels, call(): pl.pallas_call(kernel, out_shape=outs, in_specs=specs, out_specs=[out_spe...  22.2 us
    ppermute x8, starting transfers between devices, shift(): lax.ppermute(value, axis, [(i, (i + step) % count) for i in range(count)])  14.3 us
    ppermute x3, waiting for transfers between devices, sum_over(): lax.ppermute(value, axis, [(i, i ^ distance) for i in range(count)])  11.5 us
    ppermute x8, waiting for transfers between devices, shift(): lax.ppermute(value, axis, [(i, (i + step) % count) for i in range(count)])  9.15 us
    ppermute x3, starting transfers between devices, sum_over(): lax.ppermute(value, axis, [(i, i ^ distance) for i in range(count)])  4.19 us
  transfers between devices with their start and end apart: 15, of which 10 were waited for; matrix products, arithmetic and copies ran while one was open for 0% of the time, Pallas kernels for 0%

profile of v2, /device:TPU:2, one launch (start us, length us, event | category | flops | bytes accessed | tf_op | source)
XLA Modules:
  0.0 150.8 jit_solution(8054225004206997341)
XLA Ops:
  0.7 2.0 %shard_map.139 = (f32[256,256]{1,0:T(8,128)S(1)}, f32[32,24,256]{2,1,0:T(8,128)S(1)}, f32[256,256]{1,0:T(8,128)S(1)}, f32[8,256]{1,0:T(8,128)S(1)}, f32[8,256]{1...) custom-call(f32[64,4,256]{2,1,0:T(4,128)} %start_ref.1, f32[3,64,4,256]{3,2,1,0:T(4,128)} %cond_hbm.1, ...), custom_call_target="tpu_custom_call" | custom-call | bytes 1048576 | tf_op jit(solution)/shard_map/pallas_call | solution.py:375
  2.6 5.9 %collective-permute-start.3 = (f32[256,128]{1,0:T(8,128)S(1)}, f32[256,128]{1,0:T(8,128)S(1)}, u32[]{:S(2)}, u32[]{:S(2)}) collective-permute-start(f32[256,128]{1,0:T(8,128)S(1)} %get-tuple-element.40), channel_id=1, source_target_pairs={{0,7},{1,0},{2,1},{3,2},{4,3},{5,4},{6,5},{7,6},{8,15},{9,8},{10,9... | collective-permute-start | bytes 393224 | tf_op jit(solution)/shard_map/ppermute | solution.py:388
  8.6 1.7 %collective-permute-start.1 = (f32[8,256]{1,0:T(8,128)S(1)}, f32[8,256]{1,0:T(8,128)S(1)}, u32[]{:S(2)}, u32[]{:S(2)}) collective-permute-start(f32[8,256]{1,0:T(8,128)S(1)} %get-tuple-element.38), channel_id=1, source_target_pairs={{0,248},{8,0},{16,8},{24,16},{32,24},{40,32},{48,40},{56,48},{64,5... | collective-permute-start | bytes 24584 | tf_op jit(solution)/shard_map/ppermute | solution.py:388
  11.7 2.4 %collective-permute-done.2.under_ref = f32[128,128]{1,0:T(8,128)S(1)} collective-permute-done((f32[128,128]{1,0:T(8,128)S(1)}, f32[128,128]{1,0:T(8,128)S(1)}, u32[]{:S(2)}, u32[]{:S(2)}) %collective-permute-start.2) | collective-permute-done | bytes 65568 | tf_op jit(solution)/shard_map/ppermute | solution.py:388
  14.0 2.2 %shard_map.140 = (f32[32,32,256]{2,1,0:T(8,128)}, f32[256,256]{1,0:T(8,128)S(1)}) custom-call(s32[4]{0:T(128)S(1)} %pad_add_fusion.place, f32[256,256]{1,0:T(8,128)S(1)} %get-tuple-element.34.rhs_ref, f32[256,256]{1,0:T(8,128)S(1)} %get-tuple-element.35.field_ref, f32[32,24,256]{2,1,0:T(8,128)S(1)} %get-tuple-element.36.chunk_ref, ...), custom_call_target="tpu_custom_call" | custom-call | bytes 1048576 | tf_op jit(solution)/shard_map/pallas_call | solution.py:375
  16.2 8.1 %all-to-all-start = ((f32[32,32,256]{2,1,0:T(8,128)}), f32[32,32,256]{2,1,0:T(8,128)S(1)}, u32[]{:S(2)}, u32[]{:S(2)}) async-start(f32[32,32,256]{2,1,0:T(8,128)} %get-tuple-element.41), calls=%async_computation | async-start | bytes 2097152 | tf_op jit(solution)/shard_map/all_to_all | solution.py:392
  25.0 15.5 %all-to-all-done.field_ref.chunk_ref = f32[32,32,256]{2,1,0:T(8,128)S(1)} async-done(((f32[32,32,256]{2,1,0:T(8,128)}), f32[32,32,256]{2,1,0:T(8,128)S(1)}, u32[]{:S(2)}, u32[]{:S(2)}) %all-to-all-start) | async-done | bytes 1048608 | tf_op jit(solution)/shard_map/all_to_all | solution.py:392
  41.6 5.0 %all-to-all-start.1 = ((f32[32,16,256]{2,1,0:T(8,128)}), f32[32,16,256]{2,1,0:T(8,128)S(1)}, u32[]{:S(2)}, u32[]{:S(2)}) async-start(f32[32,16,256]{2,1,0:T(8,128)} %shard_map.142), calls=%async_computation.1 | async-start | bytes 1048576 | tf_op jit(solution)/shard_map/all_to_all | solution.py:392
  46.7 3.3 %collective-permute-start.5 = (f32[128,128]{1,0:T(8,128)S(1)}, f32[128,128]{1,0:T(8,128)S(1)}, u32[]{:S(2)}, u32[]{:S(2)}) collective-permute-start(f32[128,128]{1,0:T(8,128)S(1)} %get-tuple-element.45), channel_id=1, source_target_pairs={{0,7},{1,0},{2,1},{3,2},{4,3},{5,4},{6,5},{7,6},{8,15},{9,8},{10,9... | collective-permute-start | bytes 196616 | tf_op jit(solution)/shard_map/ppermute | solution.py:388
  50.1 3.2 %collective-permute-done.4.cond_next_ref = f32[32,256]{1,0:T(8,128)S(1)} collective-permute-done((f32[32,256]{1,0:T(8,128)S(1)}, f32[32,256]{1,0:T(8,128)S(1)}, u32[]{:S(2)}, u32[]{:S(2)}) %collective-permute-start.4) | collective-permute-done | bytes 32800 | tf_op jit(solution)/shard_map/ppermute | solution.py:388
  53.3 4.0 %all-to-all-done.1.parts_ref = f32[32,16,256]{2,1,0:T(8,128)S(1)} async-done(((f32[32,16,256]{2,1,0:T(8,128)}), f32[32,16,256]{2,1,0:T(8,128)S(1)}, u32[]{:S(2)}, u32[]{:S(2)}) %all-to-all-start.1) | async-done | bytes 524320 | tf_op jit(solution)/shard_map/all_to_all | solution.py:392
  58.3 6.1 %shard_map.144 = (f32[32,40,128]{2,1,0:T(8,128)}, f32[8,128]{1,0:T(8,128)S(1)}) custom-call(f32[32,16,256]{2,1,0:T(8,128)S(1)} %all-to-all-done.1.parts_ref, f32[64,64,256]{2,1,0:T(8,128)} %bitcast.9, bf16[512,512]{1,0:T(8,128)(2,1)S(1)} %copy-done.5, bf16[512,512]{1,0:T(8,128)(2,1)S(1)} %copy-done.6, f32[8,128]{1,0:T(8,128)S(1)} %broadcast_in_dim.7.dots_ref), custom_call_target="tpu_custom_call" | custom-call | flops 2000000000 | bytes 1048576 | tf_op jit(solution)/shard_map/pallas_call | solution.py:375
  64.4 5.9 %all-to-all-start.2 = ((f32[32,40,128]{2,1,0:T(8,128)}), f32[32,40,128]{2,1,0:T(8,128)S(1)}, u32[]{:S(2)}, u32[]{:S(2)}) async-start(f32[32,40,128]{2,1,0:T(8,128)} %get-tuple-element.47), calls=%async_computation.2 | async-start | bytes 1310720 | tf_op jit(solution)/shard_map/all_to_all | solution.py:392
  70.9 11.4 %all-to-all-done.2.parts_ref = f32[32,40,128]{2,1,0:T(8,128)S(1)} async-done(((f32[32,40,128]{2,1,0:T(8,128)}), f32[32,40,128]{2,1,0:T(8,128)S(1)}, u32[]{:S(2)}, u32[]{:S(2)}) %all-to-all-start.2) | async-done | bytes 655392 | tf_op jit(solution)/shard_map/all_to_all | solution.py:392
  82.9 3.2 %collective-permute-start.7 = (f32[128,128]{1,0:T(8,128)S(1)}, f32[128,128]{1,0:T(8,128)S(1)}, u32[]{:S(2)}, u32[]{:S(2)}) collective-permute-start(f32[128,128]{1,0:T(8,128)S(1)} %get-tuple-element.54), channel_id=1, source_target_pairs={{0,7},{1,0},{2,1},{3,2},{4,3},{5,4},{6,5},{7,6},{8,15},{9,8},{10,9... | collective-permute-start | bytes 196616 | tf_op jit(solution)/shard_map/ppermute | solution.py:388
  86.1 2.3 %collective-permute-done.6.under_ref = f32[128,128]{1,0:T(8,128)S(1)} collective-permute-done((f32[128,128]{1,0:T(8,128)S(1)}, f32[128,128]{1,0:T(8,128)S(1)}, u32[]{:S(2)}, u32[]{:S(2)}) %collective-permute-start.6) | collective-permute-done | bytes 65568 | tf_op jit(solution)/shard_map/ppermute | solution.py:388
  89.9 15.2 %all_to_all.30.parts_ref = f32[32,16,256]{2,1,0:T(8,128)S(1)} all-to-all(f32[32,16,256]{2,1,0:T(8,128)S(1)} %get-tuple-element.58), channel_id=1, replica_groups=mesh['gx'=32,'gy'=8] {'gx'}, dimensions={0} | all-to-all | bytes 1048576 | tf_op jit(solution)/shard_map/all_to_all | solution.py:392
  105.0 5.7 %shard_map.148 = (f32[32,40,128]{2,1,0:T(8,128)S(1)}, f32[8,128]{1,0:T(8,128)}) custom-call(f32[32,16,256]{2,1,0:T(8,128)S(1)} %all_to_all.30.parts_ref, f32[64,64,256]{2,1,0:T(8,128)} %bitcast.10, bf16[512,512]{1,0:T(8,128)(2,1)S(1)} %copy-done.5, bf16[512,512]{1,0:T(8,128)(2,1)S(1)} %copy-done.7, f32[8,128]{1,0:T(8,128)S(1)} %get-tuple-element.59.dots_ref), custom_call_target="tpu_custom_call" | custom-call | flops 2000000000 | bytes 1048576 | tf_op jit(solution)/shard_map/pallas_call | solution.py:375
  110.7 16.6 %all_to_all.31.parts_ref = f32[32,40,128]{2,1,0:T(8,128)S(1)} all-to-all(f32[32,40,128]{2,1,0:T(8,128)S(1)} %get-tuple-element.60), channel_id=1, replica_groups=mesh['gx'=32,'gy'=8] {'gx'}, dimensions={0} | all-to-all | bytes 1310720 | tf_op jit(solution)/shard_map/all_to_all | solution.py:392
  128.7 5.1 %all-to-all-start.5 = ((f32[32,24,256]{2,1,0:T(8,128)}), f32[32,24,256]{2,1,0:T(8,128)S(1)}, u32[]{:S(2)}, u32[]{:S(2)}) async-start(f32[32,24,256]{2,1,0:T(8,128)} %get-tuple-element.62), calls=%async_computation.5 | async-start | bytes 1572864 | tf_op jit(solution)/shard_map/all_to_all | solution.py:392
  133.9 3.6 %collective-permute-done.8 = f32[8,128]{1,0:T(8,128)S(1)} collective-permute-done((f32[8,128]{1,0:T(8,128)S(1)}, f32[8,128]{1,0:T(8,128)S(1)}, u32[]{:S(2)}, u32[]{:S(2)}) %collective-permute-start.8) | collective-permute-done | bytes 4128 | tf_op jit(solution)/shard_map/ppermute | solution.py:399
  139.0 3.0 %collective-permute-done.9 = f32[8,128]{1,0:T(8,128)S(1)} collective-permute-done((f32[8,128]{1,0:T(8,128)S(1)}, f32[8,128]{1,0:T(8,128)S(1)}, u32[]{:S(2)}, u32[]{:S(2)}) %collective-permute-start.9) | collective-permute-done | bytes 4128 | tf_op jit(solution)/shard_map/ppermute | solution.py:399
  142.0 2.6 %collective-permute-start.10 = (f32[8,128]{1,0:T(8,128)S(1)}, f32[8,128]{1,0:T(8,128)S(1)}, u32[]{:S(2)}, u32[]{:S(2)}) collective-permute-start(f32[8,128]{1,0:T(8,128)S(1)} %add.75), channel_id=1, source_target_pairs={{0,4},{1,5},{2,6},{3,7},{4,0},{5,1},{6,2},{7,3},{8,12},{9,13},{10,... | collective-permute-start | bytes 12296 | tf_op jit(solution)/shard_map/ppermute | solution.py:399
  144.6 5.0 %collective-permute-done.10 = f32[8,128]{1,0:T(8,128)S(1)} collective-permute-done((f32[8,128]{1,0:T(8,128)S(1)}, f32[8,128]{1,0:T(8,128)S(1)}, u32[]{:S(2)}, u32[]{:S(2)}) %collective-permute-start.10) | collective-permute-done | bytes 4128 | tf_op jit(solution)/shard_map/ppermute | solution.py:399
  (53 shorter events, 11.0 us)
Async XLA Ops:
  0.6 23.8 %copy-start.8 = (s32[32]{0:T(128)S(1)}, s32[32]{0:T(128)}, u32[]{:S(2)}) copy-start(s32[32]{0:T(128)} %constant.70.clone) | copy-start | bytes 388
  0.6 24.1 %copy-start.1 = (f32[512,256]{1,0:T(8,128)S(1)}, f32[512,256]{1,0:T(8,128)}, u32[]{:S(2)}) copy-start(f32[512,256]{1,0:T(8,128)} %constant.68.clone.cosine_ref) | copy-start | bytes 1572868
  0.7 24.1 %copy-start.2 = (f32[512,256]{1,0:T(8,128)S(1)}, f32[512,256]{1,0:T(8,128)}, u32[]{:S(2)}) copy-start(f32[512,256]{1,0:T(8,128)} %constant.69.clone.sine_ref) | copy-start | bytes 1572868
  2.6 11.4 %collective-permute-start.3 = (f32[256,128]{1,0:T(8,128)S(1)}, f32[256,128]{1,0:T(8,128)S(1)}, u32[]{:S(2)}, u32[]{:S(2)}) collective-permute-start(f32[256,128]{1,0:T(8,128)S(1)} %get-tuple-element.40), channel_id=1, source_target_pairs={{0,7},{1,0},{2,1},{3,2},{4,3},{5,4},{6,5},{7,6},{8,15},{9,8},{10,9... | collective-permute-start | bytes 393224 | tf_op jit(solution)/shard_map/ppermute | solution.py:388
  8.6 5.5 %collective-permute-start.2 = (f32[128,128]{1,0:T(8,128)S(1)}, f32[128,128]{1,0:T(8,128)S(1)}, u32[]{:S(2)}, u32[]{:S(2)}) collective-permute-start(f32[128,128]{1,0:T(8,128)S(1)} %get-tuple-element.39), channel_id=1, source_target_pairs={{0,1},{1,2},{2,3},{3,4},{4,5},{5,6},{6,7},{7,0},{8,9},{9,10},{10,1... | collective-permute-start | bytes 196616 | tf_op jit(solution)/shard_map/ppermute | solution.py:388
  8.6 3.1 %collective-permute-start = (f32[8,256]{1,0:T(8,128)S(1)}, f32[8,256]{1,0:T(8,128)S(1)}, u32[]{:S(2)}, u32[]{:S(2)}) collective-permute-start(f32[8,256]{1,0:T(8,128)S(1)} %get-tuple-element.37), channel_id=1, source_target_pairs={{0,8},{8,16},{16,24},{24,32},{32,40},{40,48},{48,56},{56,64},{64,7... | collective-permute-start | bytes 24584 | tf_op jit(solution)/shard_map/ppermute | solution.py:388
  8.6 3.1 %collective-permute-start.1 = (f32[8,256]{1,0:T(8,128)S(1)}, f32[8,256]{1,0:T(8,128)S(1)}, u32[]{:S(2)}, u32[]{:S(2)}) collective-permute-start(f32[8,256]{1,0:T(8,128)S(1)} %get-tuple-element.38), channel_id=1, source_target_pairs={{0,248},{8,0},{16,8},{24,16},{32,24},{40,32},{48,40},{56,48},{64,5... | collective-permute-start | bytes 24584 | tf_op jit(solution)/shard_map/ppermute | solution.py:388
  16.2 41.0 %copy-start.5 = (bf16[512,512]{1,0:T(8,128)(2,1)S(1)}, bf16[512,512]{1,0:T(8,128)(2,1)}, u32[]{:S(2)}) copy-start(bf16[512,512]{1,0:T(8,128)(2,1)} %constant.73.clone.high_ref) | copy-start | bytes 1572868
  16.2 24.2 %all-to-all-start = ((f32[32,32,256]{2,1,0:T(8,128)}), f32[32,32,256]{2,1,0:T(8,128)S(1)}, u32[]{:S(2)}, u32[]{:S(2)}) async-start(f32[32,32,256]{2,1,0:T(8,128)} %get-tuple-element.41), calls=%async_computation | async-start | bytes 2097152 | tf_op jit(solution)/shard_map/all_to_all | solution.py:392
  41.6 15.6 %all-to-all-start.1 = ((f32[32,16,256]{2,1,0:T(8,128)}), f32[32,16,256]{2,1,0:T(8,128)S(1)}, u32[]{:S(2)}, u32[]{:S(2)}) async-start(f32[32,16,256]{2,1,0:T(8,128)} %shard_map.142), calls=%async_computation.1 | async-start | bytes 1048576 | tf_op jit(solution)/shard_map/all_to_all | solution.py:392
  46.7 6.5 %collective-permute-start.5 = (f32[128,128]{1,0:T(8,128)S(1)}, f32[128,128]{1,0:T(8,128)S(1)}, u32[]{:S(2)}, u32[]{:S(2)}) collective-permute-start(f32[128,128]{1,0:T(8,128)S(1)} %get-tuple-element.45), channel_id=1, source_target_pairs={{0,7},{1,0},{2,1},{3,2},{4,3},{5,4},{6,5},{7,6},{8,15},{9,8},{10,9... | collective-permute-start | bytes 196616 | tf_op jit(solution)/shard_map/ppermute | solution.py:388
  50.1 3.2 %collective-permute-start.4 = (f32[32,256]{1,0:T(8,128)S(1)}, f32[32,256]{1,0:T(8,128)S(1)}, u32[]{:S(2)}, u32[]{:S(2)}) collective-permute-start(f32[32,256]{1,0:T(8,128)S(1)} %get-tuple-element.44), channel_id=1, source_target_pairs={{0,248},{8,0},{16,8},{24,16},{32,24},{40,32},{48,40},{56,48},{64,5... | collective-permute-start | bytes 98312 | tf_op jit(solution)/shard_map/ppermute | solution.py:388
  57.3 1.0 copy-start.6
  58.3 12.4 %copy-start.3 = (f32[256,128]{1,0:T(8,128)S(1)}, f32[256,128]{1,0:T(8,128)}, u32[]{:S(2)}) copy-start(f32[256,128]{1,0:T(8,128)} %constant.71.clone.cosine_ref) | copy-start | bytes 393220
  58.3 12.5 %copy-start.4 = (f32[256,128]{1,0:T(8,128)S(1)}, f32[256,128]{1,0:T(8,128)}, u32[]{:S(2)}) copy-start(f32[256,128]{1,0:T(8,128)} %constant.72.clone.sine_ref) | copy-start | bytes 393220
  64.4 17.8 %all-to-all-start.2 = ((f32[32,40,128]{2,1,0:T(8,128)}), f32[32,40,128]{2,1,0:T(8,128)S(1)}, u32[]{:S(2)}, u32[]{:S(2)}) async-start(f32[32,40,128]{2,1,0:T(8,128)} %get-tuple-element.47), calls=%async_computation.2 | async-start | bytes 1310720 | tf_op jit(solution)/shard_map/all_to_all | solution.py:392
  82.3 22.7 %copy-start.7 = (bf16[512,512]{1,0:T(8,128)(2,1)S(1)}, bf16[512,512]{1,0:T(8,128)(2,1)}, u32[]{:S(2)}) copy-start(bf16[512,512]{1,0:T(8,128)(2,1)} %constant.74.clone.low_ref) | copy-start | bytes 1572868
  82.8 5.6 %collective-permute-start.6 = (f32[128,128]{1,0:T(8,128)S(1)}, f32[128,128]{1,0:T(8,128)S(1)}, u32[]{:S(2)}, u32[]{:S(2)}) collective-permute-start(f32[128,128]{1,0:T(8,128)S(1)} %get-tuple-element.53), channel_id=1, source_target_pairs={{0,1},{1,2},{2,3},{3,4},{4,5},{5,6},{6,7},{7,0},{8,9},{9,10},{10,1... | collective-permute-start | bytes 196616 | tf_op jit(solution)/shard_map/ppermute | solution.py:388
  82.9 5.5 %collective-permute-start.7 = (f32[128,128]{1,0:T(8,128)S(1)}, f32[128,128]{1,0:T(8,128)S(1)}, u32[]{:S(2)}, u32[]{:S(2)}) collective-permute-start(f32[128,128]{1,0:T(8,128)S(1)} %get-tuple-element.54), channel_id=1, source_target_pairs={{0,7},{1,0},{2,1},{3,2},{4,3},{5,4},{6,5},{7,6},{8,15},{9,8},{10,9... | collective-permute-start | bytes 196616 | tf_op jit(solution)/shard_map/ppermute | solution.py:388
  105.0 44.5 %copy-start = (f32[64,4,256]{2,1,0:T(4,128)S(1)}, f32[64,4,256]{2,1,0:T(4,128)}, u32[]{:S(2)}) copy-start(f32[64,4,256]{2,1,0:T(4,128)} %start_ref.1) | copy-start | bytes 786436
  128.7 20.9 %all-to-all-start.5 = ((f32[32,24,256]{2,1,0:T(8,128)}), f32[32,24,256]{2,1,0:T(8,128)S(1)}, u32[]{:S(2)}, u32[]{:S(2)}) async-start(f32[32,24,256]{2,1,0:T(8,128)} %get-tuple-element.62), calls=%async_computation.5 | async-start | bytes 1572864 | tf_op jit(solution)/shard_map/all_to_all | solution.py:392
  133.8 3.7 %collective-permute-start.8 = (f32[8,128]{1,0:T(8,128)S(1)}, f32[8,128]{1,0:T(8,128)S(1)}, u32[]{:S(2)}, u32[]{:S(2)}) collective-permute-start(f32[8,128]{1,0:T(8,128)S(1)} %get-tuple-element.64), channel_id=1, source_target_pairs={{0,1},{1,0},{2,3},{3,2},{4,5},{5,4},{6,7},{7,6},{8,9},{9,8},{10,11... | collective-permute-start | bytes 12296 | tf_op jit(solution)/shard_map/ppermute | solution.py:399
  137.5 4.5 %collective-permute-start.9 = (f32[8,128]{1,0:T(8,128)S(1)}, f32[8,128]{1,0:T(8,128)S(1)}, u32[]{:S(2)}, u32[]{:S(2)}) collective-permute-start(f32[8,128]{1,0:T(8,128)S(1)} %add.74), channel_id=1, source_target_pairs={{0,2},{1,3},{2,0},{3,1},{4,6},{5,7},{6,4},{7,5},{8,10},{9,11},{10,... | collective-permute-start | bytes 12296 | tf_op jit(solution)/shard_map/ppermute | solution.py:399
  142.0 7.5 %collective-permute-start.10 = (f32[8,128]{1,0:T(8,128)S(1)}, f32[8,128]{1,0:T(8,128)S(1)}, u32[]{:S(2)}, u32[]{:S(2)}) collective-permute-start(f32[8,128]{1,0:T(8,128)S(1)} %add.75), channel_id=1, source_target_pairs={{0,4},{1,5},{2,6},{3,7},{4,0},{5,1},{6,2},{7,3},{8,12},{9,13},{10,... | collective-permute-start | bytes 12296 | tf_op jit(solution)/shard_map/ppermute | solution.py:399

commit v3 on v2

--- a/solution.py
+++ b/solution.py
@@ -1,5 +1,4 @@
 import functools
-import math
 
 import jax
 import jax.numpy as jnp
@@ -26,7 +25,7 @@
     return int(f"{number:05b}"[::-1], 2)
 
 
-def column_tables():
+def column_table():
     residue = np.array([reverse_bits(i) for i in range(GROUP)])
     angle = 2.0 * np.pi * np.outer(residue, np.arange(GROUP)) / GROUP
     same = np.eye(COLS)
@@ -36,11 +35,10 @@
         full = pair[:, :, None, :, None] * same[None, None, :, None, :]
         return full.reshape(GROUP * 2 * COLS, CELLS).astype(np.float32)
 
-    cosine, sine = np.cos(angle), np.sin(angle)
-    return table(cosine, -sine), table(-sine, -cosine)
-
-
-def edge_tables():
+    return table(np.cos(angle), -np.sin(angle))
+
+
+def edge_table():
     residue = np.array([reverse_bits(i) for i in range(GROUP)])
     angle = 2.0 * np.pi * np.outer(residue, np.arange(GROUP)) / GROUP
     same = np.eye(4).reshape(2, 2, 2, 2)
@@ -50,8 +48,24 @@
         full = pair[:, None, None, :, None, None, :] * same[None, :, :, None, :, :, None]
         return full.reshape(GROUP * 8, 4 * GROUP).astype(np.float32)
 
-    cosine, sine = np.cos(angle), np.sin(angle)
-    return table(cosine, -sine), table(-sine, -cosine)
+    return table(np.cos(angle), -np.sin(angle))
+
+
+def turn_table():
+    residue = np.array([reverse_bits(i) for i in range(GROUP)])
+    first = COLS * np.arange(GROUP)[:, None]
+    own = np.tile(np.arange(COLS), 2)[None, :] + first
+    beside = np.tile(np.array([-1, -1, COLS, COLS]), 2)[None, :] + first
+
+    def angles(columns):
+        turns = residue[None, :, None] * columns[:, None, :] % LENGTH
+        return (2.0 * np.pi / LENGTH) * turns.reshape(GROUP, -1)
+
+    full = np.zeros((GROUP, 8, 2 * CELLS), np.float32)
+    for i, angle in enumerate((angles(own), angles(beside))):
+        full[:, 2 * i, : angle.shape[1]] = np.cos(angle)
+        full[:, 2 * i + 1, : angle.shape[1]] = np.sin(angle)
+    return full
 
 
 def wave_table():
@@ -150,22 +164,18 @@
 def entry_kernel(
     start_hbm,
     cond_hbm,
-    right_hbm,
     field_ref,
     along_ref,
-    right_out,
     left_ref,
     right_ref,
     under_ref,
     over_ref,
     start_ref,
     cond_ref,
-    rhs_ref,
     semaphores,
 ):
     copies = [pltpu.make_async_copy(start_hbm, start_ref, semaphores.at[0])]
-    copies += [pltpu.make_async_copy(cond_hbm.at[i], cond_ref.at[i], semaphores.at[1 + i]) for i in range(3)]
-    copies += [pltpu.make_async_copy(right_hbm, rhs_ref, semaphores.at[4])]
+    copies += [pltpu.make_async_copy(cond_hbm.at[i], cond_ref.at[i], semaphores.at[1 + i]) for i in range(2)]
     for copy in copies:
         copy.start()
     copies[0].wait()
@@ -175,21 +185,48 @@
     right_ref[0:1] = field[CELLS - 1 :]
     under_ref[:HALF] = low_row_packed(field)
     over_ref[...] = high_row_packed(field)
-    for axis in range(3):
+    for axis in range(2):
         copies[1 + axis].wait()
         along = turned(cond_ref, (axis,))
         if axis == 0:
             left_ref[1:2] = along[0:1]
-        if axis == 1:
+        else:
             under_ref[HALF:] = low_row_packed(along)
         along_ref[:, COLS * axis : COLS * (axis + 1), :] = along.reshape(GROUP, COLS, PLANE)
+
+
+def side_kernel(place, order_ref, cond_hbm, right_hbm, turns_hbm, column_hbm, edge_hbm, *refs):
+    along_out, right_out, high_ref, low_ref, edge_high_ref, edge_low_ref = refs[:6]
+    cond_ref, rhs_ref, turns_ref, column_ref, edge_ref, semaphores = refs[6:]
+    sources = (cond_hbm.at[2], right_hbm, turns_hbm.at[place[0]], column_hbm, edge_hbm)
+    targets = (cond_ref, rhs_ref, turns_ref, column_ref, edge_ref)
+    copies = [pltpu.make_async_copy(*pair, semaphores.at[i]) for i, pair in enumerate(zip(sources, targets))]
+    for copy in copies:
+        copy.start()
+    copies[0].wait()
+    along_out[...] = turned(cond_ref).reshape(GROUP, COLS, PLANE)
+    copies[1].wait()
+    right_out[...] = turned(rhs_ref)
+    copies[2].wait()
+    turns = turns_ref[...].T
+    copies[3].wait()
+    table = column_ref[...]
+    blocks = table.reshape(GROUP, 2 * COLS, CELLS)
+    other = jnp.concatenate([blocks[:, COLS:], -blocks[:, :COLS]], axis=1).reshape(2 * CELLS, CELLS)
+    high_ref[...], low_ref[...] = split(table * turns[:, 0:1] + other * turns[:, 1:2])
     copies[4].wait()
-    right_out[...] = turned(rhs_ref)
-
-
-def residual_kernel(place, rhs_ref, field_ref, chunk_ref, left_ref, next_ref, under_ref, over_ref, out_ref, residual_ref):
+    table = edge_ref[...]
+    part = lax.broadcasted_iota(jnp.int32, (CELLS, HALF), 0) % 2
+    other = jnp.where(part == 0, pltpu.roll(table, CELLS - 1, 0), -pltpu.roll(table, 1, 0))
+    edge_high_ref[...], edge_low_ref[...] = split(table * turns[:CELLS, 2:3] + other * turns[:CELLS, 3:4])
+
+
+def residual_kernel(
+    place, rhs_ref, field_ref, along_ref, along_z_ref, left_ref, next_ref, under_ref, over_ref, out_ref, residual_ref
+):
     field = field_ref[...]
-    along = coefficients(chunk_ref)
+    along = [along_ref[:, COLS * axis : COLS * (axis + 1), :].reshape(CELLS, PLANE) for axis in range(2)]
+    along += [along_z_ref[...].reshape(CELLS, PLANE)]
     row = lax.broadcasted_iota(jnp.int32, (CELLS, PLANE), 0)
     behind_x = jnp.where(row == 0, left_ref[0:1], pltpu.roll(field, 1, 0))
     before_x = jnp.where(row == CELLS - 1, next_ref[0:1], pltpu.roll(field, CELLS - 1, 0))
@@ -200,18 +237,13 @@
     image = operate(field, (behind_x, before_x), y_pair, along, ahead_x, ahead_y)
     residual = rhs_ref[...] - image
     residual_ref[...] = residual
-    out_ref[:, 0 : 3 * COLS, :] = chunk_ref[...]
+    out_ref[:, 0 : 2 * COLS, :] = along_ref[...]
+    out_ref[:, 2 * COLS : 3 * COLS, :] = along_z_ref[...]
     out_ref[:, 3 * COLS :, :] = residual.reshape(GROUP, COLS, PLANE)
 
 
 def coefficients(chunk_ref):
     return [chunk_ref[:, COLS * axis : COLS * (axis + 1), :].reshape(CELLS, PLANE) for axis in range(3)]
-
-
-def table_kernel(cosine_ref, sine_ref, turn_ref, high_ref, low_ref):
-    turn = turn_ref[...]
-    table = cosine_ref[...] * turn[:, 0:1] + sine_ref[...] * turn[:, 1:2]
-    high_ref[...], low_ref[...] = split(table)
 
 
 def spread_kernel(field_ref, high_ref, low_ref, out_ref):
@@ -223,16 +255,16 @@
 def solve_kernel(which, parts_ref, inverse_ref, high_ref, low_ref, dots_ref, out_ref, sums_ref, wave, solved, back, held, semaphores):
     copies = []
     for half in range(2):
-        lanes = pl.ds(half * HALF, HALF)
-        source = inverse_ref.at[:, :, lanes]
-        copies.append(pltpu.make_async_copy(source, held.at[half], semaphores.at[half]))
-        copies[half].start()
+        for i in range(2):
+            planes, lanes = pl.ds(i * NZ // 2, NZ // 2), pl.ds(half * HALF, HALF)
+            target = held.at[half, planes]
+            copies.append(pltpu.make_async_copy(inverse_ref.at[planes, :, lanes], target, semaphores.at[2 * half + i]))
+            copies[-1].start()
     table = (high_ref[...], low_ref[...])
     parts = parts_ref[...].reshape(2 * CELLS, PLANE).T
     wave[...] = products(split(parts), table, ((1,), (0,)))
     total = jnp.zeros((8, HALF), f32)
     for half in range(2):
-        copies[half].wait()
         for pair in range(2):
             places = [(2 * pair + y, part * CELLS + half * HALF) for y in range(2) for part in range(2)]
 
@@ -245,7 +277,11 @@
                     sums = tuple(so_far + block * tile[z : z + 1] for so_far, tile in zip(sums, tiles))
                 return sums
 
-            sums = lax.fori_loop(0, NZ // 8, step, tuple(jnp.zeros((NZ, HALF), f32) for _ in places))
+            sums = tuple(jnp.zeros((NZ, HALF), f32) for _ in places)
+            for i in range(2):
+                if pair == 0:
+                    copies[2 * half + i].wait()
+                sums = lax.fori_loop(i * NZ // 16, (i + 1) * NZ // 16, step, sums)
             for result, (y, lane) in zip(sums, places):
                 solved[y * NZ : (y + 1) * NZ, lane : lane + HALF] = result
                 product = result * wave[y * NZ : (y + 1) * NZ, lane : lane + HALF]
@@ -401,13 +437,6 @@
     return value
 
 
-def turns(columns, repeats):
-    residues = jnp.asarray([reverse_bits(i) for i in range(GROUP)], jnp.int32)
-    angle = (residues[:, None] * columns[None, :] % LENGTH).astype(f32) * (2.0 * math.pi / LENGTH)
-    turn = jnp.stack([jnp.cos(angle), jnp.sin(angle)], axis=-1)
-    return jnp.broadcast_to(turn[:, None], (GROUP, repeats) + turn.shape[1:]).reshape(-1, 2)
-
-
 def shards(right_side, start_pressure, conductance, inverses):
     place = jnp.stack(
         [lax.axis_index("gx"), lax.axis_index("gy"), lax.axis_size("gx"), lax.axis_size("gy")]
@@ -418,12 +447,11 @@
     edge_shape, row_shape, dots_shape = shape(GROUP, PLANE), shape(HALF, HALF), shape(8, HALF)
 
     cells_shape = shape(NZ, ROWS, CELLS)
-    start, along, turned_right, to_left, to_right, to_under, to_over = call(
+    start, along, to_left, to_right, to_under, to_over = call(
         entry_kernel,
         [
             field_shape,
-            shape(GROUP, 3 * COLS, PLANE),
-            field_shape,
+            shape(GROUP, 2 * COLS, PLANE),
             shape(8, PLANE),
             shape(8, PLANE),
             shape(2 * HALF, HALF),
@@ -431,19 +459,44 @@
         ],
         start_pressure,
         conductance,
-        right_side,
-        hbm=(0, 1, 2),
+        hbm=(0, 1),
         scratch=[
             pltpu.VMEM((NZ, ROWS, CELLS), f32),
-            pltpu.VMEM((3, NZ, ROWS, CELLS), f32),
-            pltpu.VMEM((NZ, ROWS, CELLS), f32),
-            pltpu.SemaphoreType.DMA((5,)),
+            pltpu.VMEM((2, NZ, ROWS, CELLS), f32),
+            pltpu.SemaphoreType.DMA((3,)),
         ],
     )
     under = shift(to_over, "gy", 1)
     over = shift(to_under, "gy", -1)
     left = shift(to_right, "gx", 1)
     after = shift(to_left, "gx", -1)
+    along_z, turned_right, *tables = call(
+        side_kernel,
+        [shape(GROUP, COLS, PLANE), field_shape]
+        + [shape(2 * CELLS, CELLS, dtype=bf16)] * 2
+        + [shape(CELLS, HALF, dtype=bf16)] * 2,
+        place,
+        to_left,
+        conductance,
+        right_side,
+        jnp.asarray(turn_table()),
+        jnp.asarray(column_table()),
+        jnp.asarray(edge_table()),
+        smem=1,
+        hbm=(2, 3, 4, 5, 6),
+        scratch=[
+            pltpu.VMEM((NZ, ROWS, CELLS), f32),
+            pltpu.VMEM((NZ, ROWS, CELLS), f32),
+            pltpu.VMEM((8, 2 * CELLS), f32),
+            pltpu.VMEM((2 * CELLS, CELLS), f32),
+            pltpu.VMEM((CELLS, HALF), f32),
+            pltpu.SemaphoreType.DMA((5,)),
+        ],
+    )
+    under, over, left, after, along_z, turned_right, tables = lax.optimization_barrier(
+        (under, over, left, after, along_z, turned_right, tables)
+    )
+    table, beside_table = tables[:2], tables[2:]
     chunk, residual = call(
         residual_kernel,
         [shape(GROUP, 4 * COLS, PLANE), field_shape],
@@ -451,6 +504,7 @@
         turned_right,
         start,
         along,
+        along_z,
         left,
         after,
         under,
@@ -458,22 +512,6 @@
         smem=1,
     )
     chunk = exchange(chunk)
-
-    first = lax.axis_index("gx") * COLS
-    columns = first + jnp.arange(COLS, dtype=jnp.int32)
-    table = call(
-        table_kernel,
-        [shape(2 * CELLS, CELLS, dtype=bf16)] * 2,
-        *[jnp.asarray(part) for part in column_tables()],
-        turns(columns, 2),
-    )
-    beside = jnp.stack([first - 1, first - 1, first + COLS, first + COLS]).astype(jnp.int32) % LENGTH
-    edge_table = call(
-        table_kernel,
-        [shape(CELLS, HALF, dtype=bf16)] * 2,
-        *[jnp.asarray(part) for part in edge_tables()],
-        turns(beside, 2),
-    )
     waves = [jnp.asarray(part) for part in wave_table()]
     inverse = inverses.reshape(inverses.shape[1:])
 
@@ -491,7 +529,7 @@
                 pltpu.VMEM((PLANE, 2 * CELLS), f32),
                 pltpu.VMEM((GROUP, 2 * COLS, PLANE), f32),
                 pltpu.VMEM((2, NZ, NZ, HALF), f32),
-                pltpu.SemaphoreType.DMA((2,)),
+                pltpu.SemaphoreType.DMA((4,)),
             ],
             cost=2 * 10**9,
         )
@@ -500,14 +538,14 @@
     cond_edge, cond_row = call(edges_kernel, [edge_shape, row_shape], chunk)
     cond_after = shift(cond_edge, "gx", -1)
     cond_over = shift(cond_row, "gy", -1)
-    parts, cond_after, cond_over = lax.optimization_barrier((parts, cond_after, cond_over))
     parts, dots = solve(0, parts, jnp.zeros((8, HALF), f32))
+    parts, cond_after, cond_over = lax.optimization_barrier((exchange(parts), cond_after, cond_over))
     field, left, after, row_low, row_high = call(
         gather_kernel,
         [field_shape, edge_shape, edge_shape, row_shape, row_shape],
-        exchange(parts),
+        parts,
         *table,
-        *edge_table,
+        *beside_table,
     )
     under = shift(row_high, "gy", 1)
     over = shift(row_low, "gy", -1)

time: 151 us -> 147 us (0.974)
  blocking collectives: 31.8 us -> 71.2 us
  waiting for transfers between devices: 51.5 us -> 24 us
  starting transfers between devices: 42.7 us -> 28.9 us
    all_to_all x2 -> x4, blocking collectives: 31.8 us -> 71.2 us  [exchange(): return lax.all_to_all(parts, 'gx', 0, 0, tiled=True)]
    all_to_all x4 -> x2, waiting for transfers between devices: 30.9 us -> 3.99 us  [exchange(): return lax.all_to_all(parts, 'gx', 0, 0, tiled=True)]
    all_to_all x4 -> x2, starting transfers between devices: 24.2 us -> 10.2 us  [exchange(): return lax.all_to_all(parts, 'gx', 0, 0, tiled=True)]
    pallas_call x12 -> x11, Pallas kernels: 22.2 us -> 21.3 us  [call(): pl.pallas_call(kernel, out_shape=outs, in_specs=specs, out_specs=[out_spe...]
  transfers between devices with their start and end apart: 15 -> 13, of which waited for: 10 -> 8; matrix products, arithmetic and copies ran while one was open for 0% -> 0% of each run, Pallas kernels for 0% -> 2%
where the time goes in v3:
time: 147 us; the launch traced here: 146 us
  blocking collectives  71.2 us (48%)
  starting transfers between devices  28.9 us (20%)
  waiting for transfers between devices  24 us (16%)
  Pallas kernels  21.3 us (14%)
    all_to_all x4, blocking collectives, exchange(): return lax.all_to_all(parts, 'gx', 0, 0, tiled=True)  71.2 us
    pallas_call x11, Pallas kernels, call(): pl.pallas_call(kernel, out_shape=outs, in_specs=specs, out_specs=[out_spe...  21.3 us
    ppermute x8, starting transfers between devices, shift(): lax.ppermute(value, axis, [(i, (i + step) % count) for i in range(count)])  13.3 us
    ppermute x3, waiting for transfers between devices, sum_over(): lax.ppermute(value, axis, [(i, i ^ distance) for i in range(count)])  10.4 us
    all_to_all x2, starting transfers between devices, exchange(): return lax.all_to_all(parts, 'gx', 0, 0, tiled=True)  10.2 us
    ppermute x8, waiting for transfers between devices, shift(): lax.ppermute(value, axis, [(i, (i + step) % count) for i in range(count)])  9.64 us
    ppermute x3, starting transfers between devices, sum_over(): lax.ppermute(value, axis, [(i, i ^ distance) for i in range(count)])  5.33 us
    all_to_all x2, waiting for transfers between devices, exchange(): return lax.all_to_all(parts, 'gx', 0, 0, tiled=True)  3.99 us
  transfers between devices with their start and end apart: 13, of which 8 were waited for; matrix products, arithmetic and copies ran while one was open for 0% of the time, Pallas kernels for 2%

profile of v3, /device:TPU:2, one launch (start us, length us, event | category | flops | bytes accessed | tf_op | source)
XLA Modules:
  0.0 146.2 jit_solution(536178452990167880)
XLA Ops:
  0.6 1.5 %shard_map.112 = (f32[256,256]{1,0:T(8,128)S(1)}, f32[32,16,256]{2,1,0:T(8,128)S(1)}, f32[8,256]{1,0:T(8,128)S(1)}, f32[8,256]{1,0:T(8,128)S(1)}, f32[256,128]{1,0:T(8,128)S(1)}, /*index=5*/f32[128,128]{1,0:T(8,128)S(1)}) custom-call(f32[64,4,256]{2,1,0:T(4,128)} %start_ref.1, f32[3,64,4,256]{3,2,1,0:T(4,128)} %cond_hbm.3), custom_call_target="tpu_custom_call" | custom-call | bytes 1048576 | tf_op jit(solution)/shard_map/pallas_call | solution.py:411
  2.2 5.9 %collective-permute-start.1 = (f32[256,128]{1,0:T(8,128)S(1)}, f32[256,128]{1,0:T(8,128)S(1)}, u32[]{:S(2)}, u32[]{:S(2)}) collective-permute-start(f32[256,128]{1,0:T(8,128)S(1)} %get-tuple-element.46), channel_id=1, source_target_pairs={{0,7},{1,0},{2,1},{3,2},{4,3},{5,4},{6,5},{7,6},{8,15},{9,8},{10,9... | collective-permute-start | bytes 393224 | tf_op jit(solution)/shard_map/ppermute | solution.py:424
  8.7 2.4 %shard_map.113 = (f32[32,8,256]{2,1,0:T(8,128)S(1)}, f32[256,256]{1,0:T(8,128)S(1)}, bf16[512,256]{1,0:T(8,128)(2,1)S(1)}, bf16[512,256]{1,0:T(8,128)(2,1)S(1)},...) custom-call(s32[4]{0:T(128)S(1)} %pad_add_fusion.place, f32[8,256]{1,0:T(8,128)S(1)} %get-tuple-element.48.order_ref, ...), custom_call_target="tpu_custom_call" | custom-call | bytes 1048576 | tf_op jit(solution)/shard_map/pallas_call | solution.py:411
  11.2 2.6 %collective-permute-done.under_ref = f32[128,128]{1,0:T(8,128)S(1)} collective-permute-done((f32[128,128]{1,0:T(8,128)S(1)}, f32[128,128]{1,0:T(8,128)S(1)}, u32[]{:S(2)}, u32[]{:S(2)}) %collective-permute-start) | collective-permute-done | bytes 65568 | tf_op jit(solution)/shard_map/ppermute | solution.py:424
  15.1 24.5 %all_to_all.30.field_ref.chunk_ref = f32[32,32,256]{2,1,0:T(8,128)S(1)} all-to-all(f32[32,32,256]{2,1,0:T(8,128)S(1)} %get-tuple-element.63), channel_id=1, replica_groups=mesh['gx'=32,'gy'=8] {'gx'}, dimensions={0} | all-to-all | bytes 2097152 | tf_op jit(solution)/shard_map/all_to_all | solution.py:428
  39.9 15.0 %all_to_all.31.parts_ref = f32[32,16,256]{2,1,0:T(8,128)S(1)} all-to-all(f32[32,16,256]{2,1,0:T(8,128)S(1)} %shard_map.115), channel_id=1, replica_groups=mesh['gx'=32,'gy'=8] {'gx'}, dimensions={0} | all-to-all | bytes 1048576 | tf_op jit(solution)/shard_map/all_to_all | solution.py:428
  55.0 5.8 %shard_map.116 = (f32[32,40,128]{2,1,0:T(8,128)}, f32[8,128]{1,0:T(8,128)S(1)}) custom-call(f32[32,16,256]{2,1,0:T(8,128)S(1)} %all_to_all.31.parts_ref, f32[64,64,256]{2,1,0:T(8,128)} %bitcast.3, bf16[512,512]{1,0:T(8,128)(2,1)S(1)} %copy-done.1, bf16[512,512]{1,0:T(8,128)(2,1)S(1)} %copy-done.2, f32[8,128]{1,0:T(8,128)S(1)} %broadcast_in_dim.3.dots_ref), custom_call_target="tpu_custom_call" | custom-call | flops 2000000000 | bytes 1048576 | tf_op jit(solution)/shard_map/pallas_call | solution.py:411
  60.7 5.1 %all-to-all-start.2 = ((f32[32,40,128]{2,1,0:T(8,128)}), f32[32,40,128]{2,1,0:T(8,128)S(1)}, u32[]{:S(2)}, u32[]{:S(2)}) async-start(f32[32,40,128]{2,1,0:T(8,128)} %get-tuple-element.66), calls=%async_computation.2 | async-start | bytes 1310720 | tf_op jit(solution)/shard_map/all_to_all | solution.py:428
  65.9 3.3 %collective-permute-start.5 = (f32[128,128]{1,0:T(8,128)S(1)}, f32[128,128]{1,0:T(8,128)S(1)}, u32[]{:S(2)}, u32[]{:S(2)}) collective-permute-start(f32[128,128]{1,0:T(8,128)S(1)} %get-tuple-element.68), channel_id=1, source_target_pairs={{0,7},{1,0},{2,1},{3,2},{4,3},{5,4},{6,5},{7,6},{8,15},{9,8},{10,9... | collective-permute-start | bytes 196616 | tf_op jit(solution)/shard_map/ppermute | solution.py:424
  69.2 4.6 %collective-permute-done.4.cond_next_ref = f32[32,256]{1,0:T(8,128)S(1)} collective-permute-done((f32[32,256]{1,0:T(8,128)S(1)}, f32[32,256]{1,0:T(8,128)S(1)}, u32[]{:S(2)}, u32[]{:S(2)}) %collective-permute-start.4) | collective-permute-done | bytes 32800 | tf_op jit(solution)/shard_map/ppermute | solution.py:424
  73.8 4.0 %all-to-all-done.2.parts_ref = f32[32,40,128]{2,1,0:T(8,128)S(1)} async-done(((f32[32,40,128]{2,1,0:T(8,128)}), f32[32,40,128]{2,1,0:T(8,128)S(1)}, u32[]{:S(2)}, u32[]{:S(2)}) %all-to-all-start.2) | async-done | bytes 655392 | tf_op jit(solution)/shard_map/all_to_all | solution.py:428
  78.4 3.5 %collective-permute-start.7 = (f32[128,128]{1,0:T(8,128)S(1)}, f32[128,128]{1,0:T(8,128)S(1)}, u32[]{:S(2)}, u32[]{:S(2)}) collective-permute-start(f32[128,128]{1,0:T(8,128)S(1)} %get-tuple-element.76), channel_id=1, source_target_pairs={{0,7},{1,0},{2,1},{3,2},{4,3},{5,4},{6,5},{7,6},{8,15},{9,8},{10,9... | collective-permute-start | bytes 196616 | tf_op jit(solution)/shard_map/ppermute | solution.py:424
  81.9 2.3 %collective-permute-done.6.under_ref = f32[128,128]{1,0:T(8,128)S(1)} collective-permute-done((f32[128,128]{1,0:T(8,128)S(1)}, f32[128,128]{1,0:T(8,128)S(1)}, u32[]{:S(2)}, u32[]{:S(2)}) %collective-permute-start.6) | collective-permute-done | bytes 65568 | tf_op jit(solution)/shard_map/ppermute | solution.py:424
  84.2 1.4 shard_map.119
  85.7 15.1 %all_to_all.32.parts_ref = f32[32,16,256]{2,1,0:T(8,128)S(1)} all-to-all(f32[32,16,256]{2,1,0:T(8,128)S(1)} %get-tuple-element.80), channel_id=1, replica_groups=mesh['gx'=32,'gy'=8] {'gx'}, dimensions={0} | all-to-all | bytes 1048576 | tf_op jit(solution)/shard_map/all_to_all | solution.py:428
  100.8 5.4 %shard_map.120 = (f32[32,40,128]{2,1,0:T(8,128)S(1)}, f32[8,128]{1,0:T(8,128)}) custom-call(f32[32,16,256]{2,1,0:T(8,128)S(1)} %all_to_all.32.parts_ref, f32[64,64,256]{2,1,0:T(8,128)} %bitcast.4, bf16[512,512]{1,0:T(8,128)(2,1)S(1)} %copy-done.1, bf16[512,512]{1,0:T(8,128)(2,1)S(1)} %copy-done.3, f32[8,128]{1,0:T(8,128)S(1)} %get-tuple-element.81.dots_ref), custom_call_target="tpu_custom_call" | custom-call | flops 2000000000 | bytes 1048576 | tf_op jit(solution)/shard_map/pallas_call | solution.py:411
  106.1 16.6 %all_to_all.33.parts_ref = f32[32,40,128]{2,1,0:T(8,128)S(1)} all-to-all(f32[32,40,128]{2,1,0:T(8,128)S(1)} %get-tuple-element.82), channel_id=1, replica_groups=mesh['gx'=32,'gy'=8] {'gx'}, dimensions={0} | all-to-all | bytes 1310720 | tf_op jit(solution)/shard_map/all_to_all | solution.py:428
  122.8 1.3 shard_map.121
  124.1 5.1 %all-to-all-start.5 = ((f32[32,24,256]{2,1,0:T(8,128)}), f32[32,24,256]{2,1,0:T(8,128)S(1)}, u32[]{:S(2)}, u32[]{:S(2)}) async-start(f32[32,24,256]{2,1,0:T(8,128)} %get-tuple-element.84), calls=%async_computation.5 | async-start | bytes 1572864 | tf_op jit(solution)/shard_map/all_to_all | solution.py:428
  129.3 3.6 %collective-permute-done.8 = f32[8,128]{1,0:T(8,128)S(1)} collective-permute-done((f32[8,128]{1,0:T(8,128)S(1)}, f32[8,128]{1,0:T(8,128)S(1)}, u32[]{:S(2)}, u32[]{:S(2)}) %collective-permute-start.8) | collective-permute-done | bytes 4128 | tf_op jit(solution)/shard_map/ppermute | solution.py:435
  132.9 2.2 %collective-permute-start.9 = (f32[8,128]{1,0:T(8,128)S(1)}, f32[8,128]{1,0:T(8,128)S(1)}, u32[]{:S(2)}, u32[]{:S(2)}) collective-permute-start(f32[8,128]{1,0:T(8,128)S(1)} %add.9), channel_id=1, source_target_pairs={{0,2},{1,3},{2,0},{3,1},{4,6},{5,7},{6,4},{7,5},{8,10},{9,11},{10,... | collective-permute-start | bytes 12296 | tf_op jit(solution)/shard_map/ppermute | solution.py:435
  135.1 2.3 %collective-permute-done.9 = f32[8,128]{1,0:T(8,128)S(1)} collective-permute-done((f32[8,128]{1,0:T(8,128)S(1)}, f32[8,128]{1,0:T(8,128)S(1)}, u32[]{:S(2)}, u32[]{:S(2)}) %collective-permute-start.9) | collective-permute-done | bytes 4128 | tf_op jit(solution)/shard_map/ppermute | solution.py:435
  137.4 3.1 %collective-permute-start.10 = (f32[8,128]{1,0:T(8,128)S(1)}, f32[8,128]{1,0:T(8,128)S(1)}, u32[]{:S(2)}, u32[]{:S(2)}) collective-permute-start(f32[8,128]{1,0:T(8,128)S(1)} %add.10), channel_id=1, source_target_pairs={{0,4},{1,5},{2,6},{3,7},{4,0},{5,1},{6,2},{7,3},{8,12},{9,13},{10,... | collective-permute-start | bytes 12296 | tf_op jit(solution)/shard_map/ppermute | solution.py:435
  140.5 4.4 %collective-permute-done.10 = f32[8,128]{1,0:T(8,128)S(1)} collective-permute-done((f32[8,128]{1,0:T(8,128)S(1)}, f32[8,128]{1,0:T(8,128)S(1)}, u32[]{:S(2)}, u32[]{:S(2)}) %collective-permute-start.10) | collective-permute-done | bytes 4128 | tf_op jit(solution)/shard_map/ppermute | solution.py:435
  (30 shorter events, 4.4 us)
Async XLA Ops:
  2.2 11.7 %collective-permute-start.1 = (f32[256,128]{1,0:T(8,128)S(1)}, f32[256,128]{1,0:T(8,128)S(1)}, u32[]{:S(2)}, u32[]{:S(2)}) collective-permute-start(f32[256,128]{1,0:T(8,128)S(1)} %get-tuple-element.46), channel_id=1, source_target_pairs={{0,7},{1,0},{2,1},{3,2},{4,3},{5,4},{6,5},{7,6},{8,15},{9,8},{10,9... | collective-permute-start | bytes 393224 | tf_op jit(solution)/shard_map/ppermute | solution.py:424
  8.1 3.0 %collective-permute-start.3 = (f32[8,256]{1,0:T(8,128)S(1)}, f32[8,256]{1,0:T(8,128)S(1)}, u32[]{:S(2)}, u32[]{:S(2)}) collective-permute-start(f32[8,256]{1,0:T(8,128)S(1)} %get-tuple-element.48.order_ref), channel_id=1, source_target_pairs={{0,248},{8,0},{16,8},{24,16},{32,24},{40,32},{48,40},{56,48},{64,5... | collective-permute-start | bytes 24584 | tf_op jit(solution)/shard_map/ppermute | solution.py:424
  8.1 5.7 %collective-permute-start = (f32[128,128]{1,0:T(8,128)S(1)}, f32[128,128]{1,0:T(8,128)S(1)}, u32[]{:S(2)}, u32[]{:S(2)}) collective-permute-start(f32[128,128]{1,0:T(8,128)S(1)} %get-tuple-element.45), channel_id=1, source_target_pairs={{0,1},{1,2},{2,3},{3,4},{4,5},{5,6},{6,7},{7,0},{8,9},{9,10},{10,1... | collective-permute-start | bytes 196616 | tf_op jit(solution)/shard_map/ppermute | solution.py:424
  8.1 3.1 %collective-permute-start.2 = (f32[8,256]{1,0:T(8,128)S(1)}, f32[8,256]{1,0:T(8,128)S(1)}, u32[]{:S(2)}, u32[]{:S(2)}) collective-permute-start(f32[8,256]{1,0:T(8,128)S(1)} %get-tuple-element.47), channel_id=1, source_target_pairs={{0,8},{8,16},{16,24},{24,32},{32,40},{40,48},{48,56},{56,64},{64,7... | collective-permute-start | bytes 24584 | tf_op jit(solution)/shard_map/ppermute | solution.py:424
  8.7 46.3 %copy-start.1 = (bf16[512,512]{1,0:T(8,128)(2,1)S(1)}, bf16[512,512]{1,0:T(8,128)(2,1)}, u32[]{:S(2)}) copy-start(bf16[512,512]{1,0:T(8,128)(2,1)} %constant.28.clone.high_ref) | copy-start | bytes 1572868
  8.7 46.3 %copy-start.2 = (bf16[512,512]{1,0:T(8,128)(2,1)S(1)}, bf16[512,512]{1,0:T(8,128)(2,1)}, u32[]{:S(2)}) copy-start(bf16[512,512]{1,0:T(8,128)(2,1)} %constant.29.clone.low_ref) | copy-start | bytes 1572868
  60.7 17.1 %all-to-all-start.2 = ((f32[32,40,128]{2,1,0:T(8,128)}), f32[32,40,128]{2,1,0:T(8,128)S(1)}, u32[]{:S(2)}, u32[]{:S(2)}) async-start(f32[32,40,128]{2,1,0:T(8,128)} %get-tuple-element.66), calls=%async_computation.2 | async-start | bytes 1310720 | tf_op jit(solution)/shard_map/all_to_all | solution.py:428
  65.9 7.9 %collective-permute-start.5 = (f32[128,128]{1,0:T(8,128)S(1)}, f32[128,128]{1,0:T(8,128)S(1)}, u32[]{:S(2)}, u32[]{:S(2)}) collective-permute-start(f32[128,128]{1,0:T(8,128)S(1)} %get-tuple-element.68), channel_id=1, source_target_pairs={{0,7},{1,0},{2,1},{3,2},{4,3},{5,4},{6,5},{7,6},{8,15},{9,8},{10,9... | collective-permute-start | bytes 196616 | tf_op jit(solution)/shard_map/ppermute | solution.py:424
  69.2 4.6 %collective-permute-start.4 = (f32[32,256]{1,0:T(8,128)S(1)}, f32[32,256]{1,0:T(8,128)S(1)}, u32[]{:S(2)}, u32[]{:S(2)}) collective-permute-start(f32[32,256]{1,0:T(8,128)S(1)} %get-tuple-element.67), channel_id=1, source_target_pairs={{0,248},{8,0},{16,8},{24,16},{32,24},{40,32},{48,40},{56,48},{64,5... | collective-permute-start | bytes 98312 | tf_op jit(solution)/shard_map/ppermute | solution.py:424
  77.8 23.0 %copy-start.3 = (bf16[512,512]{1,0:T(8,128)(2,1)S(1)}, bf16[512,512]{1,0:T(8,128)(2,1)}, u32[]{:S(2)}) copy-start(bf16[512,512]{1,0:T(8,128)(2,1)} %constant.29.clone.low_ref) | copy-start | bytes 1572868
  78.3 5.9 %collective-permute-start.6 = (f32[128,128]{1,0:T(8,128)S(1)}, f32[128,128]{1,0:T(8,128)S(1)}, u32[]{:S(2)}, u32[]{:S(2)}) collective-permute-start(f32[128,128]{1,0:T(8,128)S(1)} %get-tuple-element.75), channel_id=1, source_target_pairs={{0,1},{1,2},{2,3},{3,4},{4,5},{5,6},{6,7},{7,0},{8,9},{9,10},{10,1... | collective-permute-start | bytes 196616 | tf_op jit(solution)/shard_map/ppermute | solution.py:424
  78.4 5.8 %collective-permute-start.7 = (f32[128,128]{1,0:T(8,128)S(1)}, f32[128,128]{1,0:T(8,128)S(1)}, u32[]{:S(2)}, u32[]{:S(2)}) collective-permute-start(f32[128,128]{1,0:T(8,128)S(1)} %get-tuple-element.76), channel_id=1, source_target_pairs={{0,7},{1,0},{2,1},{3,2},{4,3},{5,4},{6,5},{7,6},{8,15},{9,8},{10,9... | collective-permute-start | bytes 196616 | tf_op jit(solution)/shard_map/ppermute | solution.py:424
  100.8 44.2 %copy-start = (f32[64,4,256]{2,1,0:T(4,128)S(1)}, f32[64,4,256]{2,1,0:T(4,128)}, u32[]{:S(2)}) copy-start(f32[64,4,256]{2,1,0:T(4,128)} %start_ref.1) | copy-start | bytes 786436
  124.1 20.9 %all-to-all-start.5 = ((f32[32,24,256]{2,1,0:T(8,128)}), f32[32,24,256]{2,1,0:T(8,128)S(1)}, u32[]{:S(2)}, u32[]{:S(2)}) async-start(f32[32,24,256]{2,1,0:T(8,128)} %get-tuple-element.84), calls=%async_computation.5 | async-start | bytes 1572864 | tf_op jit(solution)/shard_map/all_to_all | solution.py:428
  129.2 3.7 %collective-permute-start.8 = (f32[8,128]{1,0:T(8,128)S(1)}, f32[8,128]{1,0:T(8,128)S(1)}, u32[]{:S(2)}, u32[]{:S(2)}) collective-permute-start(f32[8,128]{1,0:T(8,128)S(1)} %get-tuple-element.86), channel_id=1, source_target_pairs={{0,1},{1,0},{2,3},{3,2},{4,5},{5,4},{6,7},{7,6},{8,9},{9,8},{10,11... | collective-permute-start | bytes 12296 | tf_op jit(solution)/shard_map/ppermute | solution.py:435
  132.9 4.5 %collective-permute-start.9 = (f32[8,128]{1,0:T(8,128)S(1)}, f32[8,128]{1,0:T(8,128)S(1)}, u32[]{:S(2)}, u32[]{:S(2)}) collective-permute-start(f32[8,128]{1,0:T(8,128)S(1)} %add.9), channel_id=1, source_target_pairs={{0,2},{1,3},{2,0},{3,1},{4,6},{5,7},{6,4},{7,5},{8,10},{9,11},{10,... | collective-permute-start | bytes 12296 | tf_op jit(solution)/shard_map/ppermute | solution.py:435
  137.4 7.5 %collective-permute-start.10 = (f32[8,128]{1,0:T(8,128)S(1)}, f32[8,128]{1,0:T(8,128)S(1)}, u32[]{:S(2)}, u32[]{:S(2)}) collective-permute-start(f32[8,128]{1,0:T(8,128)S(1)} %add.10), channel_id=1, source_target_pairs={{0,4},{1,5},{2,6},{3,7},{4,0},{5,1},{6,2},{7,3},{8,12},{9,13},{10,... | collective-permute-start | bytes 12296 | tf_op jit(solution)/shard_map/ppermute | solution.py:435

commit v4 on v3

--- a/solution.py
+++ b/solution.py
@@ -155,21 +155,26 @@
     under = jnp.concatenate([under, roll_half(under)], axis=0)
     over = jnp.concatenate([roll_half(over), over], axis=0)
     cond_over = jnp.concatenate([roll_half(cond_over), cond_over], axis=0)
-    under = jnp.where(place[1] == 0, 0.0, under)
-    over = jnp.where(place[1] == place[3] - 1, 0.0, over)
+    under = jnp.where(place[1:2, :HALF] == 0, 0.0, under)
+    over = jnp.where(place[1:2, :HALF] == place[3:4, :HALF], 0.0, over)
     pair = (behind_rows(field, under), before_rows(field, over))
     return pair, before_rows(along_y, cond_over)
 
 
+def from_below(place, axis, first, second):
+    return jnp.where(place[axis : axis + 1, : first.shape[1]] % 2 == 1, first, second)
+
+
 def entry_kernel(
+    place,
     start_hbm,
     cond_hbm,
     field_ref,
     along_ref,
-    left_ref,
-    right_ref,
-    under_ref,
-    over_ref,
+    x_first_ref,
+    x_second_ref,
+    y_first_ref,
+    y_second_ref,
     start_ref,
     cond_ref,
     semaphores,
@@ -181,17 +186,21 @@
     copies[0].wait()
     field = turned(start_ref)
     field_ref[...] = field
-    left_ref[0:1] = field[0:1]
-    right_ref[0:1] = field[CELLS - 1 :]
-    under_ref[:HALF] = low_row_packed(field)
-    over_ref[...] = high_row_packed(field)
+    high, low = high_row_packed(field), low_row_packed(field)
     for axis in range(2):
         copies[1 + axis].wait()
         along = turned(cond_ref, (axis,))
         if axis == 0:
-            left_ref[1:2] = along[0:1]
+            left = jnp.concatenate([field[0:1], along[0:1]], axis=0)
+            right = jnp.concatenate([field[CELLS - 1 :], along[0:1]], axis=0)
+            x_first_ref[0:2] = from_below(place, 0, left, right)
+            x_second_ref[0:2] = from_below(place, 0, right, left)
         else:
-            under_ref[HALF:] = low_row_packed(along)
+            along_low = low_row_packed(along)
+            y_first_ref[:HALF] = from_below(place, 1, low, high)
+            y_second_ref[:HALF] = from_below(place, 1, high, low)
+            y_first_ref[HALF:] = along_low
+            y_second_ref[HALF:] = along_low
         along_ref[:, COLS * axis : COLS * (axis + 1), :] = along.reshape(GROUP, COLS, PLANE)
 
 
@@ -222,17 +231,21 @@
 
 
 def residual_kernel(
-    place, rhs_ref, field_ref, along_ref, along_z_ref, left_ref, next_ref, under_ref, over_ref, out_ref, residual_ref
+    place, rhs_ref, field_ref, along_ref, along_z_ref, x_first_ref, x_second_ref, y_first_ref, y_second_ref, *outs
 ):
+    out_ref, residual_ref = outs
+    x_swaps, y_swaps = (x_first_ref[...], x_second_ref[...]), (y_first_ref[...], y_second_ref[...])
+    left, after = from_below(place, 0, *x_swaps), from_below(place, 0, *x_swaps[::-1])
+    under, over = from_below(place, 1, *y_swaps), from_below(place, 1, *y_swaps[::-1])
     field = field_ref[...]
     along = [along_ref[:, COLS * axis : COLS * (axis + 1), :].reshape(CELLS, PLANE) for axis in range(2)]
     along += [along_z_ref[...].reshape(CELLS, PLANE)]
     row = lax.broadcasted_iota(jnp.int32, (CELLS, PLANE), 0)
-    behind_x = jnp.where(row == 0, left_ref[0:1], pltpu.roll(field, 1, 0))
-    before_x = jnp.where(row == CELLS - 1, next_ref[0:1], pltpu.roll(field, CELLS - 1, 0))
-    ahead_x = jnp.where(row == CELLS - 1, next_ref[1:2], pltpu.roll(along[0], CELLS - 1, 0))
+    behind_x = jnp.where(row == 0, left[0:1], pltpu.roll(field, 1, 0))
+    before_x = jnp.where(row == CELLS - 1, after[0:1], pltpu.roll(field, CELLS - 1, 0))
+    ahead_x = jnp.where(row == CELLS - 1, after[1:2], pltpu.roll(along[0], CELLS - 1, 0))
     y_pair, ahead_y = y_neighbours(
-        place, field, along[1], under_ref[...], over_ref[:HALF], over_ref[HALF:]
+        place, field, along[1], under[:HALF], over[:HALF], over[HALF:]
     )
     image = operate(field, (behind_x, before_x), y_pair, along, ahead_x, ahead_y)
     residual = rhs_ref[...] - image
@@ -252,7 +265,9 @@
     out_ref[...] = products(table, split(field), ((1,), (0,))).reshape(GROUP, 2 * COLS, PLANE)
 
 
-def solve_kernel(which, parts_ref, inverse_ref, high_ref, low_ref, dots_ref, out_ref, sums_ref, wave, solved, back, held, semaphores):
+def first_solve_kernel(
+    parts_ref, inverse_ref, high_ref, low_ref, dots_ref, out_ref, sums_ref, wave, solved, back, held, semaphores
+):
     copies = []
     for half in range(2):
         for i in range(2):
@@ -260,6 +275,22 @@
             target = held.at[half, planes]
             copies.append(pltpu.make_async_copy(inverse_ref.at[planes, :, lanes], target, semaphores.at[2 * half + i]))
             copies[-1].start()
+    def inverse_block(z, half):
+        return held[half, z]
+
+    solve(0, copies, inverse_block, parts_ref, high_ref, low_ref, dots_ref, out_ref, sums_ref, wave, solved, back)
+
+
+def second_solve_kernel(parts_ref, inverse_ref, high_ref, low_ref, dots_ref, out_ref, wave, solved, sums_ref):
+    def inverse_block(z, half):
+        return inverse_ref[z, :, half * HALF : (half + 1) * HALF]
+
+    solve(2, (), inverse_block, parts_ref, high_ref, low_ref, dots_ref, out_ref, sums_ref, wave, solved, None)
+
+
+def solve(
+    which, copies, inverse_block, parts_ref, high_ref, low_ref, dots_ref, out_ref, sums_ref, wave, solved, back
+):
     table = (high_ref[...], low_ref[...])
     parts = parts_ref[...].reshape(2 * CELLS, PLANE).T
     wave[...] = products(split(parts), table, ((1,), (0,)))
@@ -273,13 +304,13 @@
                     wave[pl.ds(pl.multiple_of(y * NZ + group * 8, 8), 8), lane : lane + HALF] for y, lane in places
                 ]
                 for z in range(8):
-                    block = held[half, group * 8 + z]
+                    block = inverse_block(group * 8 + z, half)
                     sums = tuple(so_far + block * tile[z : z + 1] for so_far, tile in zip(sums, tiles))
                 return sums
 
             sums = tuple(jnp.zeros((NZ, HALF), f32) for _ in places)
             for i in range(2):
-                if pair == 0:
+                if copies and pair == 0:
                     copies[2 * half + i].wait()
                 sums = lax.fori_loop(i * NZ // 16, (i + 1) * NZ // 16, step, sums)
             for result, (y, lane) in zip(sums, places):
@@ -287,7 +318,8 @@
                 product = result * wave[y * NZ : (y + 1) * NZ, lane : lane + HALF]
                 total = total + jnp.sum(product.reshape(NZ // 8, 8, HALF), axis=0)
     row = lax.broadcasted_iota(jnp.int32, (8, HALF), 0)
-    sums_ref[...] = dots_ref[...] + jnp.where(row == which, jnp.sum(total, axis=0, keepdims=True) / LENGTH, 0.0)
+    total = jnp.sum(total, axis=0, keepdims=True) / LENGTH
+    sums_ref[...] = dots_ref[...] + jnp.where(row == which, total, 0.0)
     parts = products(table, split(solved[...]), ((1,), (1,))).reshape(GROUP, 2 * COLS, PLANE)
     for half in range(2):
         out_ref[:, 16 * half : 16 * (half + 1), :] = parts[:, :, half * HALF : (half + 1) * HALF]
@@ -348,7 +380,7 @@
     along = coefficients(chunk_ref)
     column = lax.broadcasted_iota(jnp.int32, (CELLS, PLANE), 0) % COLS
     cond_after = cond_next_ref[...]
-    at_end = place[0] == place[2] - 1
+    at_end = place[0:1] == place[2:3]
     cond_after = jnp.where(at_end, pltpu.roll(cond_after, GROUP - 1, 0), cond_after)
     behind_x = jnp.where(column == 0, edge_rows(left_ref[...]), pltpu.roll(field, 1, 0))
     before_x = jnp.where(column == COLS - 1, edge_rows(next_ref[...]), pltpu.roll(field, CELLS - 1, 0))
@@ -424,30 +456,35 @@
     return lax.ppermute(value, axis, [(i, (i + step) % count) for i in range(count)])
 
 
+def swap(first, second, axis):
+    count = lax.axis_size(axis)
+    first = lax.ppermute(first, axis, [(i, i ^ 1) for i in range(count)])
+    second = lax.ppermute(second, axis, [(i, (i + 2 * (i % 2) - 1) % count) for i in range(count)])
+    return [first, second]
+
+
 def exchange(parts):
     return lax.all_to_all(parts, "gx", 0, 0, tiled=True)
 
 
-def sum_over(value, axis):
-    count = lax.axis_size(axis)
-    distance = 1
-    while distance < count:
-        value = value + lax.ppermute(value, axis, [(i, i ^ distance) for i in range(count)])
-        distance *= 2
+def sum_rows(value):
+    count = lax.axis_size("gy")
+    for mask in (1, 2, 6):
+        value = value + lax.ppermute(value, "gy", [(i, i ^ mask) for i in range(count)])
     return value
 
 
 def shards(right_side, start_pressure, conductance, inverses):
-    place = jnp.stack(
-        [lax.axis_index("gx"), lax.axis_index("gy"), lax.axis_size("gx"), lax.axis_size("gy")]
-    ).astype(jnp.int32)
+    sizes = [lax.axis_size(axis) for axis in ("gx", "gy")]
+    place = jnp.stack([lax.axis_index("gx"), lax.axis_index("gy"), *[size - 1 for size in sizes]]).astype(jnp.int32)
+    spread_place = jnp.broadcast_to(jnp.tile(place, 2)[:, None], (8, PLANE))
     field_shape = shape(CELLS, PLANE)
     parts_shape = shape(GROUP, 2 * COLS, PLANE)
     wide_shape = shape(GROUP, 5 * COLS, HALF)
     edge_shape, row_shape, dots_shape = shape(GROUP, PLANE), shape(HALF, HALF), shape(8, HALF)
 
     cells_shape = shape(NZ, ROWS, CELLS)
-    start, along, to_left, to_right, to_under, to_over = call(
+    start, along, *swaps = call(
         entry_kernel,
         [
             field_shape,
@@ -455,28 +492,26 @@
             shape(8, PLANE),
             shape(8, PLANE),
             shape(2 * HALF, HALF),
-            row_shape,
+            shape(2 * HALF, HALF),
         ],
+        spread_place,
         start_pressure,
         conductance,
-        hbm=(0, 1),
+        hbm=(1, 2),
         scratch=[
             pltpu.VMEM((NZ, ROWS, CELLS), f32),
             pltpu.VMEM((2, NZ, ROWS, CELLS), f32),
             pltpu.SemaphoreType.DMA((3,)),
         ],
     )
-    under = shift(to_over, "gy", 1)
-    over = shift(to_under, "gy", -1)
-    left = shift(to_right, "gx", 1)
-    after = shift(to_left, "gx", -1)
+    halos = swap(swaps[0], swaps[1], "gx") + swap(swaps[2], swaps[3], "gy")
     along_z, turned_right, *tables = call(
         side_kernel,
         [shape(GROUP, COLS, PLANE), field_shape]
         + [shape(2 * CELLS, CELLS, dtype=bf16)] * 2
         + [shape(CELLS, HALF, dtype=bf16)] * 2,
         place,
-        to_left,
+        swaps[0],
         conductance,
         right_side,
         jnp.asarray(turn_table()),
@@ -493,52 +528,44 @@
             pltpu.SemaphoreType.DMA((5,)),
         ],
     )
-    under, over, left, after, along_z, turned_right, tables = lax.optimization_barrier(
-        (under, over, left, after, along_z, turned_right, tables)
-    )
+    halos, along_z, turned_right, tables = lax.optimization_barrier((halos, along_z, turned_right, tables))
     table, beside_table = tables[:2], tables[2:]
     chunk, residual = call(
         residual_kernel,
         [shape(GROUP, 4 * COLS, PLANE), field_shape],
-        place,
+        spread_place,
         turned_right,
         start,
         along,
         along_z,
-        left,
-        after,
-        under,
-        over,
-        smem=1,
+        *halos,
     )
     chunk = exchange(chunk)
     waves = [jnp.asarray(part) for part in wave_table()]
     inverse = inverses.reshape(inverses.shape[1:])
-
-    def solve(which, parts, dots):
-        return call(
-            functools.partial(solve_kernel, which),
-            [wide_shape, dots_shape],
-            parts,
-            inverse,
-            *waves,
-            dots,
-            hbm=(1,),
-            scratch=[
-                pltpu.VMEM((PLANE, 2 * CELLS), f32),
-                pltpu.VMEM((PLANE, 2 * CELLS), f32),
-                pltpu.VMEM((GROUP, 2 * COLS, PLANE), f32),
-                pltpu.VMEM((2, NZ, NZ, HALF), f32),
-                pltpu.SemaphoreType.DMA((4,)),
-            ],
-            cost=2 * 10**9,
-        )
 
     parts = exchange(call(spread_kernel, parts_shape, chunk, *table))
     cond_edge, cond_row = call(edges_kernel, [edge_shape, row_shape], chunk)
     cond_after = shift(cond_edge, "gx", -1)
     cond_over = shift(cond_row, "gy", -1)
-    parts, dots = solve(0, parts, jnp.zeros((8, HALF), f32))
+    wave_shape = pltpu.VMEM((PLANE, 2 * CELLS), f32)
+    parts, dots = call(
+        first_solve_kernel,
+        [wide_shape, dots_shape],
+        parts,
+        inverse,
+        *waves,
+        jnp.zeros((8, HALF), f32),
+        hbm=(1,),
+        scratch=[
+            wave_shape,
+            wave_shape,
+            pltpu.VMEM((GROUP, 2 * COLS, PLANE), f32),
+            pltpu.VMEM((2, NZ, NZ, HALF), f32),
+            pltpu.SemaphoreType.DMA((4,)),
+        ],
+        cost=2 * 10**9,
+    )
     parts, cond_after, cond_over = lax.optimization_barrier((exchange(parts), cond_after, cond_over))
     field, left, after, row_low, row_high = call(
         gather_kernel,
@@ -552,7 +579,7 @@
     image, parts, dots = call(
         image_kernel,
         [field_shape, parts_shape, dots_shape],
-        place,
+        spread_place,
         field,
         chunk,
         left,
@@ -563,13 +590,21 @@
         cond_over,
         dots,
         *table,
-        smem=1,
-    )
-    parts, _ = solve(2, exchange(parts), dots)
+    )
+    parts = call(
+        second_solve_kernel,
+        wide_shape,
+        exchange(parts),
+        inverse,
+        *waves,
+        dots,
+        scratch=[wave_shape, wave_shape, pltpu.VMEM((8, HALF), f32)],
+        cost=2 * 10**9,
+    )
     packed, dots = call(
         pack_kernel, [shape(GROUP, 3 * COLS, PLANE), dots_shape], exchange(parts), *table, field, image
     )
-    dots = sum_over(dots, "gy")
+    dots = sum_rows(dots)
     return tuple(call(finish_kernel, [cells_shape] * 3, exchange(packed), start_pressure, residual, dots))
 
 

time: 147 us -> 145 us (0.986)
  starting transfers between devices: 28.9 us -> 25.4 us
  Pallas kernels: 21.3 us -> 18.7 us
  blocking collectives: 71.2 us -> 73.2 us
    ppermute x8 -> x4, starting transfers between devices: 13.3 us -> 3.58 us  [shift(): lax.ppermute(value, axis, [(i, (i + step) % count) for i in range(count)])]
    ppermute x3 -> x7, starting transfers between devices: 5.33 us -> 11.6 us  [the longest x2 5.59 us: swap(): lax.ppermute(second, axis, [(i, (i + 2 * (i % 2) - 1) % count) for i in r...]
    pallas_call x11, Pallas kernels: 21.3 us -> 18.7 us  [call(): pl.pallas_call(kernel, out_shape=outs, in_specs=specs, out_specs=[out_spe...]
    all_to_all x4, blocking collectives: 71.2 us -> 73.2 us  [exchange(): return lax.all_to_all(parts, 'gx', 0, 0, tiled=True)]
    ppermute x3 -> x7, waiting for transfers between devices: 10.4 us -> 10.1 us  [the longest x3 9.9 us: sum_rows(): lax.ppermute(value, 'gy', [(i, i ^ mask) for i in range(count)])]
    ppermute x8 -> x4, waiting for transfers between devices: 9.64 us -> 9.94 us  [shift(): lax.ppermute(value, axis, [(i, (i + step) % count) for i in range(count)])]
  transfers between devices with their start and end apart: 13 -> 13, of which waited for: 8 -> 7; matrix products, arithmetic and copies ran while one was open for 0% -> 0% of each run, Pallas kernels for 2% -> 2%
where the time goes in v4:
time: 145 us; the launch traced here: 143 us
  blocking collectives  73.2 us (50%)
  starting transfers between devices  25.4 us (18%)
  waiting for transfers between devices  24 us (17%)
  Pallas kernels  18.7 us (13%)
    all_to_all x4, blocking collectives, exchange(): return lax.all_to_all(parts, 'gx', 0, 0, tiled=True)  73.2 us
    pallas_call x11, Pallas kernels, call(): pl.pallas_call(kernel, out_shape=outs, in_specs=specs, out_specs=[out_spe...  18.7 us
    all_to_all x2, starting transfers between devices, exchange(): return lax.all_to_all(parts, 'gx', 0, 0, tiled=True)  10.2 us
    ppermute x4, waiting for transfers between devices, shift(): lax.ppermute(value, axis, [(i, (i + step) % count) for i in range(count)])  9.94 us
    ppermute x3, waiting for transfers between devices, sum_rows(): lax.ppermute(value, 'gy', [(i, i ^ mask) for i in range(count)])  9.9 us
    ppermute x2, starting transfers between devices, swap(): lax.ppermute(second, axis, [(i, (i + 2 * (i % 2) - 1) % count) for i in r...  5.59 us
    ppermute x3, starting transfers between devices, sum_rows(): lax.ppermute(value, 'gy', [(i, i ^ mask) for i in range(count)])  4.01 us
    all_to_all x2, waiting for transfers between devices, exchange(): return lax.all_to_all(parts, 'gx', 0, 0, tiled=True)  3.99 us
  transfers between devices with their start and end apart: 13, of which 7 were waited for; matrix products, arithmetic and copies ran while one was open for 0% of the time, Pallas kernels for 2%

profile of v4, /device:TPU:2, one launch (start us, length us, event | category | flops | bytes accessed | tf_op | source)
XLA Modules:
  0.0 143.3 jit_solution(11012978863304407713)
XLA Ops:
  0.9 1.5 %shard_map.112 = (f32[256,256]{1,0:T(8,128)S(1)}, f32[32,16,256]{2,1,0:T(8,128)S(1)}, f32[8,256]{1,0:T(8,128)S(1)}, f32[8,256]{1,0:T(8,128)S(1)}, f32[256,128]{1,0:T(8,128)S(1)}, /*index=5*/f32[256,128]{1,0:T(8,128)S(1)}) custom-call(s32[8,256]{1,0:T(8,128)S(1)} %broadcast_in_dim.11.place, f32[64,4,256]{2,1,0:T(4,128)} %start_ref.1, f32[3,64,4,256]{3,2,1,0:T(4,128)} %cond_hbm.3), custom_call_target="tpu_custom_call" | custom-call | bytes 1048576 | tf_op jit(solution)/shard_map/pallas_call | solution.py:443
  2.4 2.0 %collective-permute-start.2 = (f32[256,128]{1,0:T(8,128)S(1)}, f32[256,128]{1,0:T(8,128)S(1)}, u32[]{:S(2)}, u32[]{:S(2)}) collective-permute-start(f32[256,128]{1,0:T(8,128)S(1)} %get-tuple-element.46), channel_id=1, source_target_pairs={{0,1},{1,0},{2,3},{3,2},{4,5},{5,4},{6,7},{7,6},{8,9},{9,8},{10,11... | collective-permute-start | bytes 393224 | tf_op jit(solution)/shard_map/ppermute | solution.py:461
  4.4 4.9 %collective-permute-start.3 = (f32[256,128]{1,0:T(8,128)S(1)}, f32[256,128]{1,0:T(8,128)S(1)}, u32[]{:S(2)}, u32[]{:S(2)}) collective-permute-start(f32[256,128]{1,0:T(8,128)S(1)} %get-tuple-element.47), channel_id=1, source_target_pairs={{0,7},{1,2},{2,1},{3,4},{4,3},{5,6},{6,5},{7,0},{8,15},{9,10},{10,... | collective-permute-start | bytes 393224 | tf_op jit(solution)/shard_map/ppermute | solution.py:462
  10.0 2.4 %shard_map.113 = (f32[32,8,256]{2,1,0:T(8,128)S(1)}, f32[256,256]{1,0:T(8,128)S(1)}, bf16[512,256]{1,0:T(8,128)(2,1)S(1)}, bf16[512,256]{1,0:T(8,128)(2,1)S(1)},...) custom-call(s32[4]{0:T(128)S(1)} %pad_add_fusion.place, f32[8,256]{1,0:T(8,128)S(1)} %get-tuple-element.44.order_ref, ...), custom_call_target="tpu_custom_call" | custom-call | bytes 1048576 | tf_op jit(solution)/shard_map/pallas_call | solution.py:443
  13.4 26.4 %all_to_all.30.field_ref.chunk_ref = f32[32,32,256]{2,1,0:T(8,128)S(1)} all-to-all(f32[32,32,256]{2,1,0:T(8,128)S(1)} %get-tuple-element.62), channel_id=1, replica_groups=mesh['gx'=32,'gy'=8] {'gx'}, dimensions={0} | all-to-all | bytes 2097152 | tf_op jit(solution)/shard_map/all_to_all | solution.py:467
  40.1 15.1 %all_to_all.31.parts_ref = f32[32,16,256]{2,1,0:T(8,128)S(1)} all-to-all(f32[32,16,256]{2,1,0:T(8,128)S(1)} %shard_map.115), channel_id=1, replica_groups=mesh['gx'=32,'gy'=8] {'gx'}, dimensions={0} | all-to-all | bytes 1048576 | tf_op jit(solution)/shard_map/all_to_all | solution.py:467
  55.2 5.8 %shard_map.116 = (f32[32,40,128]{2,1,0:T(8,128)}, f32[8,128]{1,0:T(8,128)S(1)}) custom-call(f32[32,16,256]{2,1,0:T(8,128)S(1)} %all_to_all.31.parts_ref, f32[64,64,256]{2,1,0:T(8,128)} %bitcast.3, bf16[512,512]{1,0:T(8,128)(2,1)S(1)} %copy-done.2, bf16[512,512]{1,0:T(8,128)(2,1)S(1)} %copy-done.3, f32[8,128]{1,0:T(8,128)S(1)} %broadcast_in_dim.12.dots_ref), custom_call_target="tpu_custom_call" | custom-call | flops 2000000000 | bytes 1048576 | tf_op jit(solution)/shard_map/pallas_call | solution.py:443
  61.0 5.1 %all-to-all-start.2 = ((f32[32,40,128]{2,1,0:T(8,128)}), f32[32,40,128]{2,1,0:T(8,128)S(1)}, u32[]{:S(2)}, u32[]{:S(2)}) async-start(f32[32,40,128]{2,1,0:T(8,128)} %get-tuple-element.65), calls=%async_computation.2 | async-start | bytes 1310720 | tf_op jit(solution)/shard_map/all_to_all | solution.py:467
  66.4 7.6 %collective-permute-done.4.cond_next_ref = f32[32,256]{1,0:T(8,128)S(1)} collective-permute-done((f32[32,256]{1,0:T(8,128)S(1)}, f32[32,256]{1,0:T(8,128)S(1)}, u32[]{:S(2)}, u32[]{:S(2)}) %collective-permute-start.4) | collective-permute-done | bytes 32800 | tf_op jit(solution)/shard_map/ppermute | solution.py:456
  74.1 4.0 %all-to-all-done.2.parts_ref = f32[32,40,128]{2,1,0:T(8,128)S(1)} async-done(((f32[32,40,128]{2,1,0:T(8,128)}), f32[32,40,128]{2,1,0:T(8,128)S(1)}, u32[]{:S(2)}, u32[]{:S(2)}) %all-to-all-start.2) | async-done | bytes 655392 | tf_op jit(solution)/shard_map/all_to_all | solution.py:467
  78.7 3.2 %collective-permute-start.7 = (f32[128,128]{1,0:T(8,128)S(1)}, f32[128,128]{1,0:T(8,128)S(1)}, u32[]{:S(2)}, u32[]{:S(2)}) collective-permute-start(f32[128,128]{1,0:T(8,128)S(1)} %get-tuple-element.75), channel_id=1, source_target_pairs={{0,7},{1,0},{2,1},{3,2},{4,3},{5,4},{6,5},{7,6},{8,15},{9,8},{10,9... | collective-permute-start | bytes 196616 | tf_op jit(solution)/shard_map/ppermute | solution.py:456
  81.9 2.3 %collective-permute-done.6.under_ref = f32[128,128]{1,0:T(8,128)S(1)} collective-permute-done((f32[128,128]{1,0:T(8,128)S(1)}, f32[128,128]{1,0:T(8,128)S(1)}, u32[]{:S(2)}, u32[]{:S(2)}) %collective-permute-start.6) | collective-permute-done | bytes 65568 | tf_op jit(solution)/shard_map/ppermute | solution.py:456
  85.1 15.1 %all_to_all.32.parts_ref = f32[32,16,256]{2,1,0:T(8,128)S(1)} all-to-all(f32[32,16,256]{2,1,0:T(8,128)S(1)} %get-tuple-element.79), channel_id=1, replica_groups=mesh['gx'=32,'gy'=8] {'gx'}, dimensions={0} | all-to-all | bytes 1048576 | tf_op jit(solution)/shard_map/all_to_all | solution.py:467
  100.2 1.0 copy-done.4
  101.3 3.8 %shard_map.120 = f32[32,40,128]{2,1,0:T(8,128)S(1)} custom-call(f32[32,16,256]{2,1,0:T(8,128)S(1)} %all_to_all.32.parts_ref, f32[64,64,256]{2,1,0:T(8,128)S(1)} %bitcast.4, bf16[512,512]{1,0:T(8,128)(2,1)S(1)} %copy-done.2, bf16[512,512]{1,0:T(8,128)(2,1)S(1)} %copy-done.4, f32[8,128]{1,0:T(8,128)S(1)} %get-tuple-element.80.dots_ref), custom_call_target="tpu_custom_call" | custom-call | flops 2000000000 | bytes 1048576 | tf_op jit(solution)/shard_map/pallas_call | solution.py:443
  105.0 16.6 %all_to_all.33.parts_ref = f32[32,40,128]{2,1,0:T(8,128)S(1)} all-to-all(f32[32,40,128]{2,1,0:T(8,128)S(1)} %shard_map.120), channel_id=1, replica_groups=mesh['gx'=32,'gy'=8] {'gx'}, dimensions={0} | all-to-all | bytes 1310720 | tf_op jit(solution)/shard_map/all_to_all | solution.py:467
  121.7 1.3 shard_map.121
  123.0 5.1 %all-to-all-start.5 = ((f32[32,24,256]{2,1,0:T(8,128)}), f32[32,24,256]{2,1,0:T(8,128)S(1)}, u32[]{:S(2)}, u32[]{:S(2)}) async-start(f32[32,24,256]{2,1,0:T(8,128)} %get-tuple-element.82), calls=%async_computation.5 | async-start | bytes 1572864 | tf_op jit(solution)/shard_map/all_to_all | solution.py:467
  128.2 3.6 %collective-permute-done.8 = f32[8,128]{1,0:T(8,128)S(1)} collective-permute-done((f32[8,128]{1,0:T(8,128)S(1)}, f32[8,128]{1,0:T(8,128)S(1)}, u32[]{:S(2)}, u32[]{:S(2)}) %collective-permute-start.8) | collective-permute-done | bytes 4128 | tf_op jit(solution)/shard_map/ppermute | solution.py:473
  131.8 1.3 collective-permute-start.9
  133.0 3.3 %collective-permute-done.9 = f32[8,128]{1,0:T(8,128)S(1)} collective-permute-done((f32[8,128]{1,0:T(8,128)S(1)}, f32[8,128]{1,0:T(8,128)S(1)}, u32[]{:S(2)}, u32[]{:S(2)}) %collective-permute-start.9) | collective-permute-done | bytes 4128 | tf_op jit(solution)/shard_map/ppermute | solution.py:473
  136.3 2.7 %collective-permute-start.10 = (f32[8,128]{1,0:T(8,128)S(1)}, f32[8,128]{1,0:T(8,128)S(1)}, u32[]{:S(2)}, u32[]{:S(2)}) collective-permute-start(f32[8,128]{1,0:T(8,128)S(1)} %add.10), channel_id=1, source_target_pairs={{0,6},{1,7},{2,4},{3,5},{4,2},{5,3},{6,0},{7,1},{8,14},{9,15},{10,... | collective-permute-start | bytes 12296 | tf_op jit(solution)/shard_map/ppermute | solution.py:473
  139.0 3.0 %collective-permute-done.10 = f32[8,128]{1,0:T(8,128)S(1)} collective-permute-done((f32[8,128]{1,0:T(8,128)S(1)}, f32[8,128]{1,0:T(8,128)S(1)}, u32[]{:S(2)}, u32[]{:S(2)}) %collective-permute-start.10) | collective-permute-done | bytes 4128 | tf_op jit(solution)/shard_map/ppermute | solution.py:473
  142.0 1.3 shard_map.122
  (35 shorter events, 4.2 us)
Async XLA Ops:
  2.4 10.0 %collective-permute-start.2 = (f32[256,128]{1,0:T(8,128)S(1)}, f32[256,128]{1,0:T(8,128)S(1)}, u32[]{:S(2)}, u32[]{:S(2)}) collective-permute-start(f32[256,128]{1,0:T(8,128)S(1)} %get-tuple-element.46), channel_id=1, source_target_pairs={{0,1},{1,0},{2,3},{3,2},{4,5},{5,4},{6,7},{7,6},{8,9},{9,8},{10,11... | collective-permute-start | bytes 393224 | tf_op jit(solution)/shard_map/ppermute | solution.py:461
  4.4 8.2 %collective-permute-start.3 = (f32[256,128]{1,0:T(8,128)S(1)}, f32[256,128]{1,0:T(8,128)S(1)}, u32[]{:S(2)}, u32[]{:S(2)}) collective-permute-start(f32[256,128]{1,0:T(8,128)S(1)} %get-tuple-element.47), channel_id=1, source_target_pairs={{0,7},{1,2},{2,1},{3,4},{4,3},{5,6},{6,5},{7,0},{8,15},{9,10},{10,... | collective-permute-start | bytes 393224 | tf_op jit(solution)/shard_map/ppermute | solution.py:462
  9.4 3.1 %collective-permute-start = (f32[8,256]{1,0:T(8,128)S(1)}, f32[8,256]{1,0:T(8,128)S(1)}, u32[]{:S(2)}, u32[]{:S(2)}) collective-permute-start(f32[8,256]{1,0:T(8,128)S(1)} %get-tuple-element.44.order_ref), channel_id=1, source_target_pairs={{0,8},{8,0},{16,24},{24,16},{32,40},{40,32},{48,56},{56,48},{64,72... | collective-permute-start | bytes 24584 | tf_op jit(solution)/shard_map/ppermute | solution.py:461
  9.4 45.8 %copy-start.2 = (bf16[512,512]{1,0:T(8,128)(2,1)S(1)}, bf16[512,512]{1,0:T(8,128)(2,1)}, u32[]{:S(2)}) copy-start(bf16[512,512]{1,0:T(8,128)(2,1)} %constant.28.clone.high_ref) | copy-start | bytes 1572868
  9.4 45.8 %copy-start.3 = (bf16[512,512]{1,0:T(8,128)(2,1)S(1)}, bf16[512,512]{1,0:T(8,128)(2,1)}, u32[]{:S(2)}) copy-start(bf16[512,512]{1,0:T(8,128)(2,1)} %constant.29.clone.low_ref) | copy-start | bytes 1572868
  9.4 3.1 %collective-permute-start.1 = (f32[8,256]{1,0:T(8,128)S(1)}, f32[8,256]{1,0:T(8,128)S(1)}, u32[]{:S(2)}, u32[]{:S(2)}) collective-permute-start(f32[8,256]{1,0:T(8,128)S(1)} %get-tuple-element.45), channel_id=1, source_target_pairs={{0,248},{8,16},{16,8},{24,32},{32,24},{40,48},{48,40},{56,64},{64,... | collective-permute-start | bytes 24584 | tf_op jit(solution)/shard_map/ppermute | solution.py:462
  61.0 17.1 %all-to-all-start.2 = ((f32[32,40,128]{2,1,0:T(8,128)}), f32[32,40,128]{2,1,0:T(8,128)S(1)}, u32[]{:S(2)}, u32[]{:S(2)}) async-start(f32[32,40,128]{2,1,0:T(8,128)} %get-tuple-element.65), calls=%async_computation.2 | async-start | bytes 1310720 | tf_op jit(solution)/shard_map/all_to_all | solution.py:467
  66.2 7.9 %collective-permute-start.5 = (f32[128,128]{1,0:T(8,128)S(1)}, f32[128,128]{1,0:T(8,128)S(1)}, u32[]{:S(2)}, u32[]{:S(2)}) collective-permute-start(f32[128,128]{1,0:T(8,128)S(1)} %get-tuple-element.67), channel_id=1, source_target_pairs={{0,7},{1,0},{2,1},{3,2},{4,3},{5,4},{6,5},{7,6},{8,15},{9,8},{10,9... | collective-permute-start | bytes 196616 | tf_op jit(solution)/shard_map/ppermute | solution.py:456
  66.3 7.7 %collective-permute-start.4 = (f32[32,256]{1,0:T(8,128)S(1)}, f32[32,256]{1,0:T(8,128)S(1)}, u32[]{:S(2)}, u32[]{:S(2)}) collective-permute-start(f32[32,256]{1,0:T(8,128)S(1)} %get-tuple-element.66), channel_id=1, source_target_pairs={{0,248},{8,0},{16,8},{24,16},{32,24},{40,32},{48,40},{56,48},{64,5... | collective-permute-start | bytes 98312 | tf_op jit(solution)/shard_map/ppermute | solution.py:456
  78.1 22.1 %copy-start.1 = (f32[1,64,64,256]{3,2,1,0:T(8,128)S(1)}, f32[1,64,64,256]{3,2,1,0:T(8,128)}, u32[]{:S(2)}) copy-start(f32[1,64,64,256]{3,2,1,0:T(8,128)} %param.12) | copy-start | bytes 12582916
  78.6 5.6 %collective-permute-start.6 = (f32[128,128]{1,0:T(8,128)S(1)}, f32[128,128]{1,0:T(8,128)S(1)}, u32[]{:S(2)}, u32[]{:S(2)}) collective-permute-start(f32[128,128]{1,0:T(8,128)S(1)} %get-tuple-element.74), channel_id=1, source_target_pairs={{0,1},{1,2},{2,3},{3,4},{4,5},{5,6},{6,7},{7,0},{8,9},{9,10},{10,1... | collective-permute-start | bytes 196616 | tf_op jit(solution)/shard_map/ppermute | solution.py:456
  78.7 5.5 %collective-permute-start.7 = (f32[128,128]{1,0:T(8,128)S(1)}, f32[128,128]{1,0:T(8,128)S(1)}, u32[]{:S(2)}, u32[]{:S(2)}) collective-permute-start(f32[128,128]{1,0:T(8,128)S(1)} %get-tuple-element.75), channel_id=1, source_target_pairs={{0,7},{1,0},{2,1},{3,2},{4,3},{5,4},{6,5},{7,6},{8,15},{9,8},{10,9... | collective-permute-start | bytes 196616 | tf_op jit(solution)/shard_map/ppermute | solution.py:456
  100.2 1.0 copy-start.4
  101.3 40.8 %copy-start = (f32[64,4,256]{2,1,0:T(4,128)S(1)}, f32[64,4,256]{2,1,0:T(4,128)}, u32[]{:S(2)}) copy-start(f32[64,4,256]{2,1,0:T(4,128)} %start_ref.1) | copy-start | bytes 786436
  123.0 19.1 %all-to-all-start.5 = ((f32[32,24,256]{2,1,0:T(8,128)}), f32[32,24,256]{2,1,0:T(8,128)S(1)}, u32[]{:S(2)}, u32[]{:S(2)}) async-start(f32[32,24,256]{2,1,0:T(8,128)} %get-tuple-element.82), calls=%async_computation.5 | async-start | bytes 1572864 | tf_op jit(solution)/shard_map/all_to_all | solution.py:467
  128.1 3.7 %collective-permute-start.8 = (f32[8,128]{1,0:T(8,128)S(1)}, f32[8,128]{1,0:T(8,128)S(1)}, u32[]{:S(2)}, u32[]{:S(2)}) collective-permute-start(f32[8,128]{1,0:T(8,128)S(1)} %get-tuple-element.84), channel_id=1, source_target_pairs={{0,1},{1,0},{2,3},{3,2},{4,5},{5,4},{6,7},{7,6},{8,9},{9,8},{10,11... | collective-permute-start | bytes 12296 | tf_op jit(solution)/shard_map/ppermute | solution.py:473
  131.8 4.5 %collective-permute-start.9 = (f32[8,128]{1,0:T(8,128)S(1)}, f32[8,128]{1,0:T(8,128)S(1)}, u32[]{:S(2)}, u32[]{:S(2)}) collective-permute-start(f32[8,128]{1,0:T(8,128)S(1)} %add.9), channel_id=1, source_target_pairs={{0,2},{1,3},{2,0},{3,1},{4,6},{5,7},{6,4},{7,5},{8,10},{9,11},{10,... | collective-permute-start | bytes 12296 | tf_op jit(solution)/shard_map/ppermute | solution.py:473
  136.3 5.7 %collective-permute-start.10 = (f32[8,128]{1,0:T(8,128)S(1)}, f32[8,128]{1,0:T(8,128)S(1)}, u32[]{:S(2)}, u32[]{:S(2)}) collective-permute-start(f32[8,128]{1,0:T(8,128)S(1)} %add.10), channel_id=1, source_target_pairs={{0,6},{1,7},{2,4},{3,5},{4,2},{5,3},{6,0},{7,1},{8,14},{9,15},{10,... | collective-permute-start | bytes 12296 | tf_op jit(solution)/shard_map/ppermute | solution.py:473

commit v5 on v4

--- a/solution.py
+++ b/solution.py
@@ -151,22 +151,22 @@
     return jnp.concatenate(rows, axis=0).T
 
 
-def y_neighbours(place, field, along_y, under, over, cond_over):
+def y_neighbours(field, along_y, under, over, cond_over):
     under = jnp.concatenate([under, roll_half(under)], axis=0)
     over = jnp.concatenate([roll_half(over), over], axis=0)
     cond_over = jnp.concatenate([roll_half(cond_over), cond_over], axis=0)
-    under = jnp.where(place[1:2, :HALF] == 0, 0.0, under)
-    over = jnp.where(place[1:2, :HALF] == place[3:4, :HALF], 0.0, over)
+    row = lax.axis_index("gy")
+    under = jnp.where(row == 0, 0.0, under)
+    over = jnp.where(row == lax.axis_size("gy") - 1, 0.0, over)
     pair = (behind_rows(field, under), before_rows(field, over))
     return pair, before_rows(along_y, cond_over)
 
 
-def from_below(place, axis, first, second):
-    return jnp.where(place[axis : axis + 1, : first.shape[1]] % 2 == 1, first, second)
+def from_below(axis, first, second):
+    return jnp.where(lax.axis_index(axis) % 2 == 1, first, second)
 
 
 def entry_kernel(
-    place,
     start_hbm,
     cond_hbm,
     field_ref,
@@ -193,21 +193,21 @@
         if axis == 0:
             left = jnp.concatenate([field[0:1], along[0:1]], axis=0)
             right = jnp.concatenate([field[CELLS - 1 :], along[0:1]], axis=0)
-            x_first_ref[0:2] = from_below(place, 0, left, right)
-            x_second_ref[0:2] = from_below(place, 0, right, left)
+            x_first_ref[0:2] = from_below("gx", left, right)
+            x_second_ref[0:2] = from_below("gx", right, left)
         else:
             along_low = low_row_packed(along)
-            y_first_ref[:HALF] = from_below(place, 1, low, high)
-            y_second_ref[:HALF] = from_below(place, 1, high, low)
+            y_first_ref[:HALF] = from_below("gy", low, high)
+            y_second_ref[:HALF] = from_below("gy", high, low)
             y_first_ref[HALF:] = along_low
             y_second_ref[HALF:] = along_low
         along_ref[:, COLS * axis : COLS * (axis + 1), :] = along.reshape(GROUP, COLS, PLANE)
 
 
-def side_kernel(place, order_ref, cond_hbm, right_hbm, turns_hbm, column_hbm, edge_hbm, *refs):
+def side_kernel(order_ref, cond_hbm, right_hbm, turns_hbm, column_hbm, edge_hbm, *refs):
     along_out, right_out, high_ref, low_ref, edge_high_ref, edge_low_ref = refs[:6]
     cond_ref, rhs_ref, turns_ref, column_ref, edge_ref, semaphores = refs[6:]
-    sources = (cond_hbm.at[2], right_hbm, turns_hbm.at[place[0]], column_hbm, edge_hbm)
+    sources = (cond_hbm.at[2], right_hbm, turns_hbm.at[lax.axis_index("gx")], column_hbm, edge_hbm)
     targets = (cond_ref, rhs_ref, turns_ref, column_ref, edge_ref)
     copies = [pltpu.make_async_copy(*pair, semaphores.at[i]) for i, pair in enumerate(zip(sources, targets))]
     for copy in copies:
@@ -231,12 +231,12 @@
 
 
 def residual_kernel(
-    place, rhs_ref, field_ref, along_ref, along_z_ref, x_first_ref, x_second_ref, y_first_ref, y_second_ref, *outs
+    rhs_ref, field_ref, along_ref, along_z_ref, x_first_ref, x_second_ref, y_first_ref, y_second_ref, *outs
 ):
     out_ref, residual_ref = outs
     x_swaps, y_swaps = (x_first_ref[...], x_second_ref[...]), (y_first_ref[...], y_second_ref[...])
-    left, after = from_below(place, 0, *x_swaps), from_below(place, 0, *x_swaps[::-1])
-    under, over = from_below(place, 1, *y_swaps), from_below(place, 1, *y_swaps[::-1])
+    left, after = from_below("gx", *x_swaps), from_below("gx", *x_swaps[::-1])
+    under, over = from_below("gy", *y_swaps), from_below("gy", *y_swaps[::-1])
     field = field_ref[...]
     along = [along_ref[:, COLS * axis : COLS * (axis + 1), :].reshape(CELLS, PLANE) for axis in range(2)]
     along += [along_z_ref[...].reshape(CELLS, PLANE)]
@@ -245,7 +245,7 @@
     before_x = jnp.where(row == CELLS - 1, after[0:1], pltpu.roll(field, CELLS - 1, 0))
     ahead_x = jnp.where(row == CELLS - 1, after[1:2], pltpu.roll(along[0], CELLS - 1, 0))
     y_pair, ahead_y = y_neighbours(
-        place, field, along[1], under[:HALF], over[:HALF], over[HALF:]
+        field, along[1], under[:HALF], over[:HALF], over[HALF:]
     )
     image = operate(field, (behind_x, before_x), y_pair, along, ahead_x, ahead_y)
     residual = rhs_ref[...] - image
@@ -265,32 +265,15 @@
     out_ref[...] = products(table, split(field), ((1,), (0,))).reshape(GROUP, 2 * COLS, PLANE)
 
 
-def first_solve_kernel(
-    parts_ref, inverse_ref, high_ref, low_ref, dots_ref, out_ref, sums_ref, wave, solved, back, held, semaphores
-):
-    copies = []
-    for half in range(2):
-        for i in range(2):
-            planes, lanes = pl.ds(i * NZ // 2, NZ // 2), pl.ds(half * HALF, HALF)
-            target = held.at[half, planes]
-            copies.append(pltpu.make_async_copy(inverse_ref.at[planes, :, lanes], target, semaphores.at[2 * half + i]))
-            copies[-1].start()
-    def inverse_block(z, half):
-        return held[half, z]
-
-    solve(0, copies, inverse_block, parts_ref, high_ref, low_ref, dots_ref, out_ref, sums_ref, wave, solved, back)
+def first_solve_kernel(parts_ref, inverse_ref, high_ref, low_ref, out_ref, sums_ref, wave, solved, back):
+    solve(0, parts_ref, inverse_ref, high_ref, low_ref, None, out_ref, sums_ref, wave, solved, back)
 
 
 def second_solve_kernel(parts_ref, inverse_ref, high_ref, low_ref, dots_ref, out_ref, wave, solved, sums_ref):
-    def inverse_block(z, half):
-        return inverse_ref[z, :, half * HALF : (half + 1) * HALF]
-
-    solve(2, (), inverse_block, parts_ref, high_ref, low_ref, dots_ref, out_ref, sums_ref, wave, solved, None)
-
-
-def solve(
-    which, copies, inverse_block, parts_ref, high_ref, low_ref, dots_ref, out_ref, sums_ref, wave, solved, back
-):
+    solve(2, parts_ref, inverse_ref, high_ref, low_ref, dots_ref, out_ref, sums_ref, wave, solved, None)
+
+
+def solve(which, parts_ref, inverse_ref, high_ref, low_ref, dots_ref, out_ref, sums_ref, wave, solved, back):
     table = (high_ref[...], low_ref[...])
     parts = parts_ref[...].reshape(2 * CELLS, PLANE).T
     wave[...] = products(split(parts), table, ((1,), (0,)))
@@ -304,22 +287,20 @@
                     wave[pl.ds(pl.multiple_of(y * NZ + group * 8, 8), 8), lane : lane + HALF] for y, lane in places
                 ]
                 for z in range(8):
-                    block = inverse_block(group * 8 + z, half)
+                    block = inverse_ref[group * 8 + z, :, half * HALF : (half + 1) * HALF]
                     sums = tuple(so_far + block * tile[z : z + 1] for so_far, tile in zip(sums, tiles))
                 return sums
 
             sums = tuple(jnp.zeros((NZ, HALF), f32) for _ in places)
-            for i in range(2):
-                if copies and pair == 0:
-                    copies[2 * half + i].wait()
-                sums = lax.fori_loop(i * NZ // 16, (i + 1) * NZ // 16, step, sums)
+            sums = lax.fori_loop(0, NZ // 8, step, sums)
             for result, (y, lane) in zip(sums, places):
                 solved[y * NZ : (y + 1) * NZ, lane : lane + HALF] = result
                 product = result * wave[y * NZ : (y + 1) * NZ, lane : lane + HALF]
                 total = total + jnp.sum(product.reshape(NZ // 8, 8, HALF), axis=0)
     row = lax.broadcasted_iota(jnp.int32, (8, HALF), 0)
     total = jnp.sum(total, axis=0, keepdims=True) / LENGTH
-    sums_ref[...] = dots_ref[...] + jnp.where(row == which, total, 0.0)
+    others = 0.0 if dots_ref is None else dots_ref[...]
+    sums_ref[...] = jnp.where(row == which, total, others)
     parts = products(table, split(solved[...]), ((1,), (1,))).reshape(GROUP, 2 * COLS, PLANE)
     for half in range(2):
         out_ref[:, 16 * half : 16 * (half + 1), :] = parts[:, :, half * HALF : (half + 1) * HALF]
@@ -360,7 +341,6 @@
 
 
 def image_kernel(
-    place,
     field_ref,
     chunk_ref,
     left_ref,
@@ -380,12 +360,12 @@
     along = coefficients(chunk_ref)
     column = lax.broadcasted_iota(jnp.int32, (CELLS, PLANE), 0) % COLS
     cond_after = cond_next_ref[...]
-    at_end = place[0:1] == place[2:3]
+    at_end = lax.axis_index("gx") == lax.axis_size("gx") - 1
     cond_after = jnp.where(at_end, pltpu.roll(cond_after, GROUP - 1, 0), cond_after)
     behind_x = jnp.where(column == 0, edge_rows(left_ref[...]), pltpu.roll(field, 1, 0))
     before_x = jnp.where(column == COLS - 1, edge_rows(next_ref[...]), pltpu.roll(field, CELLS - 1, 0))
     ahead_x = jnp.where(column == COLS - 1, edge_rows(cond_after), pltpu.roll(along[0], CELLS - 1, 0))
-    y_pair, ahead_y = y_neighbours(place, field, along[1], under_ref[...], over_ref[...], cond_over_ref[...])
+    y_pair, ahead_y = y_neighbours(field, along[1], under_ref[...], over_ref[...], cond_over_ref[...])
     image = operate(field, (behind_x, before_x), y_pair, along, ahead_x, ahead_y)
     image_ref[...] = image
     table = (high_ref[...], low_ref[...])
@@ -432,8 +412,8 @@
     return jax.ShapeDtypeStruct(dims, dtype)
 
 
-def call(kernel, outs, *args, smem=0, hbm=(), scratch=(), cost=0):
-    specs = [pl.BlockSpec(memory_space=pltpu.SMEM if i < smem else pltpu.VMEM) for i in range(len(args))]
+def call(kernel, outs, *args, hbm=(), scratch=(), cost=0):
+    specs = [pl.BlockSpec(memory_space=pltpu.VMEM) for _ in args]
     args = list(args)
     for i in hbm:
         specs[i] = pl.BlockSpec(memory_space=pltpu.HBM)
@@ -475,9 +455,6 @@
 
 
 def shards(right_side, start_pressure, conductance, inverses):
-    sizes = [lax.axis_size(axis) for axis in ("gx", "gy")]
-    place = jnp.stack([lax.axis_index("gx"), lax.axis_index("gy"), *[size - 1 for size in sizes]]).astype(jnp.int32)
-    spread_place = jnp.broadcast_to(jnp.tile(place, 2)[:, None], (8, PLANE))
     field_shape = shape(CELLS, PLANE)
     parts_shape = shape(GROUP, 2 * COLS, PLANE)
     wide_shape = shape(GROUP, 5 * COLS, HALF)
@@ -494,10 +471,9 @@
             shape(2 * HALF, HALF),
             shape(2 * HALF, HALF),
         ],
-        spread_place,
         start_pressure,
         conductance,
-        hbm=(1, 2),
+        hbm=(0, 1),
         scratch=[
             pltpu.VMEM((NZ, ROWS, CELLS), f32),
             pltpu.VMEM((2, NZ, ROWS, CELLS), f32),
@@ -510,15 +486,13 @@
         [shape(GROUP, COLS, PLANE), field_shape]
         + [shape(2 * CELLS, CELLS, dtype=bf16)] * 2
         + [shape(CELLS, HALF, dtype=bf16)] * 2,
-        place,
         swaps[0],
         conductance,
         right_side,
         jnp.asarray(turn_table()),
         jnp.asarray(column_table()),
         jnp.asarray(edge_table()),
-        smem=1,
-        hbm=(2, 3, 4, 5, 6),
+        hbm=(1, 2, 3, 4, 5),
         scratch=[
             pltpu.VMEM((NZ, ROWS, CELLS), f32),
             pltpu.VMEM((NZ, ROWS, CELLS), f32),
@@ -533,7 +507,6 @@
     chunk, residual = call(
         residual_kernel,
         [shape(GROUP, 4 * COLS, PLANE), field_shape],
-        spread_place,
         turned_right,
         start,
         along,
@@ -555,15 +528,7 @@
         parts,
         inverse,
         *waves,
-        jnp.zeros((8, HALF), f32),
-        hbm=(1,),
-        scratch=[
-            wave_shape,
-            wave_shape,
-            pltpu.VMEM((GROUP, 2 * COLS, PLANE), f32),
-            pltpu.VMEM((2, NZ, NZ, HALF), f32),
-            pltpu.SemaphoreType.DMA((4,)),
-        ],
+        scratch=[wave_shape, wave_shape, pltpu.VMEM((GROUP, 2 * COLS, PLANE), f32)],
         cost=2 * 10**9,
     )
     parts, cond_after, cond_over = lax.optimization_barrier((exchange(parts), cond_after, cond_over))
@@ -579,7 +544,6 @@
     image, parts, dots = call(
         image_kernel,
         [field_shape, parts_shape, dots_shape],
-        spread_place,
         field,
         chunk,
         left,

time: 145 us -> 143 us (0.986)
  starting transfers between devices: 25.4 us -> 28 us
  waiting for transfers between devices: 24 us -> 22.2 us
  Pallas kernels: 18.7 us -> 17.1 us
  blocking collectives: 73.2 us -> 71.7 us
    ppermute x2, starting transfers between devices: 2.01 us -> 3.6 us  [swap(): first = lax.ppermute(first, axis, [(i, i ^ 1) for i in range(count)])]
    pallas_call x11, Pallas kernels: 18.7 us -> 17.1 us  [call(): pl.pallas_call(kernel, out_shape=outs, in_specs=specs, out_specs=[out_spe...]
    all_to_all x4, blocking collectives: 73.2 us -> 71.7 us  [exchange(): return lax.all_to_all(parts, 'gx', 0, 0, tiled=True)]
  transfers between devices with their start and end apart: 13 -> 13, of which waited for: 7 -> 6; matrix products, arithmetic and copies ran while one was open for 0% -> 0% of each run, Pallas kernels for 2% -> 1%
where the time goes in v5:
time: 143 us; the launch traced here: 141 us
  blocking collectives  71.7 us (50%)
  starting transfers between devices  28 us (20%)
  waiting for transfers between devices  22.2 us (16%)
  Pallas kernels  17.1 us (12%)
    all_to_all x4, blocking collectives, exchange(): return lax.all_to_all(parts, 'gx', 0, 0, tiled=True)  71.7 us
    pallas_call x11, Pallas kernels, call(): pl.pallas_call(kernel, out_shape=outs, in_specs=specs, out_specs=[out_spe...  17.1 us
    all_to_all x2, starting transfers between devices, exchange(): return lax.all_to_all(parts, 'gx', 0, 0, tiled=True)  10.2 us
    ppermute x3, waiting for transfers between devices, sum_rows(): lax.ppermute(value, 'gy', [(i, i ^ mask) for i in range(count)])  9.38 us
    ppermute x4, waiting for transfers between devices, shift(): lax.ppermute(value, axis, [(i, (i + step) % count) for i in range(count)])  8.8 us
    ppermute x2, starting transfers between devices, swap(): lax.ppermute(second, axis, [(i, (i + 2 * (i % 2) - 1) % count) for i in r...  4.95 us
    ppermute x4, starting transfers between devices, shift(): lax.ppermute(value, axis, [(i, (i + step) % count) for i in range(count)])  4.72 us
    ppermute x3, starting transfers between devices, sum_rows(): lax.ppermute(value, 'gy', [(i, i ^ mask) for i in range(count)])  4.53 us
  transfers between devices with their start and end apart: 13, of which 6 were waited for; matrix products, arithmetic and copies ran while one was open for 0% of the time, Pallas kernels for 1%

profile of v5, /device:TPU:2, one launch (start us, length us, event | category | flops | bytes accessed | tf_op | source)
XLA Modules:
  0.0 140.8 jit_solution(1921788787576032533)
XLA Ops:
  0.6 1.6 %shard_map.112 = (f32[256,256]{1,0:T(8,128)S(1)}, f32[32,16,256]{2,1,0:T(8,128)S(1)}, f32[8,256]{1,0:T(8,128)S(1)}, f32[8,256]{1,0:T(8,128)S(1)}, f32[256,128]{1,0:T(8,128)S(1)}, /*index=5*/f32[256,128]{1,0:T(8,128)S(1)}) custom-call(f32[64,4,256]{2,1,0:T(4,128)} %start_ref.1, f32[3,64,4,256]{3,2,1,0:T(4,128)} %cond_hbm.3), custom_call_target="tpu_custom_call" | custom-call | bytes 1048576 | tf_op jit(solution)/shard_map/pallas_call | solution.py:423
  2.2 2.0 %collective-permute-start.2 = (f32[256,128]{1,0:T(8,128)S(1)}, f32[256,128]{1,0:T(8,128)S(1)}, u32[]{:S(2)}, u32[]{:S(2)}) collective-permute-start(f32[256,128]{1,0:T(8,128)S(1)} %get-tuple-element.46), channel_id=1, source_target_pairs={{0,1},{1,0},{2,3},{3,2},{4,5},{5,4},{6,7},{7,6},{8,9},{9,8},{10,11... | collective-permute-start | bytes 393224 | tf_op jit(solution)/shard_map/ppermute | solution.py:441
  4.2 4.9 %collective-permute-start.3 = (f32[256,128]{1,0:T(8,128)S(1)}, f32[256,128]{1,0:T(8,128)S(1)}, u32[]{:S(2)}, u32[]{:S(2)}) collective-permute-start(f32[256,128]{1,0:T(8,128)S(1)} %get-tuple-element.47), channel_id=1, source_target_pairs={{0,7},{1,2},{2,1},{3,4},{4,3},{5,6},{6,5},{7,0},{8,15},{9,10},{10,... | collective-permute-start | bytes 393224 | tf_op jit(solution)/shard_map/ppermute | solution.py:442
  9.2 1.6 %collective-permute-start = (f32[8,256]{1,0:T(8,128)S(1)}, f32[8,256]{1,0:T(8,128)S(1)}, u32[]{:S(2)}, u32[]{:S(2)}) collective-permute-start(f32[8,256]{1,0:T(8,128)S(1)} %get-tuple-element.44.order_ref), channel_id=1, source_target_pairs={{0,8},{8,0},{16,24},{24,16},{32,40},{40,32},{48,56},{56,48},{64,72... | collective-permute-start | bytes 24584 | tf_op jit(solution)/shard_map/ppermute | solution.py:441
  10.8 1.8 %shard_map.113 = (f32[32,8,256]{2,1,0:T(8,128)S(1)}, f32[256,256]{1,0:T(8,128)S(1)}, bf16[512,256]{1,0:T(8,128)(2,1)S(1)}, bf16[512,256]{1,0:T(8,128)(2,1)S(1)},...) custom-call(f32[8,256]{1,0:T(8,128)S(1)} %get-tuple-element.44.order_ref, f32[3,64,4,256]{3,2,1,0:T(4,128)} %cond_hbm.3, ...), custom_call_target="tpu_custom_call" | custom-call | bytes 1048576 | tf_op jit(solution)/shard_map/pallas_call | solution.py:423
  13.4 24.9 %all_to_all.30.field_ref.chunk_ref = f32[32,32,256]{2,1,0:T(8,128)S(1)} all-to-all(f32[32,32,256]{2,1,0:T(8,128)S(1)} %get-tuple-element.62), channel_id=1, replica_groups=mesh['gx'=32,'gy'=8] {'gx'}, dimensions={0} | all-to-all | bytes 2097152 | tf_op jit(solution)/shard_map/all_to_all | solution.py:447
  38.6 15.1 %all_to_all.31.parts_ref = f32[32,16,256]{2,1,0:T(8,128)S(1)} all-to-all(f32[32,16,256]{2,1,0:T(8,128)S(1)} %shard_map.115), channel_id=1, replica_groups=mesh['gx'=32,'gy'=8] {'gx'}, dimensions={0} | all-to-all | bytes 1048576 | tf_op jit(solution)/shard_map/all_to_all | solution.py:447
  53.7 4.7 %shard_map.116 = (f32[32,40,128]{2,1,0:T(8,128)}, f32[8,128]{1,0:T(8,128)S(1)}) custom-call(f32[32,16,256]{2,1,0:T(8,128)S(1)} %all_to_all.31.parts_ref, f32[64,64,256]{2,1,0:T(8,128)S(1)} %bitcast.1, bf16[512,512]{1,0:T(8,128)(2,1)S(1)} %copy-done.4, bf16[512,512]{1,0:T(8,128)(2,1)S(1)} %copy-done.3), custom_call_target="tpu_custom_call" | custom-call | flops 2000000000 | bytes 1048576 | tf_op jit(solution)/shard_map/pallas_call | solution.py:423
  58.4 5.1 %all-to-all-start.2 = ((f32[32,40,128]{2,1,0:T(8,128)}), f32[32,40,128]{2,1,0:T(8,128)S(1)}, u32[]{:S(2)}, u32[]{:S(2)}) async-start(f32[32,40,128]{2,1,0:T(8,128)} %get-tuple-element.65), calls=%async_computation.2 | async-start | bytes 1310720 | tf_op jit(solution)/shard_map/all_to_all | solution.py:447
  63.6 1.4 %collective-permute-start.5 = (f32[128,128]{1,0:T(8,128)S(1)}, f32[128,128]{1,0:T(8,128)S(1)}, u32[]{:S(2)}, u32[]{:S(2)}) collective-permute-start(f32[128,128]{1,0:T(8,128)S(1)} %get-tuple-element.67), channel_id=1, source_target_pairs={{0,7},{1,0},{2,1},{3,2},{4,3},{5,4},{6,5},{7,6},{8,15},{9,8},{10,9... | collective-permute-start | bytes 196616 | tf_op jit(solution)/shard_map/ppermute | solution.py:436
  65.0 6.5 %collective-permute-done.4.cond_next_ref = f32[32,256]{1,0:T(8,128)S(1)} collective-permute-done((f32[32,256]{1,0:T(8,128)S(1)}, f32[32,256]{1,0:T(8,128)S(1)}, u32[]{:S(2)}, u32[]{:S(2)}) %collective-permute-start.4) | collective-permute-done | bytes 32800 | tf_op jit(solution)/shard_map/ppermute | solution.py:436
  71.5 4.0 %all-to-all-done.2.parts_ref = f32[32,40,128]{2,1,0:T(8,128)S(1)} async-done(((f32[32,40,128]{2,1,0:T(8,128)}), f32[32,40,128]{2,1,0:T(8,128)S(1)}, u32[]{:S(2)}, u32[]{:S(2)}) %all-to-all-start.2) | async-done | bytes 655392 | tf_op jit(solution)/shard_map/all_to_all | solution.py:447
  76.1 3.2 %collective-permute-start.7 = (f32[128,128]{1,0:T(8,128)S(1)}, f32[128,128]{1,0:T(8,128)S(1)}, u32[]{:S(2)}, u32[]{:S(2)}) collective-permute-start(f32[128,128]{1,0:T(8,128)S(1)} %get-tuple-element.75), channel_id=1, source_target_pairs={{0,7},{1,0},{2,1},{3,2},{4,3},{5,4},{6,5},{7,6},{8,15},{9,8},{10,9... | collective-permute-start | bytes 196616 | tf_op jit(solution)/shard_map/ppermute | solution.py:436
  79.3 2.3 %collective-permute-done.6.under_ref = f32[128,128]{1,0:T(8,128)S(1)} collective-permute-done((f32[128,128]{1,0:T(8,128)S(1)}, f32[128,128]{1,0:T(8,128)S(1)}, u32[]{:S(2)}, u32[]{:S(2)}) %collective-permute-start.6) | collective-permute-done | bytes 65568 | tf_op jit(solution)/shard_map/ppermute | solution.py:436
  82.5 15.1 %all_to_all.32.parts_ref = f32[32,16,256]{2,1,0:T(8,128)S(1)} all-to-all(f32[32,16,256]{2,1,0:T(8,128)S(1)} %get-tuple-element.79), channel_id=1, replica_groups=mesh['gx'=32,'gy'=8] {'gx'}, dimensions={0} | all-to-all | bytes 1048576 | tf_op jit(solution)/shard_map/all_to_all | solution.py:447
  98.7 3.8 %shard_map.120 = f32[32,40,128]{2,1,0:T(8,128)S(1)} custom-call(f32[32,16,256]{2,1,0:T(8,128)S(1)} %all_to_all.32.parts_ref, f32[64,64,256]{2,1,0:T(8,128)S(1)} %bitcast.2, bf16[512,512]{1,0:T(8,128)(2,1)S(1)} %copy-done.5, bf16[512,512]{1,0:T(8,128)(2,1)S(1)} %copy-done.3, f32[8,128]{1,0:T(8,128)S(1)} %get-tuple-element.80.dots_ref), custom_call_target="tpu_custom_call" | custom-call | flops 2000000000 | bytes 1048576 | tf_op jit(solution)/shard_map/pallas_call | solution.py:423
  102.5 16.6 %all_to_all.33.parts_ref = f32[32,40,128]{2,1,0:T(8,128)S(1)} all-to-all(f32[32,40,128]{2,1,0:T(8,128)S(1)} %shard_map.120), channel_id=1, replica_groups=mesh['gx'=32,'gy'=8] {'gx'}, dimensions={0} | all-to-all | bytes 1310720 | tf_op jit(solution)/shard_map/all_to_all | solution.py:447
  119.1 1.3 shard_map.121
  120.4 5.1 %all-to-all-start.5 = ((f32[32,24,256]{2,1,0:T(8,128)}), f32[32,24,256]{2,1,0:T(8,128)S(1)}, u32[]{:S(2)}, u32[]{:S(2)}) async-start(f32[32,24,256]{2,1,0:T(8,128)} %get-tuple-element.82), calls=%async_computation.5 | async-start | bytes 1572864 | tf_op jit(solution)/shard_map/all_to_all | solution.py:447
  125.6 3.6 %collective-permute-done.8 = f32[8,128]{1,0:T(8,128)S(1)} collective-permute-done((f32[8,128]{1,0:T(8,128)S(1)}, f32[8,128]{1,0:T(8,128)S(1)}, u32[]{:S(2)}, u32[]{:S(2)}) %collective-permute-start.8) | collective-permute-done | bytes 4128 | tf_op jit(solution)/shard_map/ppermute | solution.py:453
  129.2 1.8 %collective-permute-start.9 = (f32[8,128]{1,0:T(8,128)S(1)}, f32[8,128]{1,0:T(8,128)S(1)}, u32[]{:S(2)}, u32[]{:S(2)}) collective-permute-start(f32[8,128]{1,0:T(8,128)S(1)} %add.9), channel_id=1, source_target_pairs={{0,2},{1,3},{2,0},{3,1},{4,6},{5,7},{6,4},{7,5},{8,10},{9,11},{10,... | collective-permute-start | bytes 12296 | tf_op jit(solution)/shard_map/ppermute | solution.py:453
  131.0 2.7 %collective-permute-done.9 = f32[8,128]{1,0:T(8,128)S(1)} collective-permute-done((f32[8,128]{1,0:T(8,128)S(1)}, f32[8,128]{1,0:T(8,128)S(1)}, u32[]{:S(2)}, u32[]{:S(2)}) %collective-permute-start.9) | collective-permute-done | bytes 4128 | tf_op jit(solution)/shard_map/ppermute | solution.py:453
  133.7 2.7 %collective-permute-start.10 = (f32[8,128]{1,0:T(8,128)S(1)}, f32[8,128]{1,0:T(8,128)S(1)}, u32[]{:S(2)}, u32[]{:S(2)}) collective-permute-start(f32[8,128]{1,0:T(8,128)S(1)} %add.10), channel_id=1, source_target_pairs={{0,6},{1,7},{2,4},{3,5},{4,2},{5,3},{6,0},{7,1},{8,14},{9,15},{10,... | collective-permute-start | bytes 12296 | tf_op jit(solution)/shard_map/ppermute | solution.py:453
  136.4 3.0 %collective-permute-done.10 = f32[8,128]{1,0:T(8,128)S(1)} collective-permute-done((f32[8,128]{1,0:T(8,128)S(1)}, f32[8,128]{1,0:T(8,128)S(1)}, u32[]{:S(2)}, u32[]{:S(2)}) %collective-permute-start.10) | collective-permute-done | bytes 4128 | tf_op jit(solution)/shard_map/ppermute | solution.py:453
  (32 shorter events, 5.1 us)
Async XLA Ops:
  2.2 10.4 %collective-permute-start.2 = (f32[256,128]{1,0:T(8,128)S(1)}, f32[256,128]{1,0:T(8,128)S(1)}, u32[]{:S(2)}, u32[]{:S(2)}) collective-permute-start(f32[256,128]{1,0:T(8,128)S(1)} %get-tuple-element.46), channel_id=1, source_target_pairs={{0,1},{1,0},{2,3},{3,2},{4,5},{5,4},{6,7},{7,6},{8,9},{9,8},{10,11... | collective-permute-start | bytes 393224 | tf_op jit(solution)/shard_map/ppermute | solution.py:441
  4.2 8.4 %collective-permute-start.3 = (f32[256,128]{1,0:T(8,128)S(1)}, f32[256,128]{1,0:T(8,128)S(1)}, u32[]{:S(2)}, u32[]{:S(2)}) collective-permute-start(f32[256,128]{1,0:T(8,128)S(1)} %get-tuple-element.47), channel_id=1, source_target_pairs={{0,7},{1,2},{2,1},{3,4},{4,3},{5,6},{6,5},{7,0},{8,15},{9,10},{10,... | collective-permute-start | bytes 393224 | tf_op jit(solution)/shard_map/ppermute | solution.py:442
  9.1 3.5 %collective-permute-start.1 = (f32[8,256]{1,0:T(8,128)S(1)}, f32[8,256]{1,0:T(8,128)S(1)}, u32[]{:S(2)}, u32[]{:S(2)}) collective-permute-start(f32[8,256]{1,0:T(8,128)S(1)} %get-tuple-element.45), channel_id=1, source_target_pairs={{0,248},{8,16},{16,8},{24,32},{32,24},{40,48},{48,40},{56,64},{64,... | collective-permute-start | bytes 24584 | tf_op jit(solution)/shard_map/ppermute | solution.py:442
  9.1 44.5 %copy-start.1 = (f32[1,64,64,256]{3,2,1,0:T(8,128)S(1)}, f32[1,64,64,256]{3,2,1,0:T(8,128)}, u32[]{:S(2)}) copy-start(f32[1,64,64,256]{3,2,1,0:T(8,128)} %param.12) | copy-start | bytes 12582916
  9.1 44.5 %copy-start.3 = (bf16[512,512]{1,0:T(8,128)(2,1)S(1)}, bf16[512,512]{1,0:T(8,128)(2,1)}, u32[]{:S(2)}) copy-start(bf16[512,512]{1,0:T(8,128)(2,1)} %constant.14.clone.low_ref) | copy-start | bytes 1572868
  9.1 44.5 %copy-start.4 = (bf16[512,512]{1,0:T(8,128)(2,1)S(1)}, bf16[512,512]{1,0:T(8,128)(2,1)}, u32[]{:S(2)}) copy-start(bf16[512,512]{1,0:T(8,128)(2,1)} %constant.13.clone.high_ref) | copy-start | bytes 1572868
  9.2 3.5 %collective-permute-start = (f32[8,256]{1,0:T(8,128)S(1)}, f32[8,256]{1,0:T(8,128)S(1)}, u32[]{:S(2)}, u32[]{:S(2)}) collective-permute-start(f32[8,256]{1,0:T(8,128)S(1)} %get-tuple-element.44.order_ref), channel_id=1, source_target_pairs={{0,8},{8,0},{16,24},{24,16},{32,40},{40,32},{48,56},{56,48},{64,72... | collective-permute-start | bytes 24584 | tf_op jit(solution)/shard_map/ppermute | solution.py:441
  58.4 17.1 %all-to-all-start.2 = ((f32[32,40,128]{2,1,0:T(8,128)}), f32[32,40,128]{2,1,0:T(8,128)S(1)}, u32[]{:S(2)}, u32[]{:S(2)}) async-start(f32[32,40,128]{2,1,0:T(8,128)} %get-tuple-element.65), calls=%async_computation.2 | async-start | bytes 1310720 | tf_op jit(solution)/shard_map/all_to_all | solution.py:447
  63.6 7.9 %collective-permute-start.5 = (f32[128,128]{1,0:T(8,128)S(1)}, f32[128,128]{1,0:T(8,128)S(1)}, u32[]{:S(2)}, u32[]{:S(2)}) collective-permute-start(f32[128,128]{1,0:T(8,128)S(1)} %get-tuple-element.67), channel_id=1, source_target_pairs={{0,7},{1,0},{2,1},{3,2},{4,3},{5,4},{6,5},{7,6},{8,15},{9,8},{10,9... | collective-permute-start | bytes 196616 | tf_op jit(solution)/shard_map/ppermute | solution.py:436
  65.0 6.5 %collective-permute-start.4 = (f32[32,256]{1,0:T(8,128)S(1)}, f32[32,256]{1,0:T(8,128)S(1)}, u32[]{:S(2)}, u32[]{:S(2)}) collective-permute-start(f32[32,256]{1,0:T(8,128)S(1)} %get-tuple-element.66), channel_id=1, source_target_pairs={{0,248},{8,0},{16,8},{24,16},{32,24},{40,32},{48,40},{56,48},{64,5... | collective-permute-start | bytes 98312 | tf_op jit(solution)/shard_map/ppermute | solution.py:436
  75.5 22.1 %copy-start.2 = (f32[1,64,64,256]{3,2,1,0:T(8,128)S(1)}, f32[1,64,64,256]{3,2,1,0:T(8,128)}, u32[]{:S(2)}) copy-start(f32[1,64,64,256]{3,2,1,0:T(8,128)} %param.12) | copy-start | bytes 12582916
  76.0 5.6 %collective-permute-start.6 = (f32[128,128]{1,0:T(8,128)S(1)}, f32[128,128]{1,0:T(8,128)S(1)}, u32[]{:S(2)}, u32[]{:S(2)}) collective-permute-start(f32[128,128]{1,0:T(8,128)S(1)} %get-tuple-element.74), channel_id=1, source_target_pairs={{0,1},{1,2},{2,3},{3,4},{4,5},{5,6},{6,7},{7,0},{8,9},{9,10},{10,1... | collective-permute-start | bytes 196616 | tf_op jit(solution)/shard_map/ppermute | solution.py:436
  76.1 5.5 %collective-permute-start.7 = (f32[128,128]{1,0:T(8,128)S(1)}, f32[128,128]{1,0:T(8,128)S(1)}, u32[]{:S(2)}, u32[]{:S(2)}) collective-permute-start(f32[128,128]{1,0:T(8,128)S(1)} %get-tuple-element.75), channel_id=1, source_target_pairs={{0,7},{1,0},{2,1},{3,2},{4,3},{5,4},{6,5},{7,6},{8,15},{9,8},{10,9... | collective-permute-start | bytes 196616 | tf_op jit(solution)/shard_map/ppermute | solution.py:436
  97.6 1.0 copy-start.5
  98.7 40.8 %copy-start = (f32[64,4,256]{2,1,0:T(4,128)S(1)}, f32[64,4,256]{2,1,0:T(4,128)}, u32[]{:S(2)}) copy-start(f32[64,4,256]{2,1,0:T(4,128)} %start_ref.1) | copy-start | bytes 786436
  120.4 19.1 %all-to-all-start.5 = ((f32[32,24,256]{2,1,0:T(8,128)}), f32[32,24,256]{2,1,0:T(8,128)S(1)}, u32[]{:S(2)}, u32[]{:S(2)}) async-start(f32[32,24,256]{2,1,0:T(8,128)} %get-tuple-element.82), calls=%async_computation.5 | async-start | bytes 1572864 | tf_op jit(solution)/shard_map/all_to_all | solution.py:447
  125.5 3.7 %collective-permute-start.8 = (f32[8,128]{1,0:T(8,128)S(1)}, f32[8,128]{1,0:T(8,128)S(1)}, u32[]{:S(2)}, u32[]{:S(2)}) collective-permute-start(f32[8,128]{1,0:T(8,128)S(1)} %get-tuple-element.84), channel_id=1, source_target_pairs={{0,1},{1,0},{2,3},{3,2},{4,5},{5,4},{6,7},{7,6},{8,9},{9,8},{10,11... | collective-permute-start | bytes 12296 | tf_op jit(solution)/shard_map/ppermute | solution.py:453
  129.2 4.5 %collective-permute-start.9 = (f32[8,128]{1,0:T(8,128)S(1)}, f32[8,128]{1,0:T(8,128)S(1)}, u32[]{:S(2)}, u32[]{:S(2)}) collective-permute-start(f32[8,128]{1,0:T(8,128)S(1)} %add.9), channel_id=1, source_target_pairs={{0,2},{1,3},{2,0},{3,1},{4,6},{5,7},{6,4},{7,5},{8,10},{9,11},{10,... | collective-permute-start | bytes 12296 | tf_op jit(solution)/shard_map/ppermute | solution.py:453
  133.7 5.7 %collective-permute-start.10 = (f32[8,128]{1,0:T(8,128)S(1)}, f32[8,128]{1,0:T(8,128)S(1)}, u32[]{:S(2)}, u32[]{:S(2)}) collective-permute-start(f32[8,128]{1,0:T(8,128)S(1)} %add.10), channel_id=1, source_target_pairs={{0,6},{1,7},{2,4},{3,5},{4,2},{5,3},{6,0},{7,1},{8,14},{9,15},{10,... | collective-permute-start | bytes 12296 | tf_op jit(solution)/shard_map/ppermute | solution.py:453

commit v6 on v5

--- a/solution.py
+++ b/solution.py
@@ -204,11 +204,10 @@
         along_ref[:, COLS * axis : COLS * (axis + 1), :] = along.reshape(GROUP, COLS, PLANE)
 
 
-def side_kernel(order_ref, cond_hbm, right_hbm, turns_hbm, column_hbm, edge_hbm, *refs):
-    along_out, right_out, high_ref, low_ref, edge_high_ref, edge_low_ref = refs[:6]
-    cond_ref, rhs_ref, turns_ref, column_ref, edge_ref, semaphores = refs[6:]
-    sources = (cond_hbm.at[2], right_hbm, turns_hbm.at[lax.axis_index("gx")], column_hbm, edge_hbm)
-    targets = (cond_ref, rhs_ref, turns_ref, column_ref, edge_ref)
+def side_kernel(order_ref, cond_hbm, right_hbm, turns_hbm, column_hbm, *refs):
+    along_out, right_out, high_ref, low_ref, cond_ref, rhs_ref, turns_ref, column_ref, semaphores = refs
+    sources = (cond_hbm.at[2], right_hbm, turns_hbm.at[lax.axis_index("gx")], column_hbm)
+    targets = (cond_ref, rhs_ref, turns_ref, column_ref)
     copies = [pltpu.make_async_copy(*pair, semaphores.at[i]) for i, pair in enumerate(zip(sources, targets))]
     for copy in copies:
         copy.start()
@@ -223,11 +222,6 @@
     blocks = table.reshape(GROUP, 2 * COLS, CELLS)
     other = jnp.concatenate([blocks[:, COLS:], -blocks[:, :COLS]], axis=1).reshape(2 * CELLS, CELLS)
     high_ref[...], low_ref[...] = split(table * turns[:, 0:1] + other * turns[:, 1:2])
-    copies[4].wait()
-    table = edge_ref[...]
-    part = lax.broadcasted_iota(jnp.int32, (CELLS, HALF), 0) % 2
-    other = jnp.where(part == 0, pltpu.roll(table, CELLS - 1, 0), -pltpu.roll(table, 1, 0))
-    edge_high_ref[...], edge_low_ref[...] = split(table * turns[:CELLS, 2:3] + other * turns[:CELLS, 3:4])
 
 
 def residual_kernel(
@@ -338,6 +332,15 @@
 
 def edge_rows(edge):
     return jnp.broadcast_to(edge[:, None, :], (GROUP, COLS, PLANE)).reshape(CELLS, PLANE)
+
+
+def table_kernel(order_ref, high_hbm, low_hbm, high_ref, low_ref, semaphores):
+    pairs = ((high_hbm, high_ref), (low_hbm, low_ref))
+    copies = [pltpu.make_async_copy(source, target, semaphores.at[i]) for i, (source, target) in enumerate(pairs)]
+    for copy in copies:
+        copy.start()
+    for copy in copies:
+        copy.wait()
 
 
 def image_kernel(
@@ -376,9 +379,22 @@
     sums_ref[...] = dots_ref[...] + jnp.where(row == 1, total, 0.0)
 
 
-def edges_kernel(chunk_ref, edge_ref, row_ref):
+def edges_kernel(
+    chunk_ref, turns_hbm, table_hbm, edge_ref, row_ref, high_ref, low_ref, turns_ref, table_ref, semaphores
+):
+    pairs = ((turns_hbm.at[lax.axis_index("gx")], turns_ref), (table_hbm, table_ref))
+    copies = [pltpu.make_async_copy(source, target, semaphores.at[i]) for i, (source, target) in enumerate(pairs)]
+    for copy in copies:
+        copy.start()
     edge_ref[...] = chunk_ref[:, 0, :]
     row_ref[...] = low_row_packed(chunk_ref[:, COLS : 2 * COLS, :].reshape(CELLS, PLANE))
+    for copy in copies:
+        copy.wait()
+    turns = turns_ref[...].T
+    table = table_ref[...]
+    part = lax.broadcasted_iota(jnp.int32, (CELLS, HALF), 0) % 2
+    other = jnp.where(part == 0, pltpu.roll(table, CELLS - 1, 0), -pltpu.roll(table, 1, 0))
+    high_ref[...], low_ref[...] = split(table * turns[:CELLS, 2:3] + other * turns[:CELLS, 3:4])
 
 
 def pack_kernel(parts_ref, high_ref, low_ref, field_ref, image_ref, out_ref, sums_ref):
@@ -481,29 +497,25 @@
         ],
     )
     halos = swap(swaps[0], swaps[1], "gx") + swap(swaps[2], swaps[3], "gy")
-    along_z, turned_right, *tables = call(
+    turn_angles = jnp.asarray(turn_table())
+    along_z, turned_right, *table = call(
         side_kernel,
-        [shape(GROUP, COLS, PLANE), field_shape]
-        + [shape(2 * CELLS, CELLS, dtype=bf16)] * 2
-        + [shape(CELLS, HALF, dtype=bf16)] * 2,
+        [shape(GROUP, COLS, PLANE), field_shape] + [shape(2 * CELLS, CELLS, dtype=bf16)] * 2,
         swaps[0],
         conductance,
         right_side,
-        jnp.asarray(turn_table()),
+        turn_angles,
         jnp.asarray(column_table()),
-        jnp.asarray(edge_table()),
-        hbm=(1, 2, 3, 4, 5),
+        hbm=(1, 2, 3, 4),
         scratch=[
             pltpu.VMEM((NZ, ROWS, CELLS), f32),
             pltpu.VMEM((NZ, ROWS, CELLS), f32),
             pltpu.VMEM((8, 2 * CELLS), f32),
             pltpu.VMEM((2 * CELLS, CELLS), f32),
-            pltpu.VMEM((CELLS, HALF), f32),
-            pltpu.SemaphoreType.DMA((5,)),
+            pltpu.SemaphoreType.DMA((4,)),
         ],
     )
-    halos, along_z, turned_right, tables = lax.optimization_barrier((halos, along_z, turned_right, tables))
-    table, beside_table = tables[:2], tables[2:]
+    halos, along_z, turned_right, table = lax.optimization_barrier((halos, along_z, turned_right, table))
     chunk, residual = call(
         residual_kernel,
         [shape(GROUP, 4 * COLS, PLANE), field_shape],
@@ -518,7 +530,19 @@
     inverse = inverses.reshape(inverses.shape[1:])
 
     parts = exchange(call(spread_kernel, parts_shape, chunk, *table))
-    cond_edge, cond_row = call(edges_kernel, [edge_shape, row_shape], chunk)
+    cond_edge, cond_row, *beside_table = call(
+        edges_kernel,
+        [edge_shape, row_shape] + [shape(CELLS, HALF, dtype=bf16)] * 2,
+        chunk,
+        turn_angles,
+        jnp.asarray(edge_table()),
+        hbm=(1, 2),
+        scratch=[
+            pltpu.VMEM((8, 2 * CELLS), f32),
+            pltpu.VMEM((CELLS, HALF), f32),
+            pltpu.SemaphoreType.DMA((2,)),
+        ],
+    )
     cond_after = shift(cond_edge, "gx", -1)
     cond_over = shift(cond_row, "gy", -1)
     wave_shape = pltpu.VMEM((PLANE, 2 * CELLS), f32)
@@ -541,6 +565,15 @@
     )
     under = shift(row_high, "gy", 1)
     over = shift(row_low, "gy", -1)
+    tables = call(
+        table_kernel,
+        [shape(2 * CELLS, 2 * CELLS, dtype=bf16)] * 2,
+        row_low,
+        *waves,
+        hbm=(1, 2),
+        scratch=[pltpu.SemaphoreType.DMA((2,))],
+    )
+    under, over, tables = lax.optimization_barrier((under, over, tables))
     image, parts, dots = call(
         image_kernel,
         [field_shape, parts_shape, dots_shape],
@@ -560,7 +593,7 @@
         wide_shape,
         exchange(parts),
         inverse,
-        *waves,
+        *tables,
         dots,
         scratch=[wave_shape, wave_shape, pltpu.VMEM((8, HALF), f32)],
         cost=2 * 10**9,

time: 143 us -> 142 us (level)
  waiting for transfers between devices: 22.2 us -> 19.8 us
  Pallas kernels: 17.1 us -> 19.3 us
    ppermute x4, waiting for transfers between devices: 8.8 us -> 6.41 us  [shift(): lax.ppermute(value, axis, [(i, (i + step) % count) for i in range(count)])]
    pallas_call x11 -> x12, Pallas kernels: 17.1 us -> 19.3 us  [call(): pl.pallas_call(kernel, out_shape=outs, in_specs=specs, out_specs=[out_spe...]
  transfers between devices with their start and end apart: 13 -> 13, of which waited for: 6 -> 6; matrix products, arithmetic and copies ran while one was open for 0% -> 0% of each run, Pallas kernels for 1% -> 3%
where the time goes in v6:
time: 142 us; the launch traced here: 140 us
  blocking collectives  71.8 us (51%)
  starting transfers between devices  28 us (20%)
  waiting for transfers between devices  19.8 us (14%)
  Pallas kernels  19.3 us (14%)
    all_to_all x4, blocking collectives, exchange(): return lax.all_to_all(parts, 'gx', 0, 0, tiled=True)  71.8 us
    pallas_call x12, Pallas kernels, call(): pl.pallas_call(kernel, out_shape=outs, in_specs=specs, out_specs=[out_spe...  19.3 us
    all_to_all x2, starting transfers between devices, exchange(): return lax.all_to_all(parts, 'gx', 0, 0, tiled=True)  10.2 us
    ppermute x3, waiting for transfers between devices, sum_rows(): lax.ppermute(value, 'gy', [(i, i ^ mask) for i in range(count)])  9.37 us
    ppermute x4, waiting for transfers between devices, shift(): lax.ppermute(value, axis, [(i, (i + step) % count) for i in range(count)])  6.41 us
    ppermute x2, starting transfers between devices, swap(): lax.ppermute(second, axis, [(i, (i + 2 * (i % 2) - 1) % count) for i in r...  4.95 us
    ppermute x4, starting transfers between devices, shift(): lax.ppermute(value, axis, [(i, (i + step) % count) for i in range(count)])  4.71 us
    ppermute x3, starting transfers between devices, sum_rows(): lax.ppermute(value, 'gy', [(i, i ^ mask) for i in range(count)])  4.54 us
  transfers between devices with their start and end apart: 13, of which 6 were waited for; matrix products, arithmetic and copies ran while one was open for 0% of the time, Pallas kernels for 3%

profile of v6, /device:TPU:2, one launch (start us, length us, event | category | flops | bytes accessed | tf_op | source)
XLA Modules:
  0.0 139.7 jit_solution(7084233350387683077)
XLA Ops:
  0.6 1.6 %shard_map.112 = (f32[256,256]{1,0:T(8,128)S(1)}, f32[32,16,256]{2,1,0:T(8,128)S(1)}, f32[8,256]{1,0:T(8,128)S(1)}, f32[8,256]{1,0:T(8,128)S(1)}, f32[256,128]{1,0:T(8,128)S(1)}, /*index=5*/f32[256,128]{1,0:T(8,128)S(1)}) custom-call(f32[64,4,256]{2,1,0:T(4,128)} %start_ref.1, f32[3,64,4,256]{3,2,1,0:T(4,128)} %cond_hbm.3), custom_call_target="tpu_custom_call" | custom-call | bytes 1048576 | tf_op jit(solution)/shard_map/pallas_call | solution.py:439
  2.2 2.0 %collective-permute-start.2 = (f32[256,128]{1,0:T(8,128)S(1)}, f32[256,128]{1,0:T(8,128)S(1)}, u32[]{:S(2)}, u32[]{:S(2)}) collective-permute-start(f32[256,128]{1,0:T(8,128)S(1)} %get-tuple-element.50), channel_id=1, source_target_pairs={{0,1},{1,0},{2,3},{3,2},{4,5},{5,4},{6,7},{7,6},{8,9},{9,8},{10,11... | collective-permute-start | bytes 393224 | tf_op jit(solution)/shard_map/ppermute | solution.py:457
  4.2 4.9 %collective-permute-start.3 = (f32[256,128]{1,0:T(8,128)S(1)}, f32[256,128]{1,0:T(8,128)S(1)}, u32[]{:S(2)}, u32[]{:S(2)}) collective-permute-start(f32[256,128]{1,0:T(8,128)S(1)} %get-tuple-element.51), channel_id=1, source_target_pairs={{0,7},{1,2},{2,1},{3,4},{4,3},{5,6},{6,5},{7,0},{8,15},{9,10},{10,... | collective-permute-start | bytes 393224 | tf_op jit(solution)/shard_map/ppermute | solution.py:458
  9.2 1.6 %collective-permute-start = (f32[8,256]{1,0:T(8,128)S(1)}, f32[8,256]{1,0:T(8,128)S(1)}, u32[]{:S(2)}, u32[]{:S(2)}) collective-permute-start(f32[8,256]{1,0:T(8,128)S(1)} %get-tuple-element.48.order_ref), channel_id=1, source_target_pairs={{0,8},{8,0},{16,24},{24,16},{32,40},{40,32},{48,56},{56,48},{64,72... | collective-permute-start | bytes 24584 | tf_op jit(solution)/shard_map/ppermute | solution.py:457
  10.8 1.7 %shard_map.113 = (f32[32,8,256]{2,1,0:T(8,128)S(1)}, f32[256,256]{1,0:T(8,128)S(1)}, bf16[512,256]{1,0:T(8,128)(2,1)S(1)}, bf16[512,256]{1,0:T(8,128)(2,1)S(1)}) custom-call(f32[8,256]{1,0:T(8,128)S(1)} %get-tuple-element.48.order_ref, f32[3,64,4,256]{3,2,1,0:T(4,128)} %cond_hbm.3, f32[64,4,256]{2,1,0:T(4,128)} %right_hbm.1, ...), custom_call_target="tpu_custom_call" | custom-call | bytes 1048576 | tf_op jit(solution)/shard_map/pallas_call | solution.py:439
  13.2 25.0 %all_to_all.30.field_ref.chunk_ref = f32[32,32,256]{2,1,0:T(8,128)S(1)} all-to-all(f32[32,32,256]{2,1,0:T(8,128)S(1)} %get-tuple-element.64), channel_id=1, replica_groups=mesh['gx'=32,'gy'=8] {'gx'}, dimensions={0} | all-to-all | bytes 2097152 | tf_op jit(solution)/shard_map/all_to_all | solution.py:463
  38.6 15.1 %all_to_all.31.parts_ref = f32[32,16,256]{2,1,0:T(8,128)S(1)} all-to-all(f32[32,16,256]{2,1,0:T(8,128)S(1)} %shard_map.115), channel_id=1, replica_groups=mesh['gx'=32,'gy'=8] {'gx'}, dimensions={0} | all-to-all | bytes 1048576 | tf_op jit(solution)/shard_map/all_to_all | solution.py:463
  53.7 4.7 %shard_map.116 = (f32[32,40,128]{2,1,0:T(8,128)}, f32[8,128]{1,0:T(8,128)S(1)}) custom-call(f32[32,16,256]{2,1,0:T(8,128)S(1)} %all_to_all.31.parts_ref, f32[64,64,256]{2,1,0:T(8,128)S(1)} %bitcast.1, bf16[512,512]{1,0:T(8,128)(2,1)S(1)} %copy-done.2, bf16[512,512]{1,0:T(8,128)(2,1)S(1)} %copy-done.1), custom_call_target="tpu_custom_call" | custom-call | flops 2000000000 | bytes 1048576 | tf_op jit(solution)/shard_map/pallas_call | solution.py:439
  58.4 5.1 %all-to-all-start.2 = ((f32[32,40,128]{2,1,0:T(8,128)}), f32[32,40,128]{2,1,0:T(8,128)S(1)}, u32[]{:S(2)}, u32[]{:S(2)}) async-start(f32[32,40,128]{2,1,0:T(8,128)} %get-tuple-element.67), calls=%async_computation.2 | async-start | bytes 1310720 | tf_op jit(solution)/shard_map/all_to_all | solution.py:463
  64.8 1.4 %collective-permute-start.5 = (f32[128,128]{1,0:T(8,128)S(1)}, f32[128,128]{1,0:T(8,128)S(1)}, u32[]{:S(2)}, u32[]{:S(2)}) collective-permute-start(f32[128,128]{1,0:T(8,128)S(1)} %get-tuple-element.69), channel_id=1, source_target_pairs={{0,7},{1,0},{2,1},{3,2},{4,3},{5,4},{6,5},{7,6},{8,15},{9,8},{10,9... | collective-permute-start | bytes 196616 | tf_op jit(solution)/shard_map/ppermute | solution.py:452
  66.2 5.3 %collective-permute-done.4.cond_next_ref = f32[32,256]{1,0:T(8,128)S(1)} collective-permute-done((f32[32,256]{1,0:T(8,128)S(1)}, f32[32,256]{1,0:T(8,128)S(1)}, u32[]{:S(2)}, u32[]{:S(2)}) %collective-permute-start.4) | collective-permute-done | bytes 32800 | tf_op jit(solution)/shard_map/ppermute | solution.py:452
  71.5 4.0 %all-to-all-done.2.parts_ref = f32[32,40,128]{2,1,0:T(8,128)S(1)} async-done(((f32[32,40,128]{2,1,0:T(8,128)}), f32[32,40,128]{2,1,0:T(8,128)S(1)}, u32[]{:S(2)}, u32[]{:S(2)}) %all-to-all-start.2) | async-done | bytes 655392 | tf_op jit(solution)/shard_map/all_to_all | solution.py:463
  76.1 3.2 %collective-permute-start.7 = (f32[128,128]{1,0:T(8,128)S(1)}, f32[128,128]{1,0:T(8,128)S(1)}, u32[]{:S(2)}, u32[]{:S(2)}) collective-permute-start(f32[128,128]{1,0:T(8,128)S(1)} %get-tuple-element.77.order_ref), channel_id=1, source_target_pairs={{0,7},{1,0},{2,1},{3,2},{4,3},{5,4},{6,5},{7,6},{8,15},{9,8},{10,9... | collective-permute-start | bytes 196616 | tf_op jit(solution)/shard_map/ppermute | solution.py:452
  82.5 15.1 %all_to_all.32.parts_ref = f32[32,16,256]{2,1,0:T(8,128)S(1)} all-to-all(f32[32,16,256]{2,1,0:T(8,128)S(1)} %get-tuple-element.85), channel_id=1, replica_groups=mesh['gx'=32,'gy'=8] {'gx'}, dimensions={0} | all-to-all | bytes 1048576 | tf_op jit(solution)/shard_map/all_to_all | solution.py:463
  97.6 3.8 %shard_map.121 = f32[32,40,128]{2,1,0:T(8,128)S(1)} custom-call(f32[32,16,256]{2,1,0:T(8,128)S(1)} %all_to_all.32.parts_ref, f32[64,64,256]{2,1,0:T(8,128)S(1)} %bitcast.2, bf16[512,512]{1,0:T(8,128)(2,1)S(1)} %get-tuple-element.86.high_ref, bf16[512,512]{1,0:T(8,128)(2,1)S(1)} %get-tuple-element.87.low_ref, f32[8,128]{1,0:T(8,128)S(1)} %get-tuple-element.88.dots_ref), custom_call_target="tpu_custom_call" | custom-call | flops 2000000000 | bytes 1048576 | tf_op jit(solution)/shard_map/pallas_call | solution.py:439
  101.4 16.6 %all_to_all.33.parts_ref = f32[32,40,128]{2,1,0:T(8,128)S(1)} all-to-all(f32[32,40,128]{2,1,0:T(8,128)S(1)} %shard_map.121), channel_id=1, replica_groups=mesh['gx'=32,'gy'=8] {'gx'}, dimensions={0} | all-to-all | bytes 1310720 | tf_op jit(solution)/shard_map/all_to_all | solution.py:463
  118.0 1.3 shard_map.122
  119.4 5.1 %all-to-all-start.5 = ((f32[32,24,256]{2,1,0:T(8,128)}), f32[32,24,256]{2,1,0:T(8,128)S(1)}, u32[]{:S(2)}, u32[]{:S(2)}) async-start(f32[32,24,256]{2,1,0:T(8,128)} %get-tuple-element.90), calls=%async_computation.5 | async-start | bytes 1572864 | tf_op jit(solution)/shard_map/all_to_all | solution.py:463
  124.6 3.6 %collective-permute-done.8 = f32[8,128]{1,0:T(8,128)S(1)} collective-permute-done((f32[8,128]{1,0:T(8,128)S(1)}, f32[8,128]{1,0:T(8,128)S(1)}, u32[]{:S(2)}, u32[]{:S(2)}) %collective-permute-start.8) | collective-permute-done | bytes 4128 | tf_op jit(solution)/shard_map/ppermute | solution.py:469
  128.2 1.8 %collective-permute-start.9 = (f32[8,128]{1,0:T(8,128)S(1)}, f32[8,128]{1,0:T(8,128)S(1)}, u32[]{:S(2)}, u32[]{:S(2)}) collective-permute-start(f32[8,128]{1,0:T(8,128)S(1)} %add.9), channel_id=1, source_target_pairs={{0,2},{1,3},{2,0},{3,1},{4,6},{5,7},{6,4},{7,5},{8,10},{9,11},{10,... | collective-permute-start | bytes 12296 | tf_op jit(solution)/shard_map/ppermute | solution.py:469
  130.0 2.7 %collective-permute-done.9 = f32[8,128]{1,0:T(8,128)S(1)} collective-permute-done((f32[8,128]{1,0:T(8,128)S(1)}, f32[8,128]{1,0:T(8,128)S(1)}, u32[]{:S(2)}, u32[]{:S(2)}) %collective-permute-start.9) | collective-permute-done | bytes 4128 | tf_op jit(solution)/shard_map/ppermute | solution.py:469
  132.7 2.7 %collective-permute-start.10 = (f32[8,128]{1,0:T(8,128)S(1)}, f32[8,128]{1,0:T(8,128)S(1)}, u32[]{:S(2)}, u32[]{:S(2)}) collective-permute-start(f32[8,128]{1,0:T(8,128)S(1)} %add.10), channel_id=1, source_target_pairs={{0,6},{1,7},{2,4},{3,5},{4,2},{5,3},{6,0},{7,1},{8,14},{9,15},{10,... | collective-permute-start | bytes 12296 | tf_op jit(solution)/shard_map/ppermute | solution.py:469
  135.4 3.0 %collective-permute-done.10 = f32[8,128]{1,0:T(8,128)S(1)} collective-permute-done((f32[8,128]{1,0:T(8,128)S(1)}, f32[8,128]{1,0:T(8,128)S(1)}, u32[]{:S(2)}, u32[]{:S(2)}) %collective-permute-start.10) | collective-permute-done | bytes 4128 | tf_op jit(solution)/shard_map/ppermute | solution.py:469
  138.4 1.3 shard_map.123
  (31 shorter events, 6.2 us)
Async XLA Ops:
  2.2 10.3 %collective-permute-start.2 = (f32[256,128]{1,0:T(8,128)S(1)}, f32[256,128]{1,0:T(8,128)S(1)}, u32[]{:S(2)}, u32[]{:S(2)}) collective-permute-start(f32[256,128]{1,0:T(8,128)S(1)} %get-tuple-element.50), channel_id=1, source_target_pairs={{0,1},{1,0},{2,3},{3,2},{4,5},{5,4},{6,7},{7,6},{8,9},{9,8},{10,11... | collective-permute-start | bytes 393224 | tf_op jit(solution)/shard_map/ppermute | solution.py:457
  4.2 8.3 %collective-permute-start.3 = (f32[256,128]{1,0:T(8,128)S(1)}, f32[256,128]{1,0:T(8,128)S(1)}, u32[]{:S(2)}, u32[]{:S(2)}) collective-permute-start(f32[256,128]{1,0:T(8,128)S(1)} %get-tuple-element.51), channel_id=1, source_target_pairs={{0,7},{1,2},{2,1},{3,4},{4,3},{5,6},{6,5},{7,0},{8,15},{9,10},{10,... | collective-permute-start | bytes 393224 | tf_op jit(solution)/shard_map/ppermute | solution.py:458
  9.1 3.3 %collective-permute-start.1 = (f32[8,256]{1,0:T(8,128)S(1)}, f32[8,256]{1,0:T(8,128)S(1)}, u32[]{:S(2)}, u32[]{:S(2)}) collective-permute-start(f32[8,256]{1,0:T(8,128)S(1)} %get-tuple-element.49), channel_id=1, source_target_pairs={{0,248},{8,16},{16,8},{24,32},{32,24},{40,48},{48,40},{56,64},{64,... | collective-permute-start | bytes 24584 | tf_op jit(solution)/shard_map/ppermute | solution.py:458
  9.1 44.5 %copy-start.1 = (bf16[512,512]{1,0:T(8,128)(2,1)S(1)}, bf16[512,512]{1,0:T(8,128)(2,1)}, u32[]{:S(2)}) copy-start(bf16[512,512]{1,0:T(8,128)(2,1)} %constant.13.clone.low_ref.low_hbm) | copy-start | bytes 1572868
  9.1 44.5 %copy-start.2 = (bf16[512,512]{1,0:T(8,128)(2,1)S(1)}, bf16[512,512]{1,0:T(8,128)(2,1)}, u32[]{:S(2)}) copy-start(bf16[512,512]{1,0:T(8,128)(2,1)} %constant.12.clone.high_ref.high_hbm) | copy-start | bytes 1572868
  9.1 44.5 %copy-start.3 = (f32[1,64,64,256]{3,2,1,0:T(8,128)S(1)}, f32[1,64,64,256]{3,2,1,0:T(8,128)}, u32[]{:S(2)}) copy-start(f32[1,64,64,256]{3,2,1,0:T(8,128)} %param.12) | copy-start | bytes 12582916
  9.2 3.3 %collective-permute-start = (f32[8,256]{1,0:T(8,128)S(1)}, f32[8,256]{1,0:T(8,128)S(1)}, u32[]{:S(2)}, u32[]{:S(2)}) collective-permute-start(f32[8,256]{1,0:T(8,128)S(1)} %get-tuple-element.48.order_ref), channel_id=1, source_target_pairs={{0,8},{8,0},{16,24},{24,16},{32,40},{40,32},{48,56},{56,48},{64,72... | collective-permute-start | bytes 24584 | tf_op jit(solution)/shard_map/ppermute | solution.py:457
  58.4 17.1 %all-to-all-start.2 = ((f32[32,40,128]{2,1,0:T(8,128)}), f32[32,40,128]{2,1,0:T(8,128)S(1)}, u32[]{:S(2)}, u32[]{:S(2)}) async-start(f32[32,40,128]{2,1,0:T(8,128)} %get-tuple-element.67), calls=%async_computation.2 | async-start | bytes 1310720 | tf_op jit(solution)/shard_map/all_to_all | solution.py:463
  64.8 6.7 %collective-permute-start.5 = (f32[128,128]{1,0:T(8,128)S(1)}, f32[128,128]{1,0:T(8,128)S(1)}, u32[]{:S(2)}, u32[]{:S(2)}) collective-permute-start(f32[128,128]{1,0:T(8,128)S(1)} %get-tuple-element.69), channel_id=1, source_target_pairs={{0,7},{1,0},{2,1},{3,2},{4,3},{5,4},{6,5},{7,6},{8,15},{9,8},{10,9... | collective-permute-start | bytes 196616 | tf_op jit(solution)/shard_map/ppermute | solution.py:452
  66.2 5.3 %collective-permute-start.4 = (f32[32,256]{1,0:T(8,128)S(1)}, f32[32,256]{1,0:T(8,128)S(1)}, u32[]{:S(2)}, u32[]{:S(2)}) collective-permute-start(f32[32,256]{1,0:T(8,128)S(1)} %get-tuple-element.68), channel_id=1, source_target_pairs={{0,248},{8,0},{16,8},{24,16},{32,24},{40,32},{48,40},{56,48},{64,5... | collective-permute-start | bytes 98312 | tf_op jit(solution)/shard_map/ppermute | solution.py:452
  75.5 22.1 %copy-start.4 = (f32[1,64,64,256]{3,2,1,0:T(8,128)S(1)}, f32[1,64,64,256]{3,2,1,0:T(8,128)}, u32[]{:S(2)}) copy-start(f32[1,64,64,256]{3,2,1,0:T(8,128)} %param.12) | copy-start | bytes 12582916
  76.0 5.6 %collective-permute-start.6 = (f32[128,128]{1,0:T(8,128)S(1)}, f32[128,128]{1,0:T(8,128)S(1)}, u32[]{:S(2)}, u32[]{:S(2)}) collective-permute-start(f32[128,128]{1,0:T(8,128)S(1)} %get-tuple-element.76), channel_id=1, source_target_pairs={{0,1},{1,2},{2,3},{3,4},{4,5},{5,6},{6,7},{7,0},{8,9},{9,10},{10,1... | collective-permute-start | bytes 196616 | tf_op jit(solution)/shard_map/ppermute | solution.py:452
  76.1 5.5 %collective-permute-start.7 = (f32[128,128]{1,0:T(8,128)S(1)}, f32[128,128]{1,0:T(8,128)S(1)}, u32[]{:S(2)}, u32[]{:S(2)}) collective-permute-start(f32[128,128]{1,0:T(8,128)S(1)} %get-tuple-element.77.order_ref), channel_id=1, source_target_pairs={{0,7},{1,0},{2,1},{3,2},{4,3},{5,4},{6,5},{7,6},{8,15},{9,8},{10,9... | collective-permute-start | bytes 196616 | tf_op jit(solution)/shard_map/ppermute | solution.py:452
  97.6 40.8 %copy-start = (f32[64,4,256]{2,1,0:T(4,128)S(1)}, f32[64,4,256]{2,1,0:T(4,128)}, u32[]{:S(2)}) copy-start(f32[64,4,256]{2,1,0:T(4,128)} %start_ref.1) | copy-start | bytes 786436
  119.4 19.1 %all-to-all-start.5 = ((f32[32,24,256]{2,1,0:T(8,128)}), f32[32,24,256]{2,1,0:T(8,128)S(1)}, u32[]{:S(2)}, u32[]{:S(2)}) async-start(f32[32,24,256]{2,1,0:T(8,128)} %get-tuple-element.90), calls=%async_computation.5 | async-start | bytes 1572864 | tf_op jit(solution)/shard_map/all_to_all | solution.py:463
  124.5 3.7 %collective-permute-start.8 = (f32[8,128]{1,0:T(8,128)S(1)}, f32[8,128]{1,0:T(8,128)S(1)}, u32[]{:S(2)}, u32[]{:S(2)}) collective-permute-start(f32[8,128]{1,0:T(8,128)S(1)} %get-tuple-element.92), channel_id=1, source_target_pairs={{0,1},{1,0},{2,3},{3,2},{4,5},{5,4},{6,7},{7,6},{8,9},{9,8},{10,11... | collective-permute-start | bytes 12296 | tf_op jit(solution)/shard_map/ppermute | solution.py:469
  128.2 4.5 %collective-permute-start.9 = (f32[8,128]{1,0:T(8,128)S(1)}, f32[8,128]{1,0:T(8,128)S(1)}, u32[]{:S(2)}, u32[]{:S(2)}) collective-permute-start(f32[8,128]{1,0:T(8,128)S(1)} %add.9), channel_id=1, source_target_pairs={{0,2},{1,3},{2,0},{3,1},{4,6},{5,7},{6,4},{7,5},{8,10},{9,11},{10,... | collective-permute-start | bytes 12296 | tf_op jit(solution)/shard_map/ppermute | solution.py:469
  132.7 5.7 %collective-permute-start.10 = (f32[8,128]{1,0:T(8,128)S(1)}, f32[8,128]{1,0:T(8,128)S(1)}, u32[]{:S(2)}, u32[]{:S(2)}) collective-permute-start(f32[8,128]{1,0:T(8,128)S(1)} %add.10), channel_id=1, source_target_pairs={{0,6},{1,7},{2,4},{3,5},{4,2},{5,3},{6,0},{7,1},{8,14},{9,15},{10,... | collective-permute-start | bytes 12296 | tf_op jit(solution)/shard_map/ppermute | solution.py:469

commit v7 on v6

--- a/solution.py
+++ b/solution.py
@@ -170,7 +170,6 @@
     start_hbm,
     cond_hbm,
     field_ref,
-    along_ref,
     x_first_ref,
     x_second_ref,
     y_first_ref,
@@ -187,32 +186,30 @@
     field = turned(start_ref)
     field_ref[...] = field
     high, low = high_row_packed(field), low_row_packed(field)
-    for axis in range(2):
-        copies[1 + axis].wait()
-        along = turned(cond_ref, (axis,))
-        if axis == 0:
-            left = jnp.concatenate([field[0:1], along[0:1]], axis=0)
-            right = jnp.concatenate([field[CELLS - 1 :], along[0:1]], axis=0)
-            x_first_ref[0:2] = from_below("gx", left, right)
-            x_second_ref[0:2] = from_below("gx", right, left)
-        else:
-            along_low = low_row_packed(along)
-            y_first_ref[:HALF] = from_below("gy", low, high)
-            y_second_ref[:HALF] = from_below("gy", high, low)
-            y_first_ref[HALF:] = along_low
-            y_second_ref[HALF:] = along_low
-        along_ref[:, COLS * axis : COLS * (axis + 1), :] = along.reshape(GROUP, COLS, PLANE)
+    copies[1].wait()
+    column = jnp.concatenate([cond_ref[0, :, y, :HALF] for y in range(ROWS)], axis=0).T[0:1]
+    left = jnp.concatenate([field[0:1], column], axis=0)
+    right = jnp.concatenate([field[CELLS - 1 :], column], axis=0)
+    x_first_ref[0:2] = from_below("gx", left, right)
+    x_second_ref[0:2] = from_below("gx", right, left)
+    copies[2].wait()
+    along_low = jnp.concatenate([cond_ref[1, :, 0, :HALF], cond_ref[1, :, 0, HALF:]], axis=0).T
+    y_first_ref[:HALF] = from_below("gy", low, high)
+    y_second_ref[:HALF] = from_below("gy", high, low)
+    y_first_ref[HALF:] = along_low
+    y_second_ref[HALF:] = along_low
 
 
 def side_kernel(order_ref, cond_hbm, right_hbm, turns_hbm, column_hbm, *refs):
     along_out, right_out, high_ref, low_ref, cond_ref, rhs_ref, turns_ref, column_ref, semaphores = refs
-    sources = (cond_hbm.at[2], right_hbm, turns_hbm.at[lax.axis_index("gx")], column_hbm)
+    sources = (cond_hbm, right_hbm, turns_hbm.at[lax.axis_index("gx")], column_hbm)
     targets = (cond_ref, rhs_ref, turns_ref, column_ref)
     copies = [pltpu.make_async_copy(*pair, semaphores.at[i]) for i, pair in enumerate(zip(sources, targets))]
     for copy in copies:
         copy.start()
     copies[0].wait()
-    along_out[...] = turned(cond_ref).reshape(GROUP, COLS, PLANE)
+    for axis in range(3):
+        along_out[:, COLS * axis : COLS * (axis + 1), :] = turned(cond_ref, (axis,)).reshape(GROUP, COLS, PLANE)
     copies[1].wait()
     right_out[...] = turned(rhs_ref)
     copies[2].wait()
@@ -225,15 +222,14 @@
 
 
 def residual_kernel(
-    rhs_ref, field_ref, along_ref, along_z_ref, x_first_ref, x_second_ref, y_first_ref, y_second_ref, *outs
+    rhs_ref, field_ref, along_ref, x_first_ref, x_second_ref, y_first_ref, y_second_ref, *outs
 ):
     out_ref, residual_ref = outs
     x_swaps, y_swaps = (x_first_ref[...], x_second_ref[...]), (y_first_ref[...], y_second_ref[...])
     left, after = from_below("gx", *x_swaps), from_below("gx", *x_swaps[::-1])
     under, over = from_below("gy", *y_swaps), from_below("gy", *y_swaps[::-1])
     field = field_ref[...]
-    along = [along_ref[:, COLS * axis : COLS * (axis + 1), :].reshape(CELLS, PLANE) for axis in range(2)]
-    along += [along_z_ref[...].reshape(CELLS, PLANE)]
+    along = coefficients(along_ref)
     row = lax.broadcasted_iota(jnp.int32, (CELLS, PLANE), 0)
     behind_x = jnp.where(row == 0, left[0:1], pltpu.roll(field, 1, 0))
     before_x = jnp.where(row == CELLS - 1, after[0:1], pltpu.roll(field, CELLS - 1, 0))
@@ -244,8 +240,7 @@
     image = operate(field, (behind_x, before_x), y_pair, along, ahead_x, ahead_y)
     residual = rhs_ref[...] - image
     residual_ref[...] = residual
-    out_ref[:, 0 : 2 * COLS, :] = along_ref[...]
-    out_ref[:, 2 * COLS : 3 * COLS, :] = along_z_ref[...]
+    out_ref[:, : 3 * COLS, :] = along_ref[...]
     out_ref[:, 3 * COLS :, :] = residual.reshape(GROUP, COLS, PLANE)
 
 
@@ -477,11 +472,10 @@
     edge_shape, row_shape, dots_shape = shape(GROUP, PLANE), shape(HALF, HALF), shape(8, HALF)
 
     cells_shape = shape(NZ, ROWS, CELLS)
-    start, along, *swaps = call(
+    start, *swaps = call(
         entry_kernel,
         [
             field_shape,
-            shape(GROUP, 2 * COLS, PLANE),
             shape(8, PLANE),
             shape(8, PLANE),
             shape(2 * HALF, HALF),
@@ -498,9 +492,9 @@
     )
     halos = swap(swaps[0], swaps[1], "gx") + swap(swaps[2], swaps[3], "gy")
     turn_angles = jnp.asarray(turn_table())
-    along_z, turned_right, *table = call(
+    along, turned_right, *table = call(
         side_kernel,
-        [shape(GROUP, COLS, PLANE), field_shape] + [shape(2 * CELLS, CELLS, dtype=bf16)] * 2,
+        [shape(GROUP, 3 * COLS, PLANE), field_shape] + [shape(2 * CELLS, CELLS, dtype=bf16)] * 2,
         swaps[0],
         conductance,
         right_side,
@@ -508,21 +502,20 @@
         jnp.asarray(column_table()),
         hbm=(1, 2, 3, 4),
         scratch=[
-            pltpu.VMEM((NZ, ROWS, CELLS), f32),
+            pltpu.VMEM((3, NZ, ROWS, CELLS), f32),
             pltpu.VMEM((NZ, ROWS, CELLS), f32),
             pltpu.VMEM((8, 2 * CELLS), f32),
             pltpu.VMEM((2 * CELLS, CELLS), f32),
             pltpu.SemaphoreType.DMA((4,)),
         ],
     )
-    halos, along_z, turned_right, table = lax.optimization_barrier((halos, along_z, turned_right, table))
+    halos, along, turned_right, table = lax.optimization_barrier((halos, along, turned_right, table))
     chunk, residual = call(
         residual_kernel,
         [shape(GROUP, 4 * COLS, PLANE), field_shape],
         turned_right,
         start,
         along,
-        along_z,
         *halos,
     )
     chunk = exchange(chunk)

time: 142 us -> 141 us (level)
  no operation moved by 1% of the time
where the time goes in v7:
time: 141 us; the launch traced here: 140 us
  blocking collectives  71.5 us (51%)
  starting transfers between devices  28 us (20%)
  waiting for transfers between devices  19.8 us (14%)
  Pallas kernels  19.5 us (14%)
    all_to_all x4, blocking collectives, exchange(): return lax.all_to_all(parts, 'gx', 0, 0, tiled=True)  71.5 us
    pallas_call x12, Pallas kernels, call(): pl.pallas_call(kernel, out_shape=outs, in_specs=specs, out_specs=[out_spe...  19.5 us
    all_to_all x2, starting transfers between devices, exchange(): return lax.all_to_all(parts, 'gx', 0, 0, tiled=True)  10.2 us
    ppermute x3, waiting for transfers between devices, sum_rows(): lax.ppermute(value, 'gy', [(i, i ^ mask) for i in range(count)])  9.37 us
    ppermute x4, waiting for transfers between devices, shift(): lax.ppermute(value, axis, [(i, (i + step) % count) for i in range(count)])  6.41 us
    ppermute x2, starting transfers between devices, swap(): lax.ppermute(second, axis, [(i, (i + 2 * (i % 2) - 1) % count) for i in r...  4.95 us
    ppermute x4, starting transfers between devices, shift(): lax.ppermute(value, axis, [(i, (i + step) % count) for i in range(count)])  4.71 us
    ppermute x3, starting transfers between devices, sum_rows(): lax.ppermute(value, 'gy', [(i, i ^ mask) for i in range(count)])  4.54 us
  transfers between devices with their start and end apart: 13, of which 6 were waited for; matrix products, arithmetic and copies ran while one was open for 0% of the time, Pallas kernels for 3%

profile of v7, /device:TPU:2, one launch (start us, length us, event | category | flops | bytes accessed | tf_op | source)
XLA Modules:
  0.0 139.6 jit_solution(5604229664578127891)
XLA Ops:
  0.6 1.4 %shard_map.112 = (f32[256,256]{1,0:T(8,128)S(1)}, f32[8,256]{1,0:T(8,128)S(1)}, f32[8,256]{1,0:T(8,128)S(1)}, f32[256,128]{1,0:T(8,128)S(1)}, f32[256,128]{1,0:T(8,128)S(1)}) custom-call(f32[64,4,256]{2,1,0:T(4,128)} %start_ref.1, f32[3,64,4,256]{3,2,1,0:T(4,128)} %cond_hbm.3), custom_call_target="tpu_custom_call" | custom-call | bytes 1048576 | tf_op jit(solution)/shard_map/pallas_call | solution.py:434
  2.1 2.0 %collective-permute-start.2 = (f32[256,128]{1,0:T(8,128)S(1)}, f32[256,128]{1,0:T(8,128)S(1)}, u32[]{:S(2)}, u32[]{:S(2)}) collective-permute-start(f32[256,128]{1,0:T(8,128)S(1)} %get-tuple-element.49), channel_id=1, source_target_pairs={{0,1},{1,0},{2,3},{3,2},{4,5},{5,4},{6,7},{7,6},{8,9},{9,8},{10,11... | collective-permute-start | bytes 393224 | tf_op jit(solution)/shard_map/ppermute | solution.py:452
  4.1 4.9 %collective-permute-start.3 = (f32[256,128]{1,0:T(8,128)S(1)}, f32[256,128]{1,0:T(8,128)S(1)}, u32[]{:S(2)}, u32[]{:S(2)}) collective-permute-start(f32[256,128]{1,0:T(8,128)S(1)} %get-tuple-element.50), channel_id=1, source_target_pairs={{0,7},{1,2},{2,1},{3,4},{4,3},{5,6},{6,5},{7,0},{8,15},{9,10},{10,... | collective-permute-start | bytes 393224 | tf_op jit(solution)/shard_map/ppermute | solution.py:453
  9.1 1.6 %collective-permute-start = (f32[8,256]{1,0:T(8,128)S(1)}, f32[8,256]{1,0:T(8,128)S(1)}, u32[]{:S(2)}, u32[]{:S(2)}) collective-permute-start(f32[8,256]{1,0:T(8,128)S(1)} %get-tuple-element.47.order_ref), channel_id=1, source_target_pairs={{0,8},{8,0},{16,24},{24,16},{32,40},{40,32},{48,56},{56,48},{64,72... | collective-permute-start | bytes 24584 | tf_op jit(solution)/shard_map/ppermute | solution.py:452
  10.6 2.0 %shard_map.113 = (f32[32,24,256]{2,1,0:T(8,128)S(1)}, f32[256,256]{1,0:T(8,128)S(1)}, bf16[512,256]{1,0:T(8,128)(2,1)S(1)}, bf16[512,256]{1,0:T(8,128)(2,1)S(1)}) custom-call(f32[8,256]{1,0:T(8,128)S(1)} %get-tuple-element.47.order_ref, f32[3,64,4,256]{3,2,1,0:T(4,128)} %cond_hbm.3, f32[64,4,256]{2,1,0:T(4,128)} %right_hbm.1, ...), custom_call_target="tpu_custom_call" | custom-call | bytes 1048576 | tf_op jit(solution)/shard_map/pallas_call | solution.py:434
  13.4 24.7 %all_to_all.30.field_ref.chunk_ref = f32[32,32,256]{2,1,0:T(8,128)S(1)} all-to-all(f32[32,32,256]{2,1,0:T(8,128)S(1)} %get-tuple-element.62), channel_id=1, replica_groups=mesh['gx'=32,'gy'=8] {'gx'}, dimensions={0} | all-to-all | bytes 2097152 | tf_op jit(solution)/shard_map/all_to_all | solution.py:458
  38.5 15.1 %all_to_all.31.parts_ref = f32[32,16,256]{2,1,0:T(8,128)S(1)} all-to-all(f32[32,16,256]{2,1,0:T(8,128)S(1)} %shard_map.115), channel_id=1, replica_groups=mesh['gx'=32,'gy'=8] {'gx'}, dimensions={0} | all-to-all | bytes 1048576 | tf_op jit(solution)/shard_map/all_to_all | solution.py:458
  53.6 4.7 %shard_map.116 = (f32[32,40,128]{2,1,0:T(8,128)}, f32[8,128]{1,0:T(8,128)S(1)}) custom-call(f32[32,16,256]{2,1,0:T(8,128)S(1)} %all_to_all.31.parts_ref, f32[64,64,256]{2,1,0:T(8,128)S(1)} %bitcast.1, bf16[512,512]{1,0:T(8,128)(2,1)S(1)} %copy-done.2, bf16[512,512]{1,0:T(8,128)(2,1)S(1)} %copy-done.1), custom_call_target="tpu_custom_call" | custom-call | flops 2000000000 | bytes 1048576 | tf_op jit(solution)/shard_map/pallas_call | solution.py:434
  58.3 5.1 %all-to-all-start.2 = ((f32[32,40,128]{2,1,0:T(8,128)}), f32[32,40,128]{2,1,0:T(8,128)S(1)}, u32[]{:S(2)}, u32[]{:S(2)}) async-start(f32[32,40,128]{2,1,0:T(8,128)} %get-tuple-element.65), calls=%async_computation.2 | async-start | bytes 1310720 | tf_op jit(solution)/shard_map/all_to_all | solution.py:458
  64.6 1.4 %collective-permute-start.5 = (f32[128,128]{1,0:T(8,128)S(1)}, f32[128,128]{1,0:T(8,128)S(1)}, u32[]{:S(2)}, u32[]{:S(2)}) collective-permute-start(f32[128,128]{1,0:T(8,128)S(1)} %get-tuple-element.67), channel_id=1, source_target_pairs={{0,7},{1,0},{2,1},{3,2},{4,3},{5,4},{6,5},{7,6},{8,15},{9,8},{10,9... | collective-permute-start | bytes 196616 | tf_op jit(solution)/shard_map/ppermute | solution.py:447
  66.0 5.3 %collective-permute-done.4.cond_next_ref = f32[32,256]{1,0:T(8,128)S(1)} collective-permute-done((f32[32,256]{1,0:T(8,128)S(1)}, f32[32,256]{1,0:T(8,128)S(1)}, u32[]{:S(2)}, u32[]{:S(2)}) %collective-permute-start.4) | collective-permute-done | bytes 32800 | tf_op jit(solution)/shard_map/ppermute | solution.py:447
  71.4 4.0 %all-to-all-done.2.parts_ref = f32[32,40,128]{2,1,0:T(8,128)S(1)} async-done(((f32[32,40,128]{2,1,0:T(8,128)}), f32[32,40,128]{2,1,0:T(8,128)S(1)}, u32[]{:S(2)}, u32[]{:S(2)}) %all-to-all-start.2) | async-done | bytes 655392 | tf_op jit(solution)/shard_map/all_to_all | solution.py:458
  76.0 3.2 %collective-permute-start.7 = (f32[128,128]{1,0:T(8,128)S(1)}, f32[128,128]{1,0:T(8,128)S(1)}, u32[]{:S(2)}, u32[]{:S(2)}) collective-permute-start(f32[128,128]{1,0:T(8,128)S(1)} %get-tuple-element.75.order_ref), channel_id=1, source_target_pairs={{0,7},{1,0},{2,1},{3,2},{4,3},{5,4},{6,5},{7,6},{8,15},{9,8},{10,9... | collective-permute-start | bytes 196616 | tf_op jit(solution)/shard_map/ppermute | solution.py:447
  82.4 15.1 %all_to_all.32.parts_ref = f32[32,16,256]{2,1,0:T(8,128)S(1)} all-to-all(f32[32,16,256]{2,1,0:T(8,128)S(1)} %get-tuple-element.83), channel_id=1, replica_groups=mesh['gx'=32,'gy'=8] {'gx'}, dimensions={0} | all-to-all | bytes 1048576 | tf_op jit(solution)/shard_map/all_to_all | solution.py:458
  97.5 3.8 %shard_map.121 = f32[32,40,128]{2,1,0:T(8,128)S(1)} custom-call(f32[32,16,256]{2,1,0:T(8,128)S(1)} %all_to_all.32.parts_ref, f32[64,64,256]{2,1,0:T(8,128)S(1)} %bitcast.2, bf16[512,512]{1,0:T(8,128)(2,1)S(1)} %get-tuple-element.84.high_ref, bf16[512,512]{1,0:T(8,128)(2,1)S(1)} %get-tuple-element.85.low_ref, f32[8,128]{1,0:T(8,128)S(1)} %get-tuple-element.86.dots_ref), custom_call_target="tpu_custom_call" | custom-call | flops 2000000000 | bytes 1048576 | tf_op jit(solution)/shard_map/pallas_call | solution.py:434
  101.3 16.6 %all_to_all.33.parts_ref = f32[32,40,128]{2,1,0:T(8,128)S(1)} all-to-all(f32[32,40,128]{2,1,0:T(8,128)S(1)} %shard_map.121), channel_id=1, replica_groups=mesh['gx'=32,'gy'=8] {'gx'}, dimensions={0} | all-to-all | bytes 1310720 | tf_op jit(solution)/shard_map/all_to_all | solution.py:458
  117.9 1.3 shard_map.122
  119.2 5.1 %all-to-all-start.5 = ((f32[32,24,256]{2,1,0:T(8,128)}), f32[32,24,256]{2,1,0:T(8,128)S(1)}, u32[]{:S(2)}, u32[]{:S(2)}) async-start(f32[32,24,256]{2,1,0:T(8,128)} %get-tuple-element.88), calls=%async_computation.5 | async-start | bytes 1572864 | tf_op jit(solution)/shard_map/all_to_all | solution.py:458
  124.5 3.6 %collective-permute-done.8 = f32[8,128]{1,0:T(8,128)S(1)} collective-permute-done((f32[8,128]{1,0:T(8,128)S(1)}, f32[8,128]{1,0:T(8,128)S(1)}, u32[]{:S(2)}, u32[]{:S(2)}) %collective-permute-start.8) | collective-permute-done | bytes 4128 | tf_op jit(solution)/shard_map/ppermute | solution.py:464
  128.1 1.8 %collective-permute-start.9 = (f32[8,128]{1,0:T(8,128)S(1)}, f32[8,128]{1,0:T(8,128)S(1)}, u32[]{:S(2)}, u32[]{:S(2)}) collective-permute-start(f32[8,128]{1,0:T(8,128)S(1)} %add.9), channel_id=1, source_target_pairs={{0,2},{1,3},{2,0},{3,1},{4,6},{5,7},{6,4},{7,5},{8,10},{9,11},{10,... | collective-permute-start | bytes 12296 | tf_op jit(solution)/shard_map/ppermute | solution.py:464
  129.8 2.7 %collective-permute-done.9 = f32[8,128]{1,0:T(8,128)S(1)} collective-permute-done((f32[8,128]{1,0:T(8,128)S(1)}, f32[8,128]{1,0:T(8,128)S(1)}, u32[]{:S(2)}, u32[]{:S(2)}) %collective-permute-start.9) | collective-permute-done | bytes 4128 | tf_op jit(solution)/shard_map/ppermute | solution.py:464
  132.6 2.7 %collective-permute-start.10 = (f32[8,128]{1,0:T(8,128)S(1)}, f32[8,128]{1,0:T(8,128)S(1)}, u32[]{:S(2)}, u32[]{:S(2)}) collective-permute-start(f32[8,128]{1,0:T(8,128)S(1)} %add.10), channel_id=1, source_target_pairs={{0,6},{1,7},{2,4},{3,5},{4,2},{5,3},{6,0},{7,1},{8,14},{9,15},{10,... | collective-permute-start | bytes 12296 | tf_op jit(solution)/shard_map/ppermute | solution.py:464
  135.2 3.0 %collective-permute-done.10 = f32[8,128]{1,0:T(8,128)S(1)} collective-permute-done((f32[8,128]{1,0:T(8,128)S(1)}, f32[8,128]{1,0:T(8,128)S(1)}, u32[]{:S(2)}, u32[]{:S(2)}) %collective-permute-start.10) | collective-permute-done | bytes 4128 | tf_op jit(solution)/shard_map/ppermute | solution.py:464
  138.3 1.3 shard_map.123
  (31 shorter events, 6.2 us)
Async XLA Ops:
  2.1 10.6 %collective-permute-start.2 = (f32[256,128]{1,0:T(8,128)S(1)}, f32[256,128]{1,0:T(8,128)S(1)}, u32[]{:S(2)}, u32[]{:S(2)}) collective-permute-start(f32[256,128]{1,0:T(8,128)S(1)} %get-tuple-element.49), channel_id=1, source_target_pairs={{0,1},{1,0},{2,3},{3,2},{4,5},{5,4},{6,7},{7,6},{8,9},{9,8},{10,11... | collective-permute-start | bytes 393224 | tf_op jit(solution)/shard_map/ppermute | solution.py:452
  4.1 8.6 %collective-permute-start.3 = (f32[256,128]{1,0:T(8,128)S(1)}, f32[256,128]{1,0:T(8,128)S(1)}, u32[]{:S(2)}, u32[]{:S(2)}) collective-permute-start(f32[256,128]{1,0:T(8,128)S(1)} %get-tuple-element.50), channel_id=1, source_target_pairs={{0,7},{1,2},{2,1},{3,4},{4,3},{5,6},{6,5},{7,0},{8,15},{9,10},{10,... | collective-permute-start | bytes 393224 | tf_op jit(solution)/shard_map/ppermute | solution.py:453
  9.0 3.7 %collective-permute-start.1 = (f32[8,256]{1,0:T(8,128)S(1)}, f32[8,256]{1,0:T(8,128)S(1)}, u32[]{:S(2)}, u32[]{:S(2)}) collective-permute-start(f32[8,256]{1,0:T(8,128)S(1)} %get-tuple-element.48), channel_id=1, source_target_pairs={{0,248},{8,16},{16,8},{24,32},{32,24},{40,48},{48,40},{56,64},{64,... | collective-permute-start | bytes 24584 | tf_op jit(solution)/shard_map/ppermute | solution.py:453
  9.0 44.5 %copy-start.1 = (bf16[512,512]{1,0:T(8,128)(2,1)S(1)}, bf16[512,512]{1,0:T(8,128)(2,1)}, u32[]{:S(2)}) copy-start(bf16[512,512]{1,0:T(8,128)(2,1)} %constant.13.clone.low_ref.low_hbm) | copy-start | bytes 1572868
  9.0 44.5 %copy-start.2 = (bf16[512,512]{1,0:T(8,128)(2,1)S(1)}, bf16[512,512]{1,0:T(8,128)(2,1)}, u32[]{:S(2)}) copy-start(bf16[512,512]{1,0:T(8,128)(2,1)} %constant.12.clone.high_ref.high_hbm) | copy-start | bytes 1572868
  9.0 44.5 %copy-start.3 = (f32[1,64,64,256]{3,2,1,0:T(8,128)S(1)}, f32[1,64,64,256]{3,2,1,0:T(8,128)}, u32[]{:S(2)}) copy-start(f32[1,64,64,256]{3,2,1,0:T(8,128)} %param.12) | copy-start | bytes 12582916
  9.1 3.6 %collective-permute-start = (f32[8,256]{1,0:T(8,128)S(1)}, f32[8,256]{1,0:T(8,128)S(1)}, u32[]{:S(2)}, u32[]{:S(2)}) collective-permute-start(f32[8,256]{1,0:T(8,128)S(1)} %get-tuple-element.47.order_ref), channel_id=1, source_target_pairs={{0,8},{8,0},{16,24},{24,16},{32,40},{40,32},{48,56},{56,48},{64,72... | collective-permute-start | bytes 24584 | tf_op jit(solution)/shard_map/ppermute | solution.py:452
  58.3 17.1 %all-to-all-start.2 = ((f32[32,40,128]{2,1,0:T(8,128)}), f32[32,40,128]{2,1,0:T(8,128)S(1)}, u32[]{:S(2)}, u32[]{:S(2)}) async-start(f32[32,40,128]{2,1,0:T(8,128)} %get-tuple-element.65), calls=%async_computation.2 | async-start | bytes 1310720 | tf_op jit(solution)/shard_map/all_to_all | solution.py:458
  64.6 6.7 %collective-permute-start.5 = (f32[128,128]{1,0:T(8,128)S(1)}, f32[128,128]{1,0:T(8,128)S(1)}, u32[]{:S(2)}, u32[]{:S(2)}) collective-permute-start(f32[128,128]{1,0:T(8,128)S(1)} %get-tuple-element.67), channel_id=1, source_target_pairs={{0,7},{1,0},{2,1},{3,2},{4,3},{5,4},{6,5},{7,6},{8,15},{9,8},{10,9... | collective-permute-start | bytes 196616 | tf_op jit(solution)/shard_map/ppermute | solution.py:447
  66.0 5.3 %collective-permute-start.4 = (f32[32,256]{1,0:T(8,128)S(1)}, f32[32,256]{1,0:T(8,128)S(1)}, u32[]{:S(2)}, u32[]{:S(2)}) collective-permute-start(f32[32,256]{1,0:T(8,128)S(1)} %get-tuple-element.66), channel_id=1, source_target_pairs={{0,248},{8,0},{16,8},{24,16},{32,24},{40,32},{48,40},{56,48},{64,5... | collective-permute-start | bytes 98312 | tf_op jit(solution)/shard_map/ppermute | solution.py:447
  75.4 22.1 %copy-start.4 = (f32[1,64,64,256]{3,2,1,0:T(8,128)S(1)}, f32[1,64,64,256]{3,2,1,0:T(8,128)}, u32[]{:S(2)}) copy-start(f32[1,64,64,256]{3,2,1,0:T(8,128)} %param.12) | copy-start | bytes 12582916
  75.9 5.6 %collective-permute-start.6 = (f32[128,128]{1,0:T(8,128)S(1)}, f32[128,128]{1,0:T(8,128)S(1)}, u32[]{:S(2)}, u32[]{:S(2)}) collective-permute-start(f32[128,128]{1,0:T(8,128)S(1)} %get-tuple-element.74), channel_id=1, source_target_pairs={{0,1},{1,2},{2,3},{3,4},{4,5},{5,6},{6,7},{7,0},{8,9},{9,10},{10,1... | collective-permute-start | bytes 196616 | tf_op jit(solution)/shard_map/ppermute | solution.py:447
  76.0 5.5 %collective-permute-start.7 = (f32[128,128]{1,0:T(8,128)S(1)}, f32[128,128]{1,0:T(8,128)S(1)}, u32[]{:S(2)}, u32[]{:S(2)}) collective-permute-start(f32[128,128]{1,0:T(8,128)S(1)} %get-tuple-element.75.order_ref), channel_id=1, source_target_pairs={{0,7},{1,0},{2,1},{3,2},{4,3},{5,4},{6,5},{7,6},{8,15},{9,8},{10,9... | collective-permute-start | bytes 196616 | tf_op jit(solution)/shard_map/ppermute | solution.py:447
  97.5 40.8 %copy-start = (f32[64,4,256]{2,1,0:T(4,128)S(1)}, f32[64,4,256]{2,1,0:T(4,128)}, u32[]{:S(2)}) copy-start(f32[64,4,256]{2,1,0:T(4,128)} %start_ref.1) | copy-start | bytes 786436
  119.2 19.1 %all-to-all-start.5 = ((f32[32,24,256]{2,1,0:T(8,128)}), f32[32,24,256]{2,1,0:T(8,128)S(1)}, u32[]{:S(2)}, u32[]{:S(2)}) async-start(f32[32,24,256]{2,1,0:T(8,128)} %get-tuple-element.88), calls=%async_computation.5 | async-start | bytes 1572864 | tf_op jit(solution)/shard_map/all_to_all | solution.py:458
  124.4 3.7 %collective-permute-start.8 = (f32[8,128]{1,0:T(8,128)S(1)}, f32[8,128]{1,0:T(8,128)S(1)}, u32[]{:S(2)}, u32[]{:S(2)}) collective-permute-start(f32[8,128]{1,0:T(8,128)S(1)} %get-tuple-element.90), channel_id=1, source_target_pairs={{0,1},{1,0},{2,3},{3,2},{4,5},{5,4},{6,7},{7,6},{8,9},{9,8},{10,11... | collective-permute-start | bytes 12296 | tf_op jit(solution)/shard_map/ppermute | solution.py:464
  128.1 4.5 %collective-permute-start.9 = (f32[8,128]{1,0:T(8,128)S(1)}, f32[8,128]{1,0:T(8,128)S(1)}, u32[]{:S(2)}, u32[]{:S(2)}) collective-permute-start(f32[8,128]{1,0:T(8,128)S(1)} %add.9), channel_id=1, source_target_pairs={{0,2},{1,3},{2,0},{3,1},{4,6},{5,7},{6,4},{7,5},{8,10},{9,11},{10,... | collective-permute-start | bytes 12296 | tf_op jit(solution)/shard_map/ppermute | solution.py:464
  132.6 5.7 %collective-permute-start.10 = (f32[8,128]{1,0:T(8,128)S(1)}, f32[8,128]{1,0:T(8,128)S(1)}, u32[]{:S(2)}, u32[]{:S(2)}) collective-permute-start(f32[8,128]{1,0:T(8,128)S(1)} %add.10), channel_id=1, source_target_pairs={{0,6},{1,7},{2,4},{3,5},{4,2},{5,3},{6,0},{7,1},{8,14},{9,15},{10,... | collective-permute-start | bytes 12296 | tf_op jit(solution)/shard_map/ppermute | solution.py:464

commit v8 on v7

--- a/solution.py
+++ b/solution.py
@@ -254,15 +254,17 @@
     out_ref[...] = products(table, split(field), ((1,), (0,))).reshape(GROUP, 2 * COLS, PLANE)
 
 
-def first_solve_kernel(parts_ref, inverse_ref, high_ref, low_ref, out_ref, sums_ref, wave, solved, back):
-    solve(0, parts_ref, inverse_ref, high_ref, low_ref, None, out_ref, sums_ref, wave, solved, back)
+def first_solve_kernel(
+    parts_ref, inverse_ref, high_ref, low_ref, out_hbm, sums_ref, wave, solved, back, out_ref, semaphores
+):
+    solve(0, (out_hbm, semaphores), parts_ref, inverse_ref, high_ref, low_ref, None, out_ref, sums_ref, wave, solved, back)
 
 
 def second_solve_kernel(parts_ref, inverse_ref, high_ref, low_ref, dots_ref, out_ref, wave, solved, sums_ref):
-    solve(2, parts_ref, inverse_ref, high_ref, low_ref, dots_ref, out_ref, sums_ref, wave, solved, None)
-
-
-def solve(which, parts_ref, inverse_ref, high_ref, low_ref, dots_ref, out_ref, sums_ref, wave, solved, back):
+    solve(2, None, parts_ref, inverse_ref, high_ref, low_ref, dots_ref, out_ref, sums_ref, wave, solved, None)
+
+
+def solve(which, target, parts_ref, inverse_ref, high_ref, low_ref, dots_ref, out_ref, sums_ref, wave, solved, back):
     table = (high_ref[...], low_ref[...])
     parts = parts_ref[...].reshape(2 * CELLS, PLANE).T
     wave[...] = products(split(parts), table, ((1,), (0,)))
@@ -290,16 +292,27 @@
     total = jnp.sum(total, axis=0, keepdims=True) / LENGTH
     others = 0.0 if dots_ref is None else dots_ref[...]
     sums_ref[...] = jnp.where(row == which, total, others)
-    parts = products(table, split(solved[...]), ((1,), (1,))).reshape(GROUP, 2 * COLS, PLANE)
+    copies = []
     for half in range(2):
-        out_ref[:, 16 * half : 16 * (half + 1), :] = parts[:, :, half * HALF : (half + 1) * HALF]
+        lanes = slice(half * HALF, (half + 1) * HALF)
+        parts = products(table, split(solved[lanes]), ((1,), (1,))).reshape(GROUP, 2 * COLS, HALF)
+        rows = pl.ds(16 * half, 16)
+        out_ref[:, rows, :] = parts
+        if which == 0:
+            back[:, :, lanes] = parts
+            copies.append(pltpu.make_async_copy(out_ref.at[:, rows], target[0].at[:, rows], target[1].at[half]))
+            copies[half].start()
     if which == 0:
-        back[...] = parts
         for side, (column, step) in enumerate(((COLS - 1, 1), (0, GROUP - 1))):
             for part in range(2):
                 rows = pltpu.roll(back[:, part * COLS + column, :], step, 0)
                 for half in range(2):
                     out_ref[:, 32 + 4 * half + 2 * side + part, :] = rows[:, half * HALF : (half + 1) * HALF]
+        rows = pl.ds(32, 8)
+        copies.append(pltpu.make_async_copy(out_ref.at[:, rows], target[0].at[:, rows], target[1].at[2]))
+        copies[2].start()
+        for copy in copies:
+            copy.wait()
     else:
         out_ref[:, 32:40, :] = jnp.broadcast_to(sums_ref[...][None], (GROUP, 8, HALF))
 
@@ -423,19 +436,20 @@
     return jax.ShapeDtypeStruct(dims, dtype)
 
 
-def call(kernel, outs, *args, hbm=(), scratch=(), cost=0):
+def call(kernel, outs, *args, hbm=(), out_hbm=(), scratch=(), cost=0):
     specs = [pl.BlockSpec(memory_space=pltpu.VMEM) for _ in args]
     args = list(args)
     for i in hbm:
         specs[i] = pl.BlockSpec(memory_space=pltpu.HBM)
         args[i] = pltpu.with_memory_space_constraint(args[i], pltpu.HBM)
     many = isinstance(outs, (tuple, list))
-    out_spec = pl.BlockSpec(memory_space=pltpu.VMEM)
+    count = len(outs) if many else 1
+    out_specs = [pl.BlockSpec(memory_space=pltpu.HBM if i in out_hbm else pltpu.VMEM) for i in range(count)]
     return pl.pallas_call(
         kernel,
         out_shape=outs,
         in_specs=specs,
-        out_specs=[out_spec] * len(outs) if many else out_spec,
+        out_specs=out_specs if many else out_specs[0],
         scratch_shapes=list(scratch),
         compiler_params=pltpu.CompilerParams(vmem_limit_bytes=16 * 1024 * 1024),
         cost_estimate=pl.CostEstimate(flops=cost, bytes_accessed=2**20, transcendentals=0),
@@ -545,7 +559,14 @@
         parts,
         inverse,
         *waves,
-        scratch=[wave_shape, wave_shape, pltpu.VMEM((GROUP, 2 * COLS, PLANE), f32)],
+        out_hbm=(0,),
+        scratch=[
+            wave_shape,
+            wave_shape,
+            pltpu.VMEM((GROUP, 2 * COLS, PLANE), f32),
+            pltpu.VMEM((GROUP, 5 * COLS, HALF), f32),
+            pltpu.SemaphoreType.DMA((3,)),
+        ],
         cost=2 * 10**9,
     )
     parts, cond_after, cond_over = lax.optimization_barrier((exchange(parts), cond_after, cond_over))

time: 141 us -> 142 us (level)
  no operation moved by 1% of the time
where the time goes in v8:
time: 142 us; the launch traced here: 140 us
  blocking collectives  71.5 us (50%)
  starting transfers between devices  28 us (20%)
  Pallas kernels  20.2 us (14%)
  waiting for transfers between devices  19.8 us (14%)
    all_to_all x4, blocking collectives, exchange(): return lax.all_to_all(parts, 'gx', 0, 0, tiled=True)  71.5 us
    pallas_call x12, Pallas kernels, call(): pl.pallas_call(kernel, out_shape=outs, in_specs=specs, out_specs=out_spec...  20.2 us
    all_to_all x2, starting transfers between devices, exchange(): return lax.all_to_all(parts, 'gx', 0, 0, tiled=True)  10.2 us
    ppermute x3, waiting for transfers between devices, sum_rows(): lax.ppermute(value, 'gy', [(i, i ^ mask) for i in range(count)])  9.38 us
    ppermute x4, waiting for transfers between devices, shift(): lax.ppermute(value, axis, [(i, (i + step) % count) for i in range(count)])  6.4 us
    ppermute x2, starting transfers between devices, swap(): lax.ppermute(second, axis, [(i, (i + 2 * (i % 2) - 1) % count) for i in r...  4.95 us
    ppermute x4, starting transfers between devices, shift(): lax.ppermute(value, axis, [(i, (i + step) % count) for i in range(count)])  4.71 us
    ppermute x3, starting transfers between devices, sum_rows(): lax.ppermute(value, 'gy', [(i, i ^ mask) for i in range(count)])  4.53 us
  transfers between devices with their start and end apart: 13, of which 6 were waited for; matrix products, arithmetic and copies ran while one was open for 0% of the time, Pallas kernels for 3%

profile of v8, /device:TPU:2, one launch (start us, length us, event | category | flops | bytes accessed | tf_op | source)
XLA Modules:
  0.0 140.3 jit_solution(9699824497481933445)
XLA Ops:
  0.6 1.4 %shard_map.112 = (f32[256,256]{1,0:T(8,128)S(1)}, f32[8,256]{1,0:T(8,128)S(1)}, f32[8,256]{1,0:T(8,128)S(1)}, f32[256,128]{1,0:T(8,128)S(1)}, f32[256,128]{1,0:T(8,128)S(1)}) custom-call(f32[64,4,256]{2,1,0:T(4,128)} %start_ref.1, f32[3,64,4,256]{3,2,1,0:T(4,128)} %cond_hbm.3), custom_call_target="tpu_custom_call" | custom-call | bytes 1048576 | tf_op jit(solution)/shard_map/pallas_call | solution.py:448
  2.1 2.0 %collective-permute-start.2 = (f32[256,128]{1,0:T(8,128)S(1)}, f32[256,128]{1,0:T(8,128)S(1)}, u32[]{:S(2)}, u32[]{:S(2)}) collective-permute-start(f32[256,128]{1,0:T(8,128)S(1)} %get-tuple-element.49), channel_id=1, source_target_pairs={{0,1},{1,0},{2,3},{3,2},{4,5},{5,4},{6,7},{7,6},{8,9},{9,8},{10,11... | collective-permute-start | bytes 393224 | tf_op jit(solution)/shard_map/ppermute | solution.py:466
  4.1 4.9 %collective-permute-start.3 = (f32[256,128]{1,0:T(8,128)S(1)}, f32[256,128]{1,0:T(8,128)S(1)}, u32[]{:S(2)}, u32[]{:S(2)}) collective-permute-start(f32[256,128]{1,0:T(8,128)S(1)} %get-tuple-element.50), channel_id=1, source_target_pairs={{0,7},{1,2},{2,1},{3,4},{4,3},{5,6},{6,5},{7,0},{8,15},{9,10},{10,... | collective-permute-start | bytes 393224 | tf_op jit(solution)/shard_map/ppermute | solution.py:467
  9.1 1.6 %collective-permute-start = (f32[8,256]{1,0:T(8,128)S(1)}, f32[8,256]{1,0:T(8,128)S(1)}, u32[]{:S(2)}, u32[]{:S(2)}) collective-permute-start(f32[8,256]{1,0:T(8,128)S(1)} %get-tuple-element.47.order_ref), channel_id=1, source_target_pairs={{0,8},{8,0},{16,24},{24,16},{32,40},{40,32},{48,56},{56,48},{64,72... | collective-permute-start | bytes 24584 | tf_op jit(solution)/shard_map/ppermute | solution.py:466
  10.6 2.0 %shard_map.113 = (f32[32,24,256]{2,1,0:T(8,128)S(1)}, f32[256,256]{1,0:T(8,128)S(1)}, bf16[512,256]{1,0:T(8,128)(2,1)S(1)}, bf16[512,256]{1,0:T(8,128)(2,1)S(1)}) custom-call(f32[8,256]{1,0:T(8,128)S(1)} %get-tuple-element.47.order_ref, f32[3,64,4,256]{3,2,1,0:T(4,128)} %cond_hbm.3, f32[64,4,256]{2,1,0:T(4,128)} %right_hbm.1, ...), custom_call_target="tpu_custom_call" | custom-call | bytes 1048576 | tf_op jit(solution)/shard_map/pallas_call | solution.py:448
  13.4 24.7 %all_to_all.30.field_ref.chunk_ref = f32[32,32,256]{2,1,0:T(8,128)S(1)} all-to-all(f32[32,32,256]{2,1,0:T(8,128)S(1)} %get-tuple-element.62), channel_id=1, replica_groups=mesh['gx'=32,'gy'=8] {'gx'}, dimensions={0} | all-to-all | bytes 2097152 | tf_op jit(solution)/shard_map/all_to_all | solution.py:472
  38.5 15.1 %all_to_all.31.parts_ref = f32[32,16,256]{2,1,0:T(8,128)S(1)} all-to-all(f32[32,16,256]{2,1,0:T(8,128)S(1)} %shard_map.115), channel_id=1, replica_groups=mesh['gx'=32,'gy'=8] {'gx'}, dimensions={0} | all-to-all | bytes 1048576 | tf_op jit(solution)/shard_map/all_to_all | solution.py:472
  53.6 5.1 %shard_map.116 = (f32[32,40,128]{2,1,0:T(8,128)}, f32[8,128]{1,0:T(8,128)S(1)}) custom-call(f32[32,16,256]{2,1,0:T(8,128)S(1)} %all_to_all.31.parts_ref, f32[64,64,256]{2,1,0:T(8,128)S(1)} %bitcast.1, bf16[512,512]{1,0:T(8,128)(2,1)S(1)} %copy-done.2, bf16[512,512]{1,0:T(8,128)(2,1)S(1)} %copy-done.1), custom_call_target="tpu_custom_call" | custom-call | flops 2000000000 | bytes 1048576 | tf_op jit(solution)/shard_map/pallas_call | solution.py:448
  58.6 5.1 %all-to-all-start.2 = ((f32[32,40,128]{2,1,0:T(8,128)}), f32[32,40,128]{2,1,0:T(8,128)S(1)}, u32[]{:S(2)}, u32[]{:S(2)}) async-start(f32[32,40,128]{2,1,0:T(8,128)} %get-tuple-element.65), calls=%async_computation.2 | async-start | bytes 1310720 | tf_op jit(solution)/shard_map/all_to_all | solution.py:472
  65.0 1.4 %collective-permute-start.5 = (f32[128,128]{1,0:T(8,128)S(1)}, f32[128,128]{1,0:T(8,128)S(1)}, u32[]{:S(2)}, u32[]{:S(2)}) collective-permute-start(f32[128,128]{1,0:T(8,128)S(1)} %get-tuple-element.67), channel_id=1, source_target_pairs={{0,7},{1,0},{2,1},{3,2},{4,3},{5,4},{6,5},{7,6},{8,15},{9,8},{10,9... | collective-permute-start | bytes 196616 | tf_op jit(solution)/shard_map/ppermute | solution.py:461
  66.4 5.3 %collective-permute-done.4.cond_next_ref = f32[32,256]{1,0:T(8,128)S(1)} collective-permute-done((f32[32,256]{1,0:T(8,128)S(1)}, f32[32,256]{1,0:T(8,128)S(1)}, u32[]{:S(2)}, u32[]{:S(2)}) %collective-permute-start.4) | collective-permute-done | bytes 32800 | tf_op jit(solution)/shard_map/ppermute | solution.py:461
  71.7 4.0 %all-to-all-done.2.parts_ref = f32[32,40,128]{2,1,0:T(8,128)S(1)} async-done(((f32[32,40,128]{2,1,0:T(8,128)}), f32[32,40,128]{2,1,0:T(8,128)S(1)}, u32[]{:S(2)}, u32[]{:S(2)}) %all-to-all-start.2) | async-done | bytes 655392 | tf_op jit(solution)/shard_map/all_to_all | solution.py:472
  76.3 3.2 %collective-permute-start.7 = (f32[128,128]{1,0:T(8,128)S(1)}, f32[128,128]{1,0:T(8,128)S(1)}, u32[]{:S(2)}, u32[]{:S(2)}) collective-permute-start(f32[128,128]{1,0:T(8,128)S(1)} %get-tuple-element.75.order_ref), channel_id=1, source_target_pairs={{0,7},{1,0},{2,1},{3,2},{4,3},{5,4},{6,5},{7,6},{8,15},{9,8},{10,9... | collective-permute-start | bytes 196616 | tf_op jit(solution)/shard_map/ppermute | solution.py:461
  82.8 15.1 %all_to_all.32.parts_ref = f32[32,16,256]{2,1,0:T(8,128)S(1)} all-to-all(f32[32,16,256]{2,1,0:T(8,128)S(1)} %get-tuple-element.83), channel_id=1, replica_groups=mesh['gx'=32,'gy'=8] {'gx'}, dimensions={0} | all-to-all | bytes 1048576 | tf_op jit(solution)/shard_map/all_to_all | solution.py:472
  97.9 4.1 %shard_map.121 = f32[32,40,128]{2,1,0:T(8,128)S(1)} custom-call(f32[32,16,256]{2,1,0:T(8,128)S(1)} %all_to_all.32.parts_ref, f32[64,64,256]{2,1,0:T(8,128)S(1)} %bitcast.2, bf16[512,512]{1,0:T(8,128)(2,1)S(1)} %get-tuple-element.84.high_ref, bf16[512,512]{1,0:T(8,128)(2,1)S(1)} %get-tuple-element.85.low_ref, f32[8,128]{1,0:T(8,128)S(1)} %get-tuple-element.86.dots_ref), custom_call_target="tpu_custom_call" | custom-call | flops 2000000000 | bytes 1048576 | tf_op jit(solution)/shard_map/pallas_call | solution.py:448
  102.0 16.6 %all_to_all.33.parts_ref = f32[32,40,128]{2,1,0:T(8,128)S(1)} all-to-all(f32[32,40,128]{2,1,0:T(8,128)S(1)} %shard_map.121), channel_id=1, replica_groups=mesh['gx'=32,'gy'=8] {'gx'}, dimensions={0} | all-to-all | bytes 1310720 | tf_op jit(solution)/shard_map/all_to_all | solution.py:472
  118.6 1.3 shard_map.122
  119.9 5.1 %all-to-all-start.5 = ((f32[32,24,256]{2,1,0:T(8,128)}), f32[32,24,256]{2,1,0:T(8,128)S(1)}, u32[]{:S(2)}, u32[]{:S(2)}) async-start(f32[32,24,256]{2,1,0:T(8,128)} %get-tuple-element.88), calls=%async_computation.5 | async-start | bytes 1572864 | tf_op jit(solution)/shard_map/all_to_all | solution.py:472
  125.2 3.6 %collective-permute-done.8 = f32[8,128]{1,0:T(8,128)S(1)} collective-permute-done((f32[8,128]{1,0:T(8,128)S(1)}, f32[8,128]{1,0:T(8,128)S(1)}, u32[]{:S(2)}, u32[]{:S(2)}) %collective-permute-start.8) | collective-permute-done | bytes 4128 | tf_op jit(solution)/shard_map/ppermute | solution.py:478
  128.8 1.8 %collective-permute-start.9 = (f32[8,128]{1,0:T(8,128)S(1)}, f32[8,128]{1,0:T(8,128)S(1)}, u32[]{:S(2)}, u32[]{:S(2)}) collective-permute-start(f32[8,128]{1,0:T(8,128)S(1)} %add.9), channel_id=1, source_target_pairs={{0,2},{1,3},{2,0},{3,1},{4,6},{5,7},{6,4},{7,5},{8,10},{9,11},{10,... | collective-permute-start | bytes 12296 | tf_op jit(solution)/shard_map/ppermute | solution.py:478
  130.5 2.7 %collective-permute-done.9 = f32[8,128]{1,0:T(8,128)S(1)} collective-permute-done((f32[8,128]{1,0:T(8,128)S(1)}, f32[8,128]{1,0:T(8,128)S(1)}, u32[]{:S(2)}, u32[]{:S(2)}) %collective-permute-start.9) | collective-permute-done | bytes 4128 | tf_op jit(solution)/shard_map/ppermute | solution.py:478
  133.3 2.7 %collective-permute-start.10 = (f32[8,128]{1,0:T(8,128)S(1)}, f32[8,128]{1,0:T(8,128)S(1)}, u32[]{:S(2)}, u32[]{:S(2)}) collective-permute-start(f32[8,128]{1,0:T(8,128)S(1)} %add.10), channel_id=1, source_target_pairs={{0,6},{1,7},{2,4},{3,5},{4,2},{5,3},{6,0},{7,1},{8,14},{9,15},{10,... | collective-permute-start | bytes 12296 | tf_op jit(solution)/shard_map/ppermute | solution.py:478
  135.9 3.1 %collective-permute-done.10 = f32[8,128]{1,0:T(8,128)S(1)} collective-permute-done((f32[8,128]{1,0:T(8,128)S(1)}, f32[8,128]{1,0:T(8,128)S(1)}, u32[]{:S(2)}, u32[]{:S(2)}) %collective-permute-start.10) | collective-permute-done | bytes 4128 | tf_op jit(solution)/shard_map/ppermute | solution.py:478
  139.0 1.3 shard_map.123
  (31 shorter events, 6.2 us)
Async XLA Ops:
  2.1 10.6 %collective-permute-start.2 = (f32[256,128]{1,0:T(8,128)S(1)}, f32[256,128]{1,0:T(8,128)S(1)}, u32[]{:S(2)}, u32[]{:S(2)}) collective-permute-start(f32[256,128]{1,0:T(8,128)S(1)} %get-tuple-element.49), channel_id=1, source_target_pairs={{0,1},{1,0},{2,3},{3,2},{4,5},{5,4},{6,7},{7,6},{8,9},{9,8},{10,11... | collective-permute-start | bytes 393224 | tf_op jit(solution)/shard_map/ppermute | solution.py:466
  4.1 8.6 %collective-permute-start.3 = (f32[256,128]{1,0:T(8,128)S(1)}, f32[256,128]{1,0:T(8,128)S(1)}, u32[]{:S(2)}, u32[]{:S(2)}) collective-permute-start(f32[256,128]{1,0:T(8,128)S(1)} %get-tuple-element.50), channel_id=1, source_target_pairs={{0,7},{1,2},{2,1},{3,4},{4,3},{5,6},{6,5},{7,0},{8,15},{9,10},{10,... | collective-permute-start | bytes 393224 | tf_op jit(solution)/shard_map/ppermute | solution.py:467
  9.0 3.7 %collective-permute-start.1 = (f32[8,256]{1,0:T(8,128)S(1)}, f32[8,256]{1,0:T(8,128)S(1)}, u32[]{:S(2)}, u32[]{:S(2)}) collective-permute-start(f32[8,256]{1,0:T(8,128)S(1)} %get-tuple-element.48), channel_id=1, source_target_pairs={{0,248},{8,16},{16,8},{24,32},{32,24},{40,48},{48,40},{56,64},{64,... | collective-permute-start | bytes 24584 | tf_op jit(solution)/shard_map/ppermute | solution.py:467
  9.0 44.5 %copy-start.1 = (bf16[512,512]{1,0:T(8,128)(2,1)S(1)}, bf16[512,512]{1,0:T(8,128)(2,1)}, u32[]{:S(2)}) copy-start(bf16[512,512]{1,0:T(8,128)(2,1)} %constant.13.clone.low_ref.low_hbm) | copy-start | bytes 1572868
  9.0 44.5 %copy-start.2 = (bf16[512,512]{1,0:T(8,128)(2,1)S(1)}, bf16[512,512]{1,0:T(8,128)(2,1)}, u32[]{:S(2)}) copy-start(bf16[512,512]{1,0:T(8,128)(2,1)} %constant.12.clone.high_ref.high_hbm) | copy-start | bytes 1572868
  9.0 44.5 %copy-start.3 = (f32[1,64,64,256]{3,2,1,0:T(8,128)S(1)}, f32[1,64,64,256]{3,2,1,0:T(8,128)}, u32[]{:S(2)}) copy-start(f32[1,64,64,256]{3,2,1,0:T(8,128)} %param.12) | copy-start | bytes 12582916
  9.1 3.6 %collective-permute-start = (f32[8,256]{1,0:T(8,128)S(1)}, f32[8,256]{1,0:T(8,128)S(1)}, u32[]{:S(2)}, u32[]{:S(2)}) collective-permute-start(f32[8,256]{1,0:T(8,128)S(1)} %get-tuple-element.47.order_ref), channel_id=1, source_target_pairs={{0,8},{8,0},{16,24},{24,16},{32,40},{40,32},{48,56},{56,48},{64,72... | collective-permute-start | bytes 24584 | tf_op jit(solution)/shard_map/ppermute | solution.py:466
  58.6 17.1 %all-to-all-start.2 = ((f32[32,40,128]{2,1,0:T(8,128)}), f32[32,40,128]{2,1,0:T(8,128)S(1)}, u32[]{:S(2)}, u32[]{:S(2)}) async-start(f32[32,40,128]{2,1,0:T(8,128)} %get-tuple-element.65), calls=%async_computation.2 | async-start | bytes 1310720 | tf_op jit(solution)/shard_map/all_to_all | solution.py:472
  65.0 6.7 %collective-permute-start.5 = (f32[128,128]{1,0:T(8,128)S(1)}, f32[128,128]{1,0:T(8,128)S(1)}, u32[]{:S(2)}, u32[]{:S(2)}) collective-permute-start(f32[128,128]{1,0:T(8,128)S(1)} %get-tuple-element.67), channel_id=1, source_target_pairs={{0,7},{1,0},{2,1},{3,2},{4,3},{5,4},{6,5},{7,6},{8,15},{9,8},{10,9... | collective-permute-start | bytes 196616 | tf_op jit(solution)/shard_map/ppermute | solution.py:461
  66.4 5.3 %collective-permute-start.4 = (f32[32,256]{1,0:T(8,128)S(1)}, f32[32,256]{1,0:T(8,128)S(1)}, u32[]{:S(2)}, u32[]{:S(2)}) collective-permute-start(f32[32,256]{1,0:T(8,128)S(1)} %get-tuple-element.66), channel_id=1, source_target_pairs={{0,248},{8,0},{16,8},{24,16},{32,24},{40,32},{48,40},{56,48},{64,5... | collective-permute-start | bytes 98312 | tf_op jit(solution)/shard_map/ppermute | solution.py:461
  75.7 22.1 %copy-start.4 = (f32[1,64,64,256]{3,2,1,0:T(8,128)S(1)}, f32[1,64,64,256]{3,2,1,0:T(8,128)}, u32[]{:S(2)}) copy-start(f32[1,64,64,256]{3,2,1,0:T(8,128)} %param.12) | copy-start | bytes 12582916
  76.2 5.6 %collective-permute-start.6 = (f32[128,128]{1,0:T(8,128)S(1)}, f32[128,128]{1,0:T(8,128)S(1)}, u32[]{:S(2)}, u32[]{:S(2)}) collective-permute-start(f32[128,128]{1,0:T(8,128)S(1)} %get-tuple-element.74), channel_id=1, source_target_pairs={{0,1},{1,2},{2,3},{3,4},{4,5},{5,6},{6,7},{7,0},{8,9},{9,10},{10,1... | collective-permute-start | bytes 196616 | tf_op jit(solution)/shard_map/ppermute | solution.py:461
  76.3 5.5 %collective-permute-start.7 = (f32[128,128]{1,0:T(8,128)S(1)}, f32[128,128]{1,0:T(8,128)S(1)}, u32[]{:S(2)}, u32[]{:S(2)}) collective-permute-start(f32[128,128]{1,0:T(8,128)S(1)} %get-tuple-element.75.order_ref), channel_id=1, source_target_pairs={{0,7},{1,0},{2,1},{3,2},{4,3},{5,4},{6,5},{7,6},{8,15},{9,8},{10,9... | collective-permute-start | bytes 196616 | tf_op jit(solution)/shard_map/ppermute | solution.py:461
  97.9 41.2 %copy-start = (f32[64,4,256]{2,1,0:T(4,128)S(1)}, f32[64,4,256]{2,1,0:T(4,128)}, u32[]{:S(2)}) copy-start(f32[64,4,256]{2,1,0:T(4,128)} %start_ref.1) | copy-start | bytes 786436
  119.9 19.1 %all-to-all-start.5 = ((f32[32,24,256]{2,1,0:T(8,128)}), f32[32,24,256]{2,1,0:T(8,128)S(1)}, u32[]{:S(2)}, u32[]{:S(2)}) async-start(f32[32,24,256]{2,1,0:T(8,128)} %get-tuple-element.88), calls=%async_computation.5 | async-start | bytes 1572864 | tf_op jit(solution)/shard_map/all_to_all | solution.py:472
  125.1 3.7 %collective-permute-start.8 = (f32[8,128]{1,0:T(8,128)S(1)}, f32[8,128]{1,0:T(8,128)S(1)}, u32[]{:S(2)}, u32[]{:S(2)}) collective-permute-start(f32[8,128]{1,0:T(8,128)S(1)} %get-tuple-element.90), channel_id=1, source_target_pairs={{0,1},{1,0},{2,3},{3,2},{4,5},{5,4},{6,7},{7,6},{8,9},{9,8},{10,11... | collective-permute-start | bytes 12296 | tf_op jit(solution)/shard_map/ppermute | solution.py:478
  128.8 4.5 %collective-permute-start.9 = (f32[8,128]{1,0:T(8,128)S(1)}, f32[8,128]{1,0:T(8,128)S(1)}, u32[]{:S(2)}, u32[]{:S(2)}) collective-permute-start(f32[8,128]{1,0:T(8,128)S(1)} %add.9), channel_id=1, source_target_pairs={{0,2},{1,3},{2,0},{3,1},{4,6},{5,7},{6,4},{7,5},{8,10},{9,11},{10,... | collective-permute-start | bytes 12296 | tf_op jit(solution)/shard_map/ppermute | solution.py:478
  133.3 5.7 %collective-permute-start.10 = (f32[8,128]{1,0:T(8,128)S(1)}, f32[8,128]{1,0:T(8,128)S(1)}, u32[]{:S(2)}, u32[]{:S(2)}) collective-permute-start(f32[8,128]{1,0:T(8,128)S(1)} %add.10), channel_id=1, source_target_pairs={{0,6},{1,7},{2,4},{3,5},{4,2},{5,3},{6,0},{7,1},{8,14},{9,15},{10,... | collective-permute-start | bytes 12296 | tf_op jit(solution)/shard_map/ppermute | solution.py:478
